TPU v7x, 32 devices: a whole 2x2x4 slice. The times are simulated.
32 devices in a mesh: dp: 4 (over z), tensor: 8 (over y, x, core).
Axes of the slice: x: 2, y: 2, z: 4, core: 2. Of those that a mesh axis runs over, the one named last changes fastest.
Arguments:
- queries: bfloat16 [512, 8192], P('dp', 'tensor'), may hold values from -6 to 6
- keys: bfloat16 [512, 8192], P('dp', 'tensor'), may hold values from -6 to 6
- values: bfloat16 [512, 8192], P('dp', 'tensor'), may hold values from -6 to 6
- doc_start: int32 [512], P('dp'), may hold values from 0 to 511, as said below
- filters: float32 [512, 128], P('tensor'), may hold values from -0.5 to 0.5
- out_weight: bfloat16 [8192, 8192], P('tensor'), may hold values from -0.09375 to 0.09375
- out_grad: bfloat16 [512, 8192], P('dp'), may hold values from -6 to 6
Outputs:
- output: bfloat16 [512, 8192], P('dp', 'tensor')
- q_grad: bfloat16 [512, 8192], P('dp', 'tensor')
- k_grad: bfloat16 [512, 8192], P('dp', 'tensor')
- v_grad: bfloat16 [512, 8192], P('dp', 'tensor')
- filter_grad: float32 [512, 128], P('tensor')
Inputs may be any that keep to these rules, and one draw needn't show every extreme that they name: doc_start[0] = 0; for t > 0, doc_start[t] is t (a document begins) or doc_start[t - 1]; the last position begins a document.
All inputs are finite; a program needn't handle non-finite values.
Results may differ from a plain program's by a relative error of at most 0.015.
Values may be sent and summed in bfloat16 or wider, within the bound.
No kernel may reach another device: no remote copies, remote signals or barrier semaphores. Data moves between devices by JAX's collectives and lax.ppermute only.
A program may use at most 128 MiB of HBM per device.

v0:
```python
import jax
import jax.numpy as jnp
from jax import lax
from jax.sharding import PartitionSpec as P


def from_behind(value, axis, by):
    devices = lax.axis_size(axis)
    pairs = [(i, i + by) for i in range(devices) if 0 <= i + by < devices]
    return lax.ppermute(value, axis, pairs)


def banded(rows, pattern):
    groups, taps = pattern.shape
    extent = rows + taps - 1
    line = jnp.concatenate([pattern, jnp.zeros((groups, rows), pattern.dtype)], axis=1)
    flat = jnp.tile(line, (1, rows))
    return flat[:, : rows * extent].reshape(groups, rows, extent)


def diagonal_sums(product, taps):
    groups, rows, extent = product.shape
    flat = product.reshape(groups, rows * extent)
    flat = jnp.concatenate([flat, jnp.zeros((groups, rows), product.dtype)], axis=1)
    return jnp.sum(flat.reshape(groups, rows, extent + 1)[:, :, :taps], axis=1)


def on_device(queries, keys, values, doc_start, filters, out_weight, out_grad):
    rows, chan = queries.shape
    groups, taps = filters.shape
    member = chan // groups
    rim = taps - 1
    first = lax.axis_index("dp") * rows
    place = first + jnp.arange(rows, dtype=jnp.int32)
    ext_place = first - rim + jnp.arange(rows + rim, dtype=jnp.int32)
    high = lax.Precision.HIGHEST
    mixed = (keys.astype(jnp.float32) * values.astype(jnp.float32)).astype(jnp.bfloat16)
    before = from_behind(mixed[rows - rim :], "dp", 1)
    mixed_ext = jnp.concatenate([before, mixed], axis=0)
    mixed_f = mixed_ext.astype(jnp.float32).reshape(rows + rim, groups, member)
    fwd_mask = (ext_place[None, :] >= doc_start[:, None]).astype(jnp.float32)
    fwd_band = banded(rows, filters[:, ::-1]) * fwd_mask[None]
    conv = jnp.einsum("gts,sgi->tgi", fwd_band, mixed_f, precision=high).reshape(rows, chan)
    gated = (queries.astype(jnp.float32) * conv).astype(jnp.bfloat16)
    partial_out = jnp.dot(gated, out_weight, preferred_element_type=jnp.float32)
    output = lax.psum_scatter(
        partial_out.astype(jnp.bfloat16), "tensor", scatter_dimension=1, tiled=True
    )
    gated_grad = lax.dot_general(
        out_grad, out_weight, (((1,), (1,)), ((), ())), preferred_element_type=jnp.float32
    )
    q_grad = (gated_grad * conv).astype(jnp.bfloat16)
    conv_grad = (gated_grad * queries.astype(jnp.float32)).astype(jnp.bfloat16)
    carried = (doc_start[:rim] < first)[:, None]
    leading = jnp.where(carried, conv_grad[:rim], jnp.zeros((rim, chan), jnp.bfloat16))
    after = from_behind(leading, "dp", -1)
    grad_ext = (
        jnp.concatenate([conv_grad, after], axis=0)
        .astype(jnp.float32)
        .reshape(rows + rim, groups, member)
    )
    ext_doc = jnp.concatenate([doc_start, jnp.full((rim,), doc_start[rows - 1], jnp.int32)], axis=0)
    bwd_mask = (place[:, None] >= ext_doc[None, :]).astype(jnp.float32)
    bwd_band = banded(rows, filters) * bwd_mask[None]
    mixed_grad = jnp.einsum("gst,tgi->sgi", bwd_band, grad_ext, precision=high).reshape(rows, chan)
    k_grad = (mixed_grad * values.astype(jnp.float32)).astype(jnp.bfloat16)
    v_grad = (mixed_grad * keys.astype(jnp.float32)).astype(jnp.bfloat16)
    local_grad = conv_grad.astype(jnp.float32).reshape(rows, groups, member)
    product = jnp.einsum("tgi,sgi->gts", local_grad, mixed_f, precision=high) * fwd_mask[None]
    local_terms = diagonal_sums(product, taps)[:, ::-1]
    total_terms = lax.psum(local_terms, "dp")
    scale = (rows * lax.axis_size("dp") * member) ** (-0.5)
    filter_grad = total_terms * jnp.float32(scale)
    return (output, q_grad, k_grad, v_grad, filter_grad)


def solution(mesh):
    return jax.shard_map(
        on_device,
        mesh=mesh,
        in_specs=(
            P("dp", "tensor"),
            P("dp", "tensor"),
            P("dp", "tensor"),
            P("dp"),
            P("tensor", None),
            P("tensor", None),
            P("dp", None),
        ),
        out_specs=(
            P("dp", "tensor"),
            P("dp", "tensor"),
            P("dp", "tensor"),
            P("dp", "tensor"),
            P("tensor", None),
        ),
        check_vma=False,
    )
```

profile of v0, /device:TPU:0, one launch (start us, length us, event | category | flops | bytes accessed | tf_op | source)
XLA Modules:
  0.0 153.0 jit_solution(7414972986052480978)
XLA Ops:
  7.2 0.8 slice_compare_fusion
  8.0 0.7 copy-done
  8.8 11.4 %fusion.7 = (bf16[128,1024]{1,0:T(8,128)(2,1)S(1)}, f32[128,1024]{1,0:T(8,128)S(1)}) fusion(bf16[128,1024]{1,0:T(8,128)(2,1)} %param.7, bf16[128,8192]{1,0:T(8,128)(2,1)S(1)} %copy-done, bf16[1024,8192]{1,0:T(8,128)(2,1)} %param.12), kind=kOutput, calls=%fused_computation.15 | convolution fusion | flops 2147876864 | bytes 19922944 | tf_op jit(solution)/shard_map/dot_general | solution.py:49
  20.3 1.5 collective-permute-start.1
  23.1 0.7 tile.20
  23.7 4.7 %copy.27 = f32[8,8,128,256]{3,1,2,0:T(8,128)S(1)} copy(f32[8,8,128,256]{3,2,1,0:T(8,128)S(1)} %bitcast.24) | data formatting | bytes 16777216
  28.5 3.8 %slice.31 = f32[64,32640]{1,0:T(8,128)} slice(f32[64,32768]{1,0:T(8,128)S(1)} %bitcast.26), slice={[0:64], [0:32640]} | slice | bytes 16711680 | tf_op jit(solution)/shard_map/slice | solution.py:18
  32.2 15.9 %reshape.114 = f32[64,128,255]{2,1,0:T(8,128)} reshape(f32[64,32640]{1,0:T(8,128)} %slice.31) | data formatting | bytes 16711680 | tf_op jit(solution)/shard_map/reshape | solution.py:18
  48.5 6.6 %fusion = f32[64,16,128]{2,1,0:T(8,128)S(1)} fusion(bf16[255,64,16]{0,2,1:T(8,128)(2,1)S(1)} %bitcast.31, f32[64,128,255]{2,1,0:T(8,128)} %reshape.114, f32[128,255]{1,0:T(8,128)S(1)} %compare_convert_fusion), kind=kOutput, calls=%fused_computation.1 | convolution fusion | flops 403169280 | bytes 9532928 | tf_op jit(solution)/shard_map/gst,tgi->sgi/dot_general | solution.py:65
  55.4 1.0 fusion.8
  56.4 5.8 %collective-permute-start = (bf16[127,1024]{1,0:T(8,128)(2,1)S(1)}, bf16[127,1024]{1,0:T(8,128)(2,1)S(1)}, u32[]{:S(2)}, u32[]{:S(2)}) collective-permute-start(bf16[127,1024]{1,0:T(8,128)(2,1)S(1)} %slice.28), channel_id=1, source_target_pairs={{0,8},{8,16},{16,24},{1,9},{9,17},{17,25},{2,10},{10,18},{18,26},{... | collective-permute-start | bytes 780296 | tf_op jit(solution)/shard_map/ppermute | solution.py:10
  62.3 0.7 tile.8
  62.9 4.7 %copy.26 = f32[8,8,128,256]{3,1,2,0:T(8,128)S(1)} copy(f32[8,8,128,256]{3,2,1,0:T(8,128)S(1)} %bitcast.25) | data formatting | bytes 16777216
  67.7 3.8 %slice.29 = f32[64,32640]{1,0:T(8,128)} slice(f32[64,32768]{1,0:T(8,128)S(1)} %bitcast.27), slice={[0:64], [0:32640]} | slice | bytes 16711680 | tf_op jit(solution)/shard_map/slice | solution.py:18
  71.4 15.9 %reshape.111 = f32[64,128,255]{2,1,0:T(8,128)} reshape(f32[64,32640]{1,0:T(8,128)} %slice.29) | data formatting | bytes 16711680 | tf_op jit(solution)/shard_map/reshape | solution.py:18
  87.8 6.6 %fusion.2 = f32[64,16,128]{2,1,0:T(8,128)S(1)} fusion(bf16[255,64,16]{0,2,1:T(8,128)(2,1)S(1)} %bitcast.29, f32[64,128,255]{2,1,0:T(8,128)} %reshape.111, f32[128,255]{1,0:T(8,128)S(1)} %compare_convert_fusion.1), kind=kOutput, calls=%fused_computation.3 | convolution fusion | flops 403169280 | bytes 9532928 | tf_op jit(solution)/shard_map/gts,sgi->tgi/dot_general | solution.py:43
  94.6 9.5 %convolution_convert_fusion = bf16[128,8192]{1,0:T(8,128)(2,1)} fusion(bf16[1024,8192]{1,0:T(8,128)(2,1)} %param.12, f32[128,1024]{1,0:T(8,128)S(1)} %copy.20, bf16[128,1024]{1,0:T(8,128)(2,1)S(1)} %copy-done.2), kind=kOutput, calls=%fused_computation | convolution fusion | flops 2148925440 | bytes 19660800 | tf_op jit(solution)/shard_map/dot_general | solution.py:45
  104.3 4.5 %broadcast_multiply_fusion = f32[64,128,255]{2,1,0:T(8,128)} fusion(f32[128,255]{1,0:T(8,128)S(1)} %compare_convert_fusion.1, bf16[128,64,16]{0,2,1:T(8,128)(2,1)S(1)} %bitcast.34, bf16[255,64,16]{0,2,1:T(8,128)(2,1)S(1)} %bitcast.30), kind=kOutput, calls=%fused_computation.7 | convolution fusion | flops 68935680 | bytes 9270784 | tf_op jit(solution)/shard_map/tgi,sgi->gts/dot_general | solution.py:69
  108.8 9.6 %reshape.117 = f32[64,32640]{1,0:T(8,128)} reshape(f32[64,128,255]{2,1,0:T(8,128)} %broadcast_multiply_fusion) | data formatting | bytes 16711680 | tf_op jit(solution)/shard_map/reshape | solution.py:23
  118.4 4.0 %concatenate.23 = f32[64,32768]{1,0:T(8,128)S(1)} pad(f32[64,32640]{1,0:T(8,128)} %reshape.117, f32[]{:T(128)} %constant.6.clone.1), padding=0_0x0_128 | pad | bytes 16744452 | tf_op jit(solution)/shard_map/concatenate | solution.py:24
  122.4 2.5 %copy.28 = f32[8,8,128,256]{3,2,1,0:T(8,128)S(1)} copy(f32[8,8,128,256]{3,1,2,0:T(8,128)S(1)} %bitcast.23) | data formatting | bytes 16777216
  125.5 17.9 %psum.7 = f32[64,128]{1,0:T(8,128)S(1)} all-reduce(f32[64,128]{1,0:T(8,128)S(1)} %rev.7), channel_id=1, replica_groups=mesh['dp'=4,'tensor'=8] {'dp'}, use_global_device_ids=true, to_apply=%region_2.3 | all-reduce | flops 8192 | bytes 65536 | tf_op jit(solution)/shard_map/psum | solution.py:71
  144.0 0.8 multiply_convert_fusion
  144.8 1.4 reduce-scatter.2.cloned.1.call-done
  (38 shorter events, 4.0 us)
Async XLA Ops:
  7.2 1.6 %copy-start = (bf16[128,8192]{1,0:T(8,128)(2,1)S(1)}, bf16[128,8192]{1,0:T(8,128)(2,1)}, u32[]{:S(2)}) copy-start(bf16[128,8192]{1,0:T(8,128)(2,1)} %param.13) | copy-start | bytes 6291460
  7.2 139.0 %reduce-scatter.2.cloned.1.call-start = ((), (), s32[]{:S(2)}) async-start(), calls=%async_computation.1 | async-start | bytes 2359296 | tf_op jit(solution)/shard_map/reduce_scatter | solution.py:46
  8.8 13.0 %copy-start.6 = (s32[128]{0:T(128)S(1)}, s32[128]{0:T(128)}, u32[]{:S(2)}) copy-start(s32[128]{0:T(128)} %param.10) | copy-start | bytes 1540
  8.8 14.2 %copy-start.5 = (f32[64,128]{1,0:T(8,128)S(1)}, f32[64,128]{1,0:T(8,128)}, u32[]{:S(2)}) copy-start(f32[64,128]{1,0:T(8,128)} %param.11) | copy-start | bytes 98308
  20.3 28.0 %collective-permute-start.1 = (bf16[127,1024]{1,0:T(8,128)(2,1)S(1)}, bf16[127,1024]{1,0:T(8,128)(2,1)S(1)}, u32[]{:S(2)}, u32[]{:S(2)}) collective-permute-start(bf16[127,1024]{1,0:T(8,128)(2,1)S(1)} %slice_select_fusion), channel_id=1, source_target_pairs={{8,0},{16,8},{24,16},{9,1},{17,9},{25,17},{10,2},{18,10},{26,18},{... | collective-permute-start | bytes 780296 | tf_op jit(solution)/shard_map/ppermute | solution.py:10
  48.2 7.2 %copy-start.3 = (bf16[128,1024]{1,0:T(8,128)(2,1)S(1)}, bf16[128,1024]{1,0:T(8,128)(2,1)}, u32[]{:S(2)}) copy-start(bf16[128,1024]{1,0:T(8,128)(2,1)} %param.8) | copy-start | bytes 786436
  48.2 7.2 %copy-start.4 = (bf16[128,1024]{1,0:T(8,128)(2,1)S(1)}, bf16[128,1024]{1,0:T(8,128)(2,1)}, u32[]{:S(2)}) copy-start(bf16[128,1024]{1,0:T(8,128)(2,1)} %param.9) | copy-start | bytes 786436
  56.4 31.1 %collective-permute-start = (bf16[127,1024]{1,0:T(8,128)(2,1)S(1)}, bf16[127,1024]{1,0:T(8,128)(2,1)S(1)}, u32[]{:S(2)}, u32[]{:S(2)}) collective-permute-start(bf16[127,1024]{1,0:T(8,128)(2,1)S(1)} %slice.28), channel_id=1, source_target_pairs={{0,8},{8,16},{16,24},{1,9},{9,17},{17,25},{2,10},{10,18},{18,26},{... | collective-permute-start | bytes 780296 | tf_op jit(solution)/shard_map/ppermute | solution.py:10
  87.4 7.2 %copy-start.2 = (bf16[128,1024]{1,0:T(8,128)(2,1)S(1)}, bf16[128,1024]{1,0:T(8,128)(2,1)}, u32[]{:S(2)}) copy-start(bf16[128,1024]{1,0:T(8,128)(2,1)} %param.7) | copy-start | bytes 786436
  122.4 23.7 %copy-start.1 = (bf16[128,8192]{1,0:T(8,128)(2,1)S(1)}, bf16[128,8192]{1,0:T(8,128)(2,1)}, u32[]{:S(2)}) copy-start(bf16[128,8192]{1,0:T(8,128)(2,1)} %param.13) | copy-start | bytes 6291460
Sparse Core Ops, SparseCore 0:
  104.2 41.9 reduce-scatter.1
where the time goes:
time: 153 us
  local copies, waits for them, and re-layouts  69.5 us (45%)
  matrix products  38.6 us (25%)
  blocking collectives  17.9 us (12%)
  between operations  14.3 us (9%)
  starting transfers between devices  7.3 us (5%)
  other arithmetic  4.04 us (3%)
    reshape x2, local copies, waits for them, and re-layouts, banded(): return flat[:, :rows * extent].reshape(groups, rows, extent)  31.9 us
    psum x1, blocking collectives, on_device(): total_terms = lax.psum(local_terms, 'dp')  17.9 us
    unnamed x17, local copies, waits for them, and re-layouts  12.7 us
    dot_general x1, matrix products, on_device(): lax.dot_general(out_grad, out_weight, (((1,), (1,)), ((), ())), preferred...  11.4 us
    reshape x1, local copies, waits for them, and re-layouts, diagonal_sums(): flat = product.reshape(groups, rows * extent)  9.57 us
    dot_general x1, matrix products, on_device(): partial_out = jnp.dot(gated, out_weight, preferred_element_type=jnp.float32)  9.46 us
    slice x2, local copies, waits for them, and re-layouts, banded(): return flat[:, :rows * extent].reshape(groups, rows, extent)  7.51 us
    ppermute x2, starting transfers between devices, from_behind(): return lax.ppermute(value, axis, pairs)  7.26 us
  transfers between devices with their start and end apart: 3, of which 1 were waited for; matrix products, arithmetic and copies ran while one was open for 49% of the time, Pallas kernels for 0%

commit v1 on v0

v1 whole, which is shorter than its diff:
```python
import functools

import jax
import jax.numpy as jnp
from jax import lax
from jax.experimental import pallas as pl
from jax.experimental.pallas import tpu as pltpu
from jax.sharding import PartitionSpec as P

F32, BF16 = jnp.float32, jnp.bfloat16
LANES = 128
SUBLANES = 8
NT = (((1,), (1,)), ((), ()))
VMEM = pl.BlockSpec(memory_space=pltpu.VMEM)
MIB = 1 << 20


def call(body, operands, outs, name, scratch=(), held=None):
    shapes = [jax.ShapeDtypeStruct(*s) for s in outs]
    aliases = {}
    if held is not None:
        operands = [held_in_vmem(v) if k == held else v for k, v in enumerate(operands)]
        shapes = [pltpu.VMEM(operands[held].shape, operands[held].dtype)] + shapes
        aliases = {held: 0}
    return pl.pallas_call(
        body,
        out_shape=shapes,
        in_specs=[VMEM] * len(operands),
        out_specs=[VMEM] * len(shapes),
        input_output_aliases=aliases,
        scratch_shapes=list(scratch),
        compiler_params=pltpu.CompilerParams(vmem_limit_bytes=16 * MIB),
        name=name,
    )(*operands)


def held_in_vmem(value):
    return pltpu.with_memory_space_constraint(value, pltpu.VMEM)


def mirror(taps):
    i = lax.broadcasted_iota(jnp.int32, (taps, taps), 0)
    j = lax.broadcasted_iota(jnp.int32, (taps, taps), 1)
    return (i + j == taps) | ((i == 0) & (j == 0))


def doc_offsets(doc_ref, taps):
    first = lax.axis_index("dp") * taps
    lane = jnp.broadcast_to((doc_ref[...] - first).astype(F32), (taps, taps))
    return lane, lane.T


def grid_of(taps):
    return (
        lax.broadcasted_iota(jnp.int32, (taps, taps), 0).astype(F32),
        lax.broadcasted_iota(jnp.int32, (taps, taps), 1).astype(F32),
    )


def row_masks(doc_ref, taps):
    _, doc = doc_offsets(doc_ref, taps)
    t, s = grid_of(taps)
    return (s <= t) & (s >= doc), (s > t) & (s - taps >= doc)


def column_masks(doc_ref, taps):
    doc, _ = doc_offsets(doc_ref, taps)
    s, t = grid_of(taps)
    return (s <= t) & (s >= doc), (s > t) & (s >= doc[:, taps - 1 :])


def front_body(chunks, doc_ref, filt_ref, grad_ref, weight_ref, queries_ref,
               fwd_ref, bwd_ref, gated_ref, conv_ref, lead_ref, held_ref, turned, arrived):
    groups, taps = filt_ref.shape
    step = weight_ref.shape[0] // chunks
    copies = [
        pltpu.make_async_copy(weight_ref.at[pl.ds(k * step, step)], held_ref.at[pl.ds(k * step, step)], arrived.at[k])
        for k in range(chunks)
    ]
    for copy in copies:
        copy.start()
    turned[...] = jnp.dot(
        filt_ref[...].astype(BF16), mirror(taps).astype(BF16), preferred_element_type=F32
    )
    here, before = [m.astype(BF16) for m in row_masks(doc_ref, taps)]
    here_t, after = [m.astype(BF16) for m in column_masks(doc_ref, taps)]

    @pl.loop(0, groups, unroll=16)
    def _(g):
        rows = pl.ds(pl.multiple_of(g * taps, taps), taps)

        def circulant(ref):
            line = jnp.broadcast_to(ref[pl.ds(g, 1), :], (taps, taps))
            return pltpu.roll(line, 0, 1, stride=1, stride_axis=0).astype(BF16)

        fwd = circulant(turned)
        fwd_ref[rows, :taps] = fwd * here
        fwd_ref[rows, taps:] = fwd * before
        bwd = circulant(filt_ref)
        bwd_ref[rows, :taps] = bwd * here_t
        bwd_ref[rows, taps:] = bwd * after

    _, doc = doc_offsets(doc_ref, taps)
    for k, copy in enumerate(copies):
        copy.wait()
        columns = pl.ds(k * step, step)
        total = lax.dot_general(grad_ref[...], held_ref[columns, :], NT, preferred_element_type=F32)
        gated_ref[:, columns] = total
        conv_grad = (total * queries_ref[:, columns].astype(F32)).astype(BF16)
        conv_ref[:, columns] = conv_grad
        lead_ref[:, columns] = jnp.where(doc[:, :1] < 0, conv_grad, jnp.zeros_like(conv_grad))


def filtered(band_ref, near_ref, far_ref, columns, member):
    taps = near_ref.shape[0]
    groups = LANES // member
    both = jnp.concatenate([near_ref[:, columns], far_ref[:, columns]], axis=0)
    bands = pl.ds(columns.start // LANES * groups * taps, groups * taps)
    every = jnp.dot(band_ref[bands, :], both, preferred_element_type=F32)
    owner = lax.div(lax.broadcasted_iota(jnp.int32, (taps, LANES), 1), member)
    total = every[:taps]
    for g in range(1, groups):
        total = jnp.where(owner == g, every[g * taps : (g + 1) * taps], total)
    return total


def block_columns(offset, sibling, width):
    me = lax.axis_index("tensor")
    chip, core = lax.div(me, 2), lax.rem(me, 2)
    owner = 2 * jnp.bitwise_xor(chip, offset) + (1 - core if sibling else core)
    return pl.ds(pl.multiple_of(owner * width, width), width)


def conv_body(member, offsets, band_ref, mixed_ref, before_ref, queries_ref, weight_ref, held_ref, conv_ref, gated_ref, *part_refs):
    chan = mixed_ref.shape[1]

    for tile in range(chan // LANES):
        columns = pl.ds(tile * LANES, LANES)
        conv = filtered(band_ref, mixed_ref, before_ref, columns, member)
        conv_ref[:, columns] = conv
        gated_ref[:, columns] = (queries_ref[:, columns].astype(F32) * conv).astype(BF16)

    part_body(offsets, True, weight_ref, gated_ref, held_ref, *part_refs)


def part_body(offsets, sibling, weight_ref, gated_ref, *refs):
    count = len(offsets)
    adds, outs = refs[: -1 - count], refs[-count:]
    for k, offset in enumerate(offsets):
        columns = block_columns(offset, sibling, outs[k].shape[1])
        part = jnp.dot(gated_ref[...], weight_ref[:, columns], preferred_element_type=F32)
        if adds:
            part = part.astype(BF16).astype(F32) + adds[k][...].astype(F32)
        outs[k][...] = part.astype(BF16)


def filter_grad_body(member, scale, doc_ref, grad_ref, mixed_ref, before_ref, out_ref, sums):
    taps, chan = grad_ref.shape
    groups = LANES // member
    here, before = [m.astype(F32) for m in row_masks(doc_ref, taps)]
    owner = lax.div(lax.broadcasted_iota(jnp.int32, (taps, LANES), 1), member)

    for tile in range(chan // LANES):
        columns = pl.ds(tile * LANES, LANES)
        both = jnp.concatenate([mixed_ref[:, columns], before_ref[:, columns]], axis=0)
        grad = grad_ref[:, columns]
        apart = jnp.concatenate([grad * (owner == g).astype(BF16) for g in range(groups)], axis=0)
        every = lax.dot_general(apart, both, NT, preferred_element_type=F32)
        for g in range(groups):
            one = every[g * taps : (g + 1) * taps]
            one = one[:, :taps] * here + one[:, taps:] * before
            total = one[:SUBLANES]
            for b in range(SUBLANES, taps, SUBLANES):
                total = total + pltpu.roll(one[b : b + SUBLANES], taps - b, 1)
            sums[tile * groups + g] = total

    total = sums[:, 0, :]
    for i in range(1, SUBLANES):
        total = total + pltpu.roll(sums[:, i, :], taps - i, 1)
    out_ref[...] = scale * jnp.dot(
        total, mirror(taps).astype(F32), precision=lax.Precision.HIGHEST, preferred_element_type=F32
    )


def input_grads_body(member, band_ref, grad_ref, after_ref, keys_ref, values_ref, gated_ref, conv_ref, q_ref, k_ref, v_ref):
    chan = grad_ref.shape[1]

    for tile in range(chan // LANES):
        columns = pl.ds(tile * LANES, LANES)
        mixed_grad = filtered(band_ref, grad_ref, after_ref, columns, member)
        k_ref[:, columns] = (mixed_grad * values_ref[:, columns].astype(F32)).astype(BF16)
        v_ref[:, columns] = (mixed_grad * keys_ref[:, columns].astype(F32)).astype(BF16)
        q_ref[:, columns] = (gated_ref[:, columns] * conv_ref[:, columns]).astype(BF16)


def shift(value, axis, by):
    devices = lax.axis_size(axis)
    return lax.ppermute(value, axis, [(i, i + by) for i in range(devices) if 0 <= i + by < devices])


def swap(value, mask):
    devices = lax.axis_size("tensor")
    return lax.ppermute(value, "tensor", [(i, i ^ mask) for i in range(devices)])


def summed_over_dp(terms):
    devices = lax.axis_size("dp")
    if devices > 4:
        return lax.psum(terms, "dp")
    total = terms
    for by in range(1, devices):
        total = total + lax.ppermute(terms, "dp", [(i, (i + by) % devices) for i in range(devices)])
    return total


def on_device(queries, keys, values, doc_start, filters, out_weight, out_grad):
    rows, chan = queries.shape
    groups, taps = filters.shape
    member = chan // groups
    n = lax.axis_size("tensor")
    width = out_weight.shape[1] // n
    assert rows == taps == LANES and LANES % member == 0
    doc = doc_start.reshape(1, rows)
    tile, tile32, block = ((rows, chan), BF16), ((rows, chan), F32), ((rows, width), BF16)
    bands = pltpu.VMEM((groups * taps, 2 * taps), BF16)

    mixed = (keys.astype(F32) * values.astype(F32)).astype(BF16)
    before = shift(mixed, "dp", 1)
    chunks = max(1, chan // LANES)
    fwd, bwd, gated_grad, conv_grad, leading, weight = pl.pallas_call(
        functools.partial(front_body, chunks),
        out_shape=[bands, bands] + [jax.ShapeDtypeStruct(*s) for s in (tile32, tile, tile)] + [pltpu.VMEM(out_weight.shape, BF16)],
        in_specs=[VMEM, VMEM, VMEM, pl.BlockSpec(memory_space=pl.ANY), VMEM],
        out_specs=[VMEM] * 6,
        scratch_shapes=[pltpu.VMEM((groups, taps), F32), pltpu.SemaphoreType.DMA((chunks,))],
        compiler_params=pltpu.CompilerParams(vmem_limit_bytes=16 * MIB),
        name="front",
    )(doc, filters, out_grad, out_weight, queries)
    fwd, bwd = held_in_vmem(fwd), held_in_vmem(bwd)

    if n == 8:
        some, rest = (3, 1), (2, 0)
        weight, conv, gated, *first = call(
            functools.partial(conv_body, member, some), (fwd, mixed, before, queries, weight),
            [tile32, tile, block, block], "conv", held=4,
        )
        first = [swap(v, 1) for v in first]
        weight, *second = call(
            functools.partial(part_body, rest, True), (weight, gated), [block, block], "part_rest", held=0
        )
        second = [swap(v, 1) for v in second]
        weight, far, near_x = call(
            functools.partial(part_body, some, False), (weight, gated, *first), [block, block], "sum_some", held=0
        )
        far, near_x = swap(far, 6), swap(near_x, 2)
        weight, near_y, own = call(
            functools.partial(part_body, rest, False), (weight, gated, *second), [block, block], "sum_rest", held=0
        )
        near_y, leading, conv_grad = lax.optimization_barrier((near_y, leading, conv_grad))
        near_y = swap(near_y, 4)
        output = sum(v.astype(F32) for v in (own, near_x, near_y, far)).astype(BF16)
    else:
        weight, conv, gated = call(
            functools.partial(conv_body, member, ()), (fwd, mixed, before, queries, weight), [tile32, tile], "conv", held=4
        )
        partial_out = jnp.dot(gated, out_weight, preferred_element_type=F32).astype(BF16)
        output = lax.psum_scatter(partial_out, "tensor", scatter_dimension=1, tiled=True)
    after = shift(leading, "dp", -1)
    scale = (rows * lax.axis_size("dp") * member) ** (-0.5)
    (terms,) = call(
        functools.partial(filter_grad_body, member, scale), (doc, conv_grad, mixed, before),
        [((groups, taps), F32)], "filter_grad", scratch=[pltpu.VMEM((groups, SUBLANES, taps), F32)],
    )
    filter_grad = summed_over_dp(terms)
    q_grad, k_grad, v_grad = call(
        functools.partial(input_grads_body, member), (bwd, conv_grad, after, keys, values, gated_grad, conv),
        [tile, tile, tile], "input_grads",
    )
    return (output, q_grad, k_grad, v_grad, filter_grad)


def solution(mesh):
    split = P("dp", "tensor")
    return jax.shard_map(
        on_device,
        mesh=mesh,
        in_specs=(split, split, split, P("dp"), P("tensor", None), P("tensor", None), P("dp", None)),
        out_specs=(split, split, split, split, P("tensor", None)),
        check_vma=False,
    )
```

time: 153 us -> 51.3 us (0.34)
  local copies, waits for them, and re-layouts: 69.5 us -> 3.96 us
  matrix products: 38.6 us -> 0 us
  Pallas kernels: 0 us -> 19.8 us
  blocking collectives: 17.9 us -> 0 us
  between operations: 14.3 us -> 0.74 us
  starting transfers between devices: 7.3 us -> 15.5 us
  waiting for transfers between devices: 1.38 us -> 8.4 us
    reshape x5 -> x0, local copies, waits for them, and re-layouts: 41.9 us -> none  [the longest x2 31.9 us: banded(): return flat[:, :rows * extent].reshape(groups, rows, extent)]
    dot_general x5 -> x0, matrix products: 38.6 us -> none  [the longest x1 11.4 us: on_device(): lax.dot_general(out_grad, out_weight, (((1,), (1,)), ((), ())), preferred...]
    pallas_call x0 -> x7, Pallas kernels: none -> 19.8 us  [the longest x1 11.8 us: on_device(): pl.pallas_call(functools.partial(front_body, chunks), out_shape=[bands, b...]
    psum x1 -> x0, blocking collectives: 17.9 us -> none  [on_device(): total_terms = lax.psum(local_terms, 'dp')]
    unnamed x17 -> x14, local copies, waits for them, and re-layouts: 12.7 us -> 3.96 us
    ppermute x2 -> x12, waiting for transfers between devices: 0.01 us -> 8.4 us  [the longest x7 5.26 us: swap(): lax.ppermute(value, 'tensor', [(i, i ^ mask) for i in range(devices)])]
    ppermute x2 -> x12, starting transfers between devices: 7.26 us -> 15.5 us  [the longest x2 6.22 us: shift(): lax.ppermute(value, axis, [(i, i + by) for i in range(devices) if 0 <= i...]
    slice x4 -> x0, local copies, waits for them, and re-layouts: 8.15 us -> none  [the longest x2 7.51 us: banded(): return flat[:, :rows * extent].reshape(groups, rows, extent)]
  transfers between devices with their start and end apart: 3 -> 12, of which waited for: 1 -> 8; matrix products, arithmetic and copies ran while one was open for 49% -> 3% of each run, Pallas kernels for 0% -> 26%
where the time goes in v1:
time: 51.3 us; the launch traced here: 51 us
  Pallas kernels  19.8 us (39%)
  starting transfers between devices  15.5 us (30%)
  waiting for transfers between devices  8.4 us (16%)
  local copies, waits for them, and re-layouts  3.96 us (8%)
  other arithmetic  2.61 us (5%)
  between operations  0.74 us (1%)
    pallas_call x1, Pallas kernels, on_device(): pl.pallas_call(functools.partial(front_body, chunks), out_shape=[bands, b...  11.8 us
    pallas_call x6, Pallas kernels, call(): pl.pallas_call(body, out_shape=shapes, in_specs=[VMEM] * len(operands), o...  7.94 us
    ppermute x2, starting transfers between devices, shift(): lax.ppermute(value, axis, [(i, i + by) for i in range(devices) if 0 <= i...  6.22 us
    ppermute x7, waiting for transfers between devices, swap(): lax.ppermute(value, 'tensor', [(i, i ^ mask) for i in range(devices)])  5.26 us
    ppermute x3, starting transfers between devices, summed_over_dp(): lax.ppermute(terms, 'dp', [(i, (i + by) % devices) for i in range(devices)])  4.64 us
    ppermute x7, starting transfers between devices, swap(): lax.ppermute(value, 'tensor', [(i, i ^ mask) for i in range(devices)])  4.63 us
    unnamed x14, local copies, waits for them, and re-layouts  3.96 us
    ppermute x3, waiting for transfers between devices, summed_over_dp(): lax.ppermute(terms, 'dp', [(i, (i + by) % devices) for i in range(devices)])  2.86 us
  transfers between devices with their start and end apart: 12, of which 8 were waited for; matrix products, arithmetic and copies ran while one was open for 3% of the time, Pallas kernels for 26%

profile of v1, /device:TPU:0, one launch (start us, length us, event | category | flops | bytes accessed | tf_op | source)
XLA Modules:
  0.0 51.0 jit_solution(16111377351133738319)
XLA Ops:
  0.6 1.1 %multiply_convert_fusion.mixed_ref = bf16[128,1024]{1,0:T(8,128)(2,1)S(1)} fusion(bf16[128,1024]{1,0:T(8,128)(2,1)} %values_ref.1, bf16[128,1024]{1,0:T(8,128)(2,1)} %keys_ref.1), kind=kLoop, calls=%fused_computation.1 | loop fusion | flops 524288 | bytes 786432 | tf_op jit(solution)/shard_map/convert_element_type | solution.py:227
  1.7 4.9 %collective-permute-start = (bf16[128,1024]{1,0:T(8,128)(2,1)S(1)}, bf16[128,1024]{1,0:T(8,128)(2,1)S(1)}, u32[]{:S(2)}, u32[]{:S(2)}) collective-permute-start(bf16[128,1024]{1,0:T(8,128)(2,1)S(1)} %multiply_convert_fusion.mixed_ref), channel_id=1, source_target_pairs={{0,8},{8,16},{16,24},{1,9},{9,17},{17,25},{2,10},{10,18},{18,26},{... | collective-permute-start | bytes 786440 | tf_op jit(solution)/shard_map/ppermute | solution.py:198
  6.7 1.6 %copy-done = bf16[128,8192]{1,0:T(8,128)(2,1)S(1)} copy-done((bf16[128,8192]{1,0:T(8,128)(2,1)S(1)}, bf16[128,8192]{1,0:T(8,128)(2,1)}, u32[]{:S(2)}) %copy-start) | copy-done | bytes 2097176
  8.3 0.9 %copy-done.1 = bf16[128,1024]{1,0:T(8,128)(2,1)S(1)} copy-done((bf16[128,1024]{1,0:T(8,128)(2,1)S(1)}, bf16[128,1024]{1,0:T(8,128)(2,1)}, u32[]{:S(2)}) %copy-start.1) | copy-done | bytes 262168
  9.2 0.8 %copy-done.4 = f32[64,128]{1,0:T(8,128)S(1)} copy-done((f32[64,128]{1,0:T(8,128)S(1)}, f32[64,128]{1,0:T(8,128)}, u32[]{:S(2)}) %copy-start.4) | copy-done | bytes 32792
  10.0 0.7 %copy-done.5 = s32[128]{0:T(128)S(1)} copy-done((s32[128]{0:T(128)S(1)}, s32[128]{0:T(128)}, u32[]{:S(2)}) %copy-start.5) | copy-done | bytes 536
  10.7 11.8 %front.1 = (bf16[8192,256]{1,0:T(8,128)(2,1)S(1)}, bf16[8192,256]{1,0:T(8,128)(2,1)S(1)}, f32[128,1024]{1,0:T(8,128)S(1)}, bf16[128,1024]{1,0:T(8,128)(2,1)S(1)}...) custom-call(s32[1,128]{1,0:T(1,128)S(1)} %bitcast.1, f32[64,128]{1,0:T(8,128)S(1)} %copy-done.4, ...), custom_call_target="tpu_custom_call" | custom-call | tf_op jit(solution)/shard_map/front/pallas_call | solution.py:230
  22.5 1.8 %conv.1 = (bf16[1024,8192]{1,0:T(8,128)(2,1)S(1)}, f32[128,1024]{1,0:T(8,128)S(1)}, bf16[128,1024]{1,0:T(8,128)(2,1)S(1)}, bf16[128,1024]{1,0:T(8,128)(2,1)S(1)}, bf16[128,1024]{1,0:T(8,128)(2,1)S(1)}) custom-call(bf16[8192,256]{1,0:T(8,128)(2,1)S(1)} %get-tuple-element.30.band_ref, ...), custom_call_target="tpu_custom_call", output_to_operand_aliasing={{0}: (4, {})} | custom-call | tf_op jit(solution)/shard_map/conv/pallas_call | solution.py:25
  24.9 0.7 %part_rest.1 = (bf16[1024,8192]{1,0:T(8,128)(2,1)S(1)}, bf16[128,1024]{1,0:T(8,128)(2,1)S(1)}, bf16[128,1024]{1,0:T(8,128)(2,1)S(1)}) custom-call(bf16[1024,8192]{1,0:T(8,128)(2,1)S(1)} %get-tuple-element.32.weight_ref, bf16[128,1024]{1,0:T(8,128)(2,1)S(1)} %get-tuple-element.33.gated_ref), custom_call_target="tpu_custom_call", output_to_operand_aliasing={{0}: (0, {})} | custom-call | tf_op jit(solution)/shard_map/part_rest/pallas_call | solution.py:25
  26.3 0.8 %sum_some.1 = (bf16[1024,8192]{1,0:T(8,128)(2,1)S(1)}, bf16[128,1024]{1,0:T(8,128)(2,1)S(1)}, bf16[128,1024]{1,0:T(8,128)(2,1)S(1)}) custom-call(bf16[1024,8192]{1,0:T(8,128)(2,1)S(1)} %get-tuple-element.34.weight_ref, bf16[128,1024]{1,0:T(8,128)(2,1)S(1)} %get-tuple-element.33.gated_ref, ...), custom_call_target="tpu_custom_call", output_to_operand_aliasing={{0}: (0, {})} | custom-call | tf_op jit(solution)/shard_map/sum_some/pallas_call | solution.py:25
  27.6 0.8 %sum_rest.1 = (bf16[1024,8192]{1,0:T(8,128)(2,1)S(1)}, bf16[128,1024]{1,0:T(8,128)(2,1)S(1)}, bf16[128,1024]{1,0:T(8,128)(2,1)S(1)}) custom-call(bf16[1024,8192]{1,0:T(8,128)(2,1)S(1)} %get-tuple-element.37.weight_ref, bf16[128,1024]{1,0:T(8,128)(2,1)S(1)} %get-tuple-element.33.gated_ref, ...), custom_call_target="tpu_custom_call", output_to_operand_aliasing={{0}: (0, {})} | custom-call | tf_op jit(solution)/shard_map/sum_rest/pallas_call | solution.py:25
  28.4 1.7 %filter_grad.1 = f32[64,128]{1,0:T(8,128)S(1)} custom-call(s32[1,128]{1,0:T(1,128)S(1)} %bitcast.2, bf16[128,1024]{1,0:T(8,128)(2,1)S(1)} %get-tuple-element.48.grad_ref, bf16[128,1024]{1,0:T(8,128)(2,1)S(1)} %multiply_convert_fusion.mixed_ref, bf16[128,1024]{1,0:T(8,128)(2,1)S(1)} %collective-permute-done.before_ref), custom_call_target="tpu_custom_call" | custom-call | tf_op jit(solution)/shard_map/filter_grad/pallas_call | solution.py:25
  30.1 1.4 %collective-permute-start.11 = (f32[64,128]{1,0:T(8,128)S(1)}, f32[64,128]{1,0:T(8,128)S(1)}, u32[]{:S(2)}, u32[]{:S(2)}) collective-permute-start(f32[64,128]{1,0:T(8,128)S(1)} %filter_grad.1), channel_id=1, source_target_pairs={{0,24},{8,0},{16,8},{24,16},{1,25},{9,1},{17,9},{25,17},{2,26},{10... | collective-permute-start | bytes 98312 | tf_op jit(solution)/shard_map/ppermute | solution.py:212
  31.5 1.5 %collective-permute-start.5 = (bf16[128,1024]{1,0:T(8,128)(2,1)S(1)}, bf16[128,1024]{1,0:T(8,128)(2,1)S(1)}, u32[]{:S(2)}, u32[]{:S(2)}) collective-permute-start(bf16[128,1024]{1,0:T(8,128)(2,1)S(1)} %get-tuple-element.41), channel_id=1, source_target_pairs={{0,2},{1,3},{2,0},{3,1},{4,6},{5,7},{6,4},{7,5},{8,10},{9,11},{10,... | collective-permute-start | bytes 786440 | tf_op jit(solution)/shard_map/ppermute | solution.py:203
  33.0 1.5 %collective-permute-start.7 = (bf16[128,1024]{1,0:T(8,128)(2,1)S(1)}, bf16[128,1024]{1,0:T(8,128)(2,1)S(1)}, u32[]{:S(2)}, u32[]{:S(2)}) collective-permute-start(bf16[128,1024]{1,0:T(8,128)(2,1)S(1)} %get-tuple-element.46), channel_id=1, source_target_pairs={{0,6},{1,7},{2,4},{3,5},{4,2},{5,3},{6,0},{7,1},{8,14},{9,15},{10,... | collective-permute-start | bytes 786440 | tf_op jit(solution)/shard_map/ppermute | solution.py:203
  35.0 1.6 %collective-permute-start.10 = (f32[64,128]{1,0:T(8,128)S(1)}, f32[64,128]{1,0:T(8,128)S(1)}, u32[]{:S(2)}, u32[]{:S(2)}) collective-permute-start(f32[64,128]{1,0:T(8,128)S(1)} %filter_grad.1), channel_id=1, source_target_pairs={{0,16},{8,24},{16,0},{24,8},{1,17},{9,25},{17,1},{25,9},{2,18},{10... | collective-permute-start | bytes 98312 | tf_op jit(solution)/shard_map/ppermute | solution.py:212
  36.6 1.6 %collective-permute-start.9 = (f32[64,128]{1,0:T(8,128)S(1)}, f32[64,128]{1,0:T(8,128)S(1)}, u32[]{:S(2)}, u32[]{:S(2)}) collective-permute-start(f32[64,128]{1,0:T(8,128)S(1)} %filter_grad.1), channel_id=1, source_target_pairs={{0,8},{8,16},{16,24},{24,0},{1,9},{9,17},{17,25},{25,1},{2,10},{10... | collective-permute-start | bytes 98312 | tf_op jit(solution)/shard_map/ppermute | solution.py:212
  38.2 2.3 %collective-permute-done.10 = f32[64,128]{1,0:T(8,128)S(1)} collective-permute-done((f32[64,128]{1,0:T(8,128)S(1)}, f32[64,128]{1,0:T(8,128)S(1)}, u32[]{:S(2)}, u32[]{:S(2)}) %collective-permute-start.10) | collective-permute-done | bytes 32800 | tf_op jit(solution)/shard_map/ppermute | solution.py:212
  40.5 1.3 %collective-permute-start.8 = (bf16[128,1024]{1,0:T(8,128)(2,1)S(1)}, bf16[128,1024]{1,0:T(8,128)(2,1)S(1)}, u32[]{:S(2)}, u32[]{:S(2)}) collective-permute-start(bf16[128,1024]{1,0:T(8,128)(2,1)S(1)} %get-tuple-element.49), channel_id=1, source_target_pairs={{8,0},{16,8},{24,16},{9,1},{17,9},{25,17},{10,2},{18,10},{26,18},{... | collective-permute-start | bytes 786440 | tf_op jit(solution)/shard_map/ppermute | solution.py:198
  42.3 0.6 %add_add_fusion = f32[64,128]{1,0:T(8,128)} fusion(f32[64,128]{1,0:T(8,128)S(1)} %collective-permute-done.11, f32[64,128]{1,0:T(8,128)S(1)} %collective-permute-done.10, f32[64,128]{1,0:T(8,128)S(1)} %filter_grad.1, f32[64,128]{1,0:T(8,128)S(1)} %collective-permute-done.9), kind=kLoop, calls=%fused_computation.2 | loop fusion | flops 24576 | bytes 163840 | tf_op jit(solution)/shard_map/add | solution.py:212
  43.0 3.3 %collective-permute-done.7 = bf16[128,1024]{1,0:T(8,128)(2,1)S(1)} collective-permute-done((bf16[128,1024]{1,0:T(8,128)(2,1)S(1)}, bf16[128,1024]{1,0:T(8,128)(2,1)S(1)}, u32[]{:S(2)}, u32[]{:S(2)}) %collective-permute-start.7) | collective-permute-done | bytes 262176 | tf_op jit(solution)/shard_map/ppermute | solution.py:203
  46.2 1.4 %collective-permute-done.6 = bf16[128,1024]{1,0:T(8,128)(2,1)S(1)} collective-permute-done((bf16[128,1024]{1,0:T(8,128)(2,1)S(1)}, bf16[128,1024]{1,0:T(8,128)(2,1)S(1)}, u32[]{:S(2)}, u32[]{:S(2)}) %collective-permute-start.6) | collective-permute-done | bytes 262176 | tf_op jit(solution)/shard_map/ppermute | solution.py:203
  47.6 0.9 %add_convert_fusion = bf16[128,1024]{1,0:T(8,128)(2,1)} fusion(bf16[128,1024]{1,0:T(8,128)(2,1)S(1)} %collective-permute-done.7, bf16[128,1024]{1,0:T(8,128)(2,1)S(1)} %collective-permute-done.6, bf16[128,1024]{1,0:T(8,128)(2,1)S(1)} %collective-permute-done.5, bf16[128,1024]{1,0:T(8,128)(2,1)S(1)} %get-tuple-element.40), kind=kLoop, calls=%fused_computation | loop fusion | flops 1048576 | bytes 1310720 | tf_op jit(solution)/shard_map/convert_element_type | solution.py:261
  48.8 2.2 %input_grads.1 = (bf16[128,1024]{1,0:T(8,128)(2,1)}, bf16[128,1024]{1,0:T(8,128)(2,1)}, bf16[128,1024]{1,0:T(8,128)(2,1)}) custom-call(bf16[8192,256]{1,0:T(8,128)(2,1)S(1)} %get-tuple-element.47.band_ref, bf16[128,1024]{1,0:T(8,128)(2,1)S(1)} %get-tuple-element.48.grad_ref, bf16[128,1024]{1,0:T(8,128)(2,1)S(1)} %collective-permute-done.8.after_ref, ...), custom_call_target="tpu_custom_call" | custom-call | tf_op jit(solution)/shard_map/input_grads/pallas_call | solution.py:25
  (24 shorter events, 3.1 us)
Async XLA Ops:
  1.7 20.7 %collective-permute-start = (bf16[128,1024]{1,0:T(8,128)(2,1)S(1)}, bf16[128,1024]{1,0:T(8,128)(2,1)S(1)}, u32[]{:S(2)}, u32[]{:S(2)}) collective-permute-start(bf16[128,1024]{1,0:T(8,128)(2,1)S(1)} %multiply_convert_fusion.mixed_ref), channel_id=1, source_target_pairs={{0,8},{8,16},{16,24},{1,9},{9,17},{17,25},{2,10},{10,18},{18,26},{... | collective-permute-start | bytes 786440 | tf_op jit(solution)/shard_map/ppermute | solution.py:198
  6.7 1.6 %copy-start = (bf16[128,8192]{1,0:T(8,128)(2,1)S(1)}, bf16[128,8192]{1,0:T(8,128)(2,1)}, u32[]{:S(2)}) copy-start(bf16[128,8192]{1,0:T(8,128)(2,1)} %grad_ref.1) | copy-start | bytes 6291460
  8.3 0.9 %copy-start.1 = (bf16[128,1024]{1,0:T(8,128)(2,1)S(1)}, bf16[128,1024]{1,0:T(8,128)(2,1)}, u32[]{:S(2)}) copy-start(bf16[128,1024]{1,0:T(8,128)(2,1)} %queries_ref.3) | copy-start | bytes 786436
  9.2 0.8 %copy-start.4 = (f32[64,128]{1,0:T(8,128)S(1)}, f32[64,128]{1,0:T(8,128)}, u32[]{:S(2)}) copy-start(f32[64,128]{1,0:T(8,128)} %filt_ref.1) | copy-start | bytes 98308
  10.0 0.7 %copy-start.5 = (s32[128]{0:T(128)S(1)}, s32[128]{0:T(128)}, u32[]{:S(2)}) copy-start(s32[128]{0:T(128)} %param.10) | copy-start | bytes 1540
  24.3 1.9 %collective-permute-start.1 = (bf16[128,1024]{1,0:T(8,128)(2,1)S(1)}, bf16[128,1024]{1,0:T(8,128)(2,1)S(1)}, u32[]{:S(2)}, u32[]{:S(2)}) collective-permute-start(bf16[128,1024]{1,0:T(8,128)(2,1)S(1)} %get-tuple-element.35), channel_id=1, source_target_pairs={{0,1},{1,0},{2,3},{3,2},{4,5},{5,4},{6,7},{7,6},{8,9},{9,8},{10,11... | collective-permute-start | bytes 786440 | tf_op jit(solution)/shard_map/ppermute | solution.py:203
  24.4 1.9 %collective-permute-start.2 = (bf16[128,1024]{1,0:T(8,128)(2,1)S(1)}, bf16[128,1024]{1,0:T(8,128)(2,1)S(1)}, u32[]{:S(2)}, u32[]{:S(2)}) collective-permute-start(bf16[128,1024]{1,0:T(8,128)(2,1)S(1)} %get-tuple-element.36), channel_id=1, source_target_pairs={{0,1},{1,0},{2,3},{3,2},{4,5},{5,4},{6,7},{7,6},{8,9},{9,8},{10,11... | collective-permute-start | bytes 786440 | tf_op jit(solution)/shard_map/ppermute | solution.py:203
  25.6 1.6 %collective-permute-start.3 = (bf16[128,1024]{1,0:T(8,128)(2,1)S(1)}, bf16[128,1024]{1,0:T(8,128)(2,1)S(1)}, u32[]{:S(2)}, u32[]{:S(2)}) collective-permute-start(bf16[128,1024]{1,0:T(8,128)(2,1)S(1)} %get-tuple-element.38), channel_id=1, source_target_pairs={{0,1},{1,0},{2,3},{3,2},{4,5},{5,4},{6,7},{7,6},{8,9},{9,8},{10,11... | collective-permute-start | bytes 786440 | tf_op jit(solution)/shard_map/ppermute | solution.py:203
  25.8 1.8 %collective-permute-start.4 = (bf16[128,1024]{1,0:T(8,128)(2,1)S(1)}, bf16[128,1024]{1,0:T(8,128)(2,1)S(1)}, u32[]{:S(2)}, u32[]{:S(2)}) collective-permute-start(bf16[128,1024]{1,0:T(8,128)(2,1)S(1)} %get-tuple-element.39), channel_id=1, source_target_pairs={{0,1},{1,0},{2,3},{3,2},{4,5},{5,4},{6,7},{7,6},{8,9},{9,8},{10,11... | collective-permute-start | bytes 786440 | tf_op jit(solution)/shard_map/ppermute | solution.py:203
  26.3 2.1 %copy-start.6 = (s32[128]{0:T(128)S(1)}, s32[128]{0:T(128)}, u32[]{:S(2)}) copy-start(s32[128]{0:T(128)} %param.10) | copy-start | bytes 1540
  26.3 22.5 %copy-start.2 = (bf16[128,1024]{1,0:T(8,128)(2,1)S(1)}, bf16[128,1024]{1,0:T(8,128)(2,1)}, u32[]{:S(2)}) copy-start(bf16[128,1024]{1,0:T(8,128)(2,1)} %values_ref.1) | copy-start | bytes 786436
  26.3 22.5 %copy-start.3 = (bf16[128,1024]{1,0:T(8,128)(2,1)S(1)}, bf16[128,1024]{1,0:T(8,128)(2,1)}, u32[]{:S(2)}) copy-start(bf16[128,1024]{1,0:T(8,128)(2,1)} %keys_ref.1) | copy-start | bytes 786436
  30.1 6.6 %collective-permute-start.11 = (f32[64,128]{1,0:T(8,128)S(1)}, f32[64,128]{1,0:T(8,128)S(1)}, u32[]{:S(2)}, u32[]{:S(2)}) collective-permute-start(f32[64,128]{1,0:T(8,128)S(1)} %filter_grad.1), channel_id=1, source_target_pairs={{0,24},{8,0},{16,8},{24,16},{1,25},{9,1},{17,9},{25,17},{2,26},{10... | collective-permute-start | bytes 98312 | tf_op jit(solution)/shard_map/ppermute | solution.py:212
  31.5 11.5 %collective-permute-start.5 = (bf16[128,1024]{1,0:T(8,128)(2,1)S(1)}, bf16[128,1024]{1,0:T(8,128)(2,1)S(1)}, u32[]{:S(2)}, u32[]{:S(2)}) collective-permute-start(bf16[128,1024]{1,0:T(8,128)(2,1)S(1)} %get-tuple-element.41), channel_id=1, source_target_pairs={{0,2},{1,3},{2,0},{3,1},{4,6},{5,7},{6,4},{7,5},{8,10},{9,11},{10,... | collective-permute-start | bytes 786440 | tf_op jit(solution)/shard_map/ppermute | solution.py:203
  33.0 13.3 %collective-permute-start.7 = (bf16[128,1024]{1,0:T(8,128)(2,1)S(1)}, bf16[128,1024]{1,0:T(8,128)(2,1)S(1)}, u32[]{:S(2)}, u32[]{:S(2)}) collective-permute-start(bf16[128,1024]{1,0:T(8,128)(2,1)S(1)} %get-tuple-element.46), channel_id=1, source_target_pairs={{0,6},{1,7},{2,4},{3,5},{4,2},{5,3},{6,0},{7,1},{8,14},{9,15},{10,... | collective-permute-start | bytes 786440 | tf_op jit(solution)/shard_map/ppermute | solution.py:203
  34.5 13.1 %collective-permute-start.6 = (bf16[128,1024]{1,0:T(8,128)(2,1)S(1)}, bf16[128,1024]{1,0:T(8,128)(2,1)S(1)}, u32[]{:S(2)}, u32[]{:S(2)}) collective-permute-start(bf16[128,1024]{1,0:T(8,128)(2,1)S(1)} %get-tuple-element.45), channel_id=1, source_target_pairs={{0,4},{1,5},{2,6},{3,7},{4,0},{5,1},{6,2},{7,3},{8,12},{9,13},{10,... | collective-permute-start | bytes 786440 | tf_op jit(solution)/shard_map/ppermute | solution.py:203
  35.0 5.5 %collective-permute-start.10 = (f32[64,128]{1,0:T(8,128)S(1)}, f32[64,128]{1,0:T(8,128)S(1)}, u32[]{:S(2)}, u32[]{:S(2)}) collective-permute-start(f32[64,128]{1,0:T(8,128)S(1)} %filter_grad.1), channel_id=1, source_target_pairs={{0,16},{8,24},{16,0},{24,8},{1,17},{9,25},{17,1},{25,9},{2,18},{10... | collective-permute-start | bytes 98312 | tf_op jit(solution)/shard_map/ppermute | solution.py:212
  36.6 5.7 %collective-permute-start.9 = (f32[64,128]{1,0:T(8,128)S(1)}, f32[64,128]{1,0:T(8,128)S(1)}, u32[]{:S(2)}, u32[]{:S(2)}) collective-permute-start(f32[64,128]{1,0:T(8,128)S(1)} %filter_grad.1), channel_id=1, source_target_pairs={{0,8},{8,16},{16,24},{24,0},{1,9},{9,17},{17,25},{25,1},{2,10},{10... | collective-permute-start | bytes 98312 | tf_op jit(solution)/shard_map/ppermute | solution.py:212
  40.5 8.3 %collective-permute-start.8 = (bf16[128,1024]{1,0:T(8,128)(2,1)S(1)}, bf16[128,1024]{1,0:T(8,128)(2,1)S(1)}, u32[]{:S(2)}, u32[]{:S(2)}) collective-permute-start(bf16[128,1024]{1,0:T(8,128)(2,1)S(1)} %get-tuple-element.49), channel_id=1, source_target_pairs={{8,0},{16,8},{24,16},{9,1},{17,9},{25,17},{10,2},{18,10},{26,18},{... | collective-permute-start | bytes 786440 | tf_op jit(solution)/shard_map/ppermute | solution.py:198

commit v2 on v1

--- a/solution.py
+++ b/solution.py
@@ -15,7 +15,11 @@
 MIB = 1 << 20
 
 
-def call(body, operands, outs, name, scratch=(), held=None):
+def cost(us):
+    return pl.CostEstimate(flops=int(us * 1.1e9), bytes_accessed=int(us * 3.6e6), transcendentals=0)
+
+
+def call(body, operands, outs, name, us, scratch=(), held=None):
     shapes = [jax.ShapeDtypeStruct(*s) for s in outs]
     aliases = {}
     if held is not None:
@@ -30,6 +34,7 @@
         input_output_aliases=aliases,
         scratch_shapes=list(scratch),
         compiler_params=pltpu.CompilerParams(vmem_limit_bytes=16 * MIB),
+        cost_estimate=cost(us),
         name=name,
     )(*operands)
 
@@ -69,42 +74,55 @@
     return (s <= t) & (s >= doc), (s > t) & (s >= doc[:, taps - 1 :])
 
 
-def front_body(chunks, doc_ref, filt_ref, grad_ref, weight_ref, queries_ref,
-               fwd_ref, bwd_ref, gated_ref, conv_ref, lead_ref, held_ref, turned, arrived):
+def front_body(ahead, doc_hbm, filt_hbm, grad_hbm, weight_hbm, queries_hbm, fwd_ref, bwd_ref, gated_ref, conv_ref,
+               lead_ref, weight_ref, doc_ref, filt_ref, turned, grad_ref, grad_t, queries_ref, arrived, came):
     groups, taps = filt_ref.shape
-    step = weight_ref.shape[0] // chunks
-    copies = [
-        pltpu.make_async_copy(weight_ref.at[pl.ds(k * step, step)], held_ref.at[pl.ds(k * step, step)], arrived.at[k])
-        for k in range(chunks)
+    chan = weight_ref.shape[0]
+    step = min(2 * LANES, chan)
+    count = chan // step
+    share = -(-groups // count)
+    small = [
+        pltpu.make_async_copy(src, dst, came.at[k])
+        for k, (src, dst) in enumerate(
+            ((doc_hbm, doc_ref), (filt_hbm, filt_ref), (grad_hbm, grad_ref), (queries_hbm, queries_ref))
+        )
     ]
-    for copy in copies:
+    large = [
+        pltpu.make_async_copy(weight_hbm.at[pl.ds(k * step, step)], weight_ref.at[pl.ds(k * step, step)], arrived.at[k])
+        for k in range(count)
+    ]
+    for copy in small + large[:ahead]:
         copy.start()
-    turned[...] = jnp.dot(
-        filt_ref[...].astype(BF16), mirror(taps).astype(BF16), preferred_element_type=F32
-    )
+    small[0].wait()
     here, before = [m.astype(BF16) for m in row_masks(doc_ref, taps)]
     here_t, after = [m.astype(BF16) for m in column_masks(doc_ref, taps)]
-
-    @pl.loop(0, groups, unroll=16)
-    def _(g):
-        rows = pl.ds(pl.multiple_of(g * taps, taps), taps)
-
-        def circulant(ref):
-            line = jnp.broadcast_to(ref[pl.ds(g, 1), :], (taps, taps))
-            return pltpu.roll(line, 0, 1, stride=1, stride_axis=0).astype(BF16)
-
-        fwd = circulant(turned)
-        fwd_ref[rows, :taps] = fwd * here
-        fwd_ref[rows, taps:] = fwd * before
-        bwd = circulant(filt_ref)
-        bwd_ref[rows, :taps] = bwd * here_t
-        bwd_ref[rows, taps:] = bwd * after
-
     _, doc = doc_offsets(doc_ref, taps)
-    for k, copy in enumerate(copies):
-        copy.wait()
+    small[1].wait()
+    turned[...] = jnp.dot(filt_ref[...].astype(BF16), mirror(taps).astype(BF16), preferred_element_type=F32)
+
+    def circulant(ref, g):
+        line = jnp.broadcast_to(ref[pl.ds(g, 1), :], (taps, taps))
+        return pltpu.roll(line, 0, 1, stride=1, stride_axis=0).astype(BF16)
+
+    for k in range(count):
+        for g in range(k * share, min(groups, (k + 1) * share)):
+            rows = pl.ds(g * taps, taps)
+            fwd = circulant(turned, g)
+            fwd_ref[rows, :taps] = fwd * here
+            fwd_ref[rows, taps:] = fwd * before
+            bwd = circulant(filt_ref, g)
+            bwd_ref[rows, :taps] = bwd * here_t
+            bwd_ref[rows, taps:] = bwd * after
+        if k == 0:
+            small[2].wait()
+            for c in range(0, grad_ref.shape[1], LANES):
+                grad_t[pl.ds(c, LANES), :] = grad_ref[:, pl.ds(c, LANES)].T
+            small[3].wait()
+        large[k].wait()
+        if k + ahead < count:
+            large[k + ahead].start()
         columns = pl.ds(k * step, step)
-        total = lax.dot_general(grad_ref[...], held_ref[columns, :], NT, preferred_element_type=F32)
+        total = jnp.dot(weight_ref[columns, :], grad_t[...], preferred_element_type=F32).T
         gated_ref[:, columns] = total
         conv_grad = (total * queries_ref[:, columns].astype(F32)).astype(BF16)
         conv_ref[:, columns] = conv_grad
@@ -144,14 +162,17 @@
 
 
 def part_body(offsets, sibling, weight_ref, gated_ref, *refs):
-    count = len(offsets)
-    adds, outs = refs[: -1 - count], refs[-count:]
+    rows = gated_ref.shape[0]
     for k, offset in enumerate(offsets):
-        columns = block_columns(offset, sibling, outs[k].shape[1])
+        width = refs[-1].shape[1]
+        stacked = pl.ds(k * rows, rows)
+        columns = block_columns(offset, sibling, width)
         part = jnp.dot(gated_ref[...], weight_ref[:, columns], preferred_element_type=F32)
-        if adds:
-            part = part.astype(BF16).astype(F32) + adds[k][...].astype(F32)
-        outs[k][...] = part.astype(BF16)
+        if sibling:
+            refs[-1][stacked, :] = part.astype(BF16)
+        else:
+            summed = part.astype(BF16).astype(F32) + refs[0][stacked, :].astype(F32)
+            refs[k - len(offsets)][...] = summed.astype(BF16)
 
 
 def filter_grad_body(member, scale, doc_ref, grad_ref, mixed_ref, before_ref, out_ref, sums):
@@ -182,9 +203,13 @@
     )
 
 
-def input_grads_body(member, band_ref, grad_ref, after_ref, keys_ref, values_ref, gated_ref, conv_ref, q_ref, k_ref, v_ref):
+def input_grads_body(member, band_ref, grad_ref, after_ref, keys_ref, values_ref, gated_ref, conv_ref, *refs):
     chan = grad_ref.shape[1]
-
+    *term_refs, q_ref, k_ref, v_ref, filter_ref = refs
+    total = term_refs[0][...]
+    for ref in term_refs[1:]:
+        total = total + ref[...]
+    filter_ref[...] = total
     for tile in range(chan // LANES):
         columns = pl.ds(tile * LANES, LANES)
         mixed_grad = filtered(band_ref, grad_ref, after_ref, columns, member)
@@ -203,14 +228,13 @@
     return lax.ppermute(value, "tensor", [(i, i ^ mask) for i in range(devices)])
 
 
-def summed_over_dp(terms):
+def over_dp(terms):
     devices = lax.axis_size("dp")
     if devices > 4:
-        return lax.psum(terms, "dp")
-    total = terms
-    for by in range(1, devices):
-        total = total + lax.ppermute(terms, "dp", [(i, (i + by) % devices) for i in range(devices)])
-    return total
+        return [lax.psum(terms, "dp")]
+    return [terms] + [
+        lax.ppermute(terms, "dp", [(i, (i + by) % devices) for i in range(devices)]) for by in range(1, devices)
+    ]
 
 
 def on_device(queries, keys, values, doc_start, filters, out_weight, out_grad):
@@ -226,42 +250,46 @@
 
     mixed = (keys.astype(F32) * values.astype(F32)).astype(BF16)
     before = shift(mixed, "dp", 1)
-    chunks = max(1, chan // LANES)
+    hbm = pl.BlockSpec(memory_space=pltpu.HBM)
     fwd, bwd, gated_grad, conv_grad, leading, weight = pl.pallas_call(
-        functools.partial(front_body, chunks),
+        functools.partial(front_body, 2),
         out_shape=[bands, bands] + [jax.ShapeDtypeStruct(*s) for s in (tile32, tile, tile)] + [pltpu.VMEM(out_weight.shape, BF16)],
-        in_specs=[VMEM, VMEM, VMEM, pl.BlockSpec(memory_space=pl.ANY), VMEM],
+        in_specs=[hbm] * 5,
         out_specs=[VMEM] * 6,
-        scratch_shapes=[pltpu.VMEM((groups, taps), F32), pltpu.SemaphoreType.DMA((chunks,))],
+        scratch_shapes=[
+            pltpu.VMEM(doc.shape, jnp.int32), pltpu.VMEM((groups, taps), F32), pltpu.VMEM((groups, taps), F32),
+            pltpu.VMEM(out_grad.shape, BF16), pltpu.VMEM(out_grad.shape[::-1], BF16), pltpu.VMEM(queries.shape, BF16),
+            pltpu.SemaphoreType.DMA((max(1, chan // (2 * LANES)),)), pltpu.SemaphoreType.DMA((4,)),
+        ],
         compiler_params=pltpu.CompilerParams(vmem_limit_bytes=16 * MIB),
+        cost_estimate=cost(6.5),
         name="front",
-    )(doc, filters, out_grad, out_weight, queries)
+    )(*(pltpu.with_memory_space_constraint(v, pltpu.HBM) for v in (doc, filters, out_grad, out_weight, queries)))
     fwd, bwd = held_in_vmem(fwd), held_in_vmem(bwd)
 
     if n == 8:
         some, rest = (3, 1), (2, 0)
-        weight, conv, gated, *first = call(
+        pair = ((2 * rows, width), BF16)
+        weight, conv, gated, first = call(
             functools.partial(conv_body, member, some), (fwd, mixed, before, queries, weight),
-            [tile32, tile, block, block], "conv", held=4,
-        )
-        first = [swap(v, 1) for v in first]
-        weight, *second = call(
-            functools.partial(part_body, rest, True), (weight, gated), [block, block], "part_rest", held=0
-        )
-        second = [swap(v, 1) for v in second]
+            [tile32, tile, pair], "conv", 1.9, held=4,
+        )
+        first = swap(first, 1)
+        weight, second = call(functools.partial(part_body, rest, True), (weight, gated), [pair], "part_rest", 0.8, held=0)
+        second = swap(second, 1)
         weight, far, near_x = call(
-            functools.partial(part_body, some, False), (weight, gated, *first), [block, block], "sum_some", held=0
+            functools.partial(part_body, some, False), (weight, gated, first), [block, block], "sum_some", 0.8, held=0
         )
         far, near_x = swap(far, 6), swap(near_x, 2)
         weight, near_y, own = call(
-            functools.partial(part_body, rest, False), (weight, gated, *second), [block, block], "sum_rest", held=0
+            functools.partial(part_body, rest, False), (weight, gated, second), [block, block], "sum_rest", 0.8, held=0
         )
         near_y, leading, conv_grad = lax.optimization_barrier((near_y, leading, conv_grad))
         near_y = swap(near_y, 4)
         output = sum(v.astype(F32) for v in (own, near_x, near_y, far)).astype(BF16)
     else:
         weight, conv, gated = call(
-            functools.partial(conv_body, member, ()), (fwd, mixed, before, queries, weight), [tile32, tile], "conv", held=4
+            functools.partial(conv_body, member, ()), (fwd, mixed, before, queries, weight), [tile32, tile], "conv", 1.2, held=4
         )
         partial_out = jnp.dot(gated, out_weight, preferred_element_type=F32).astype(BF16)
         output = lax.psum_scatter(partial_out, "tensor", scatter_dimension=1, tiled=True)
@@ -269,12 +297,12 @@
     scale = (rows * lax.axis_size("dp") * member) ** (-0.5)
     (terms,) = call(
         functools.partial(filter_grad_body, member, scale), (doc, conv_grad, mixed, before),
-        [((groups, taps), F32)], "filter_grad", scratch=[pltpu.VMEM((groups, SUBLANES, taps), F32)],
-    )
-    filter_grad = summed_over_dp(terms)
-    q_grad, k_grad, v_grad = call(
-        functools.partial(input_grads_body, member), (bwd, conv_grad, after, keys, values, gated_grad, conv),
-        [tile, tile, tile], "input_grads",
+        [((groups, taps), F32)], "filter_grad", 1.7, scratch=[pltpu.VMEM((groups, SUBLANES, taps), F32)],
+    )
+    terms = over_dp(terms)
+    q_grad, k_grad, v_grad, filter_grad = call(
+        functools.partial(input_grads_body, member), (bwd, conv_grad, after, keys, values, gated_grad, conv, *terms),
+        [tile, tile, tile, ((groups, taps), F32)], "input_grads", 2.0,
     )
     return (output, q_grad, k_grad, v_grad, filter_grad)
 

time: 51.3 us -> 40.8 us (0.80)
  local copies, waits for them, and re-layouts: 3.96 us -> 0.02 us
  waiting for transfers between devices: 8.4 us -> 4.75 us
  Pallas kernels: 19.8 us -> 16.7 us
  starting transfers between devices: 15.5 us -> 16.3 us
  other arithmetic: 2.61 us -> 2.01 us
    unnamed x14 -> x8, local copies, waits for them, and re-layouts: 3.96 us -> 0.02 us
    pallas_call x1, Pallas kernels: 11.8 us -> 8.79 us  [on_device(): pl.pallas_call(functools.partial(front_body, 2), out_shape=[bands, bands]...]
    ppermute x3, waiting for transfers between devices: 2.86 us -> 0.97 us  [over_dp(): lax.ppermute(terms, 'dp', [(i, (i + by) % devices) for i in range(devices)])]
    ppermute x7 -> x5, waiting for transfers between devices: 5.26 us -> 3.77 us  [swap(): lax.ppermute(value, 'tensor', [(i, i ^ mask) for i in range(devices)])]
    ppermute x3, starting transfers between devices: 4.64 us -> 5.7 us  [over_dp(): lax.ppermute(terms, 'dp', [(i, (i + by) % devices) for i in range(devices)])]
    add x1 -> x0, other arithmetic: 0.62 us -> none  [summed_over_dp(): total + lax.ppermute(terms, 'dp', [(i, (i + by) % devices) for i in range...]
    ppermute x7 -> x5, starting transfers between devices: 4.63 us -> 4.19 us  [swap(): lax.ppermute(value, 'tensor', [(i, i ^ mask) for i in range(devices)])]
  transfers between devices with their start and end apart: 12 -> 10, of which waited for: 8 -> 4; matrix products, arithmetic and copies ran while one was open for 3% -> 2% of each run, Pallas kernels for 26% -> 29%
where the time goes in v2:
time: 40.8 us; the launch traced here: 40.6 us
  Pallas kernels  16.7 us (41%)
  starting transfers between devices  16.3 us (40%)
  waiting for transfers between devices  4.75 us (12%)
  other arithmetic  2.01 us (5%)
  between operations  0.76 us (2%)
    pallas_call x1, Pallas kernels, on_device(): pl.pallas_call(functools.partial(front_body, 2), out_shape=[bands, bands]...  8.79 us
    pallas_call x6, Pallas kernels, call(): pl.pallas_call(body, out_shape=shapes, in_specs=[VMEM] * len(operands), o...  7.96 us
    ppermute x2, starting transfers between devices, shift(): lax.ppermute(value, axis, [(i, i + by) for i in range(devices) if 0 <= i...  6.4 us
    ppermute x3, starting transfers between devices, over_dp(): lax.ppermute(terms, 'dp', [(i, (i + by) % devices) for i in range(devices)])  5.7 us
    ppermute x5, starting transfers between devices, swap(): lax.ppermute(value, 'tensor', [(i, i ^ mask) for i in range(devices)])  4.19 us
    ppermute x5, waiting for transfers between devices, swap(): lax.ppermute(value, 'tensor', [(i, i ^ mask) for i in range(devices)])  3.77 us
    convert_element_type x1, other arithmetic, on_device(): mixed = (keys.astype(F32) * values.astype(F32)).astype(BF16)  1.14 us
    ppermute x3, waiting for transfers between devices, over_dp(): lax.ppermute(terms, 'dp', [(i, (i + by) % devices) for i in range(devices)])  0.97 us
  transfers between devices with their start and end apart: 10, of which 4 were waited for; matrix products, arithmetic and copies ran while one was open for 2% of the time, Pallas kernels for 29%

profile of v2, /device:TPU:0, one launch (start us, length us, event | category | flops | bytes accessed | tf_op | source)
XLA Modules:
  0.0 40.6 jit_solution(15860249848112325979)
XLA Ops:
  0.6 0.0 copy-start
  0.6 1.1 %multiply_convert_fusion.mixed_ref = bf16[128,1024]{1,0:T(8,128)(2,1)S(1)} fusion(bf16[128,1024]{1,0:T(8,128)(2,1)} %values_ref.1, bf16[128,1024]{1,0:T(8,128)(2,1)} %keys_ref.1), kind=kLoop, calls=%fused_computation.1 | loop fusion | flops 524288 | bytes 786432 | tf_op jit(solution)/shard_map/convert_element_type | solution.py:251
  1.8 4.9 %collective-permute-start = (bf16[128,1024]{1,0:T(8,128)(2,1)S(1)}, bf16[128,1024]{1,0:T(8,128)(2,1)S(1)}, u32[]{:S(2)}, u32[]{:S(2)}) collective-permute-start(bf16[128,1024]{1,0:T(8,128)(2,1)S(1)} %multiply_convert_fusion.mixed_ref), channel_id=1, source_target_pairs={{0,8},{8,16},{16,24},{1,9},{9,17},{17,25},{2,10},{10,18},{18,26},{... | collective-permute-start | bytes 786440 | tf_op jit(solution)/shard_map/ppermute | solution.py:223
  6.7 8.8 %front.1 = (bf16[8192,256]{1,0:T(8,128)(2,1)S(1)}, bf16[8192,256]{1,0:T(8,128)(2,1)S(1)}, f32[128,1024]{1,0:T(8,128)S(1)}, bf16[128,1024]{1,0:T(8,128)(2,1)S(1)}...) custom-call(s32[1,128]{1,0:T(1,128)} %bitcast.1, f32[64,128]{1,0:T(8,128)} %filt_hbm.1, ...), custom_call_target="tpu_custom_call" | custom-call | flops 7150000128 | bytes 23400000 | tf_op jit(solution)/shard_map/front/pallas_call | solution.py:254
  15.6 1.8 %conv.1 = (bf16[1024,8192]{1,0:T(8,128)(2,1)S(1)}, f32[128,1024]{1,0:T(8,128)S(1)}, bf16[128,1024]{1,0:T(8,128)(2,1)S(1)}, bf16[256,1024]{1,0:T(8,128)(2,1)S(1)}) custom-call(bf16[8192,256]{1,0:T(8,128)(2,1)S(1)} %get-tuple-element.29.band_ref, bf16[128,1024]{1,0:T(8,128)(2,1)S(1)} %multiply_convert_fusion.mixed_ref, ...), custom_call_target="tpu_custom_call", output_to_operand_aliasing={{0}: (4, {})} | custom-call | flops 2090000000 | bytes 6840000 | tf_op jit(solution)/shard_map/conv/pallas_call | solution.py:29
  17.4 0.1 collective-permute-start.1
  17.5 0.7 %part_rest.1 = (bf16[1024,8192]{1,0:T(8,128)(2,1)S(1)}, bf16[256,1024]{1,0:T(8,128)(2,1)S(1)}) custom-call(bf16[1024,8192]{1,0:T(8,128)(2,1)S(1)} %get-tuple-element.31.weight_ref, bf16[128,1024]{1,0:T(8,128)(2,1)S(1)} %get-tuple-element.32.gated_ref), custom_call_target="tpu_custom_call", output_to_operand_aliasing={{0}: (0, {})} | custom-call | flops 880000000 | bytes 2880000 | tf_op jit(solution)/shard_map/part_rest/pallas_call | solution.py:29
  18.2 0.6 %collective-permute-start.2 = (bf16[256,1024]{1,0:T(8,128)(2,1)S(1)}, bf16[256,1024]{1,0:T(8,128)(2,1)S(1)}, u32[]{:S(2)}, u32[]{:S(2)}) collective-permute-start(bf16[256,1024]{1,0:T(8,128)(2,1)S(1)} %get-tuple-element.36), channel_id=1, source_target_pairs={{0,1},{1,0},{2,3},{3,2},{4,5},{5,4},{6,7},{7,6},{8,9},{9,8},{10,11... | collective-permute-start | bytes 1572872 | tf_op jit(solution)/shard_map/ppermute | solution.py:228
  18.7 0.6 %collective-permute-done.1.refs_0_ = bf16[256,1024]{1,0:T(8,128)(2,1)S(1)} collective-permute-done((bf16[256,1024]{1,0:T(8,128)(2,1)S(1)}, bf16[256,1024]{1,0:T(8,128)(2,1)S(1)}, u32[]{:S(2)}, u32[]{:S(2)}) %collective-permute-start.1) | collective-permute-done | bytes 524320 | tf_op jit(solution)/shard_map/ppermute | solution.py:228
  19.4 0.8 %sum_some.1 = (bf16[1024,8192]{1,0:T(8,128)(2,1)S(1)}, bf16[128,1024]{1,0:T(8,128)(2,1)S(1)}, bf16[128,1024]{1,0:T(8,128)(2,1)S(1)}) custom-call(bf16[1024,8192]{1,0:T(8,128)(2,1)S(1)} %get-tuple-element.33.weight_ref, bf16[128,1024]{1,0:T(8,128)(2,1)S(1)} %get-tuple-element.32.gated_ref, ...), custom_call_target="tpu_custom_call", output_to_operand_aliasing={{0}: (0, {})} | custom-call | flops 880000000 | bytes 2880000 | tf_op jit(solution)/shard_map/sum_some/pallas_call | solution.py:29
  20.1 0.0 copy-start.1
  20.1 0.1 collective-permute-done.2.refs_0_
  20.3 0.8 %sum_rest.1 = (bf16[1024,8192]{1,0:T(8,128)(2,1)S(1)}, bf16[128,1024]{1,0:T(8,128)(2,1)S(1)}, bf16[128,1024]{1,0:T(8,128)(2,1)S(1)}) custom-call(bf16[1024,8192]{1,0:T(8,128)(2,1)S(1)} %get-tuple-element.35.weight_ref, bf16[128,1024]{1,0:T(8,128)(2,1)S(1)} %get-tuple-element.32.gated_ref, ...), custom_call_target="tpu_custom_call", output_to_operand_aliasing={{0}: (0, {})} | custom-call | flops 880000000 | bytes 2880000 | tf_op jit(solution)/shard_map/sum_rest/pallas_call | solution.py:29
  21.0 1.6 %collective-permute-start.4 = (bf16[128,1024]{1,0:T(8,128)(2,1)S(1)}, bf16[128,1024]{1,0:T(8,128)(2,1)S(1)}, u32[]{:S(2)}, u32[]{:S(2)}) collective-permute-start(bf16[128,1024]{1,0:T(8,128)(2,1)S(1)} %get-tuple-element.42), channel_id=1, source_target_pairs={{0,4},{1,5},{2,6},{3,7},{4,0},{5,1},{6,2},{7,3},{8,12},{9,13},{10,... | collective-permute-start | bytes 786440 | tf_op jit(solution)/shard_map/ppermute | solution.py:228
  22.7 1.5 %collective-permute-start.3 = (bf16[128,1024]{1,0:T(8,128)(2,1)S(1)}, bf16[128,1024]{1,0:T(8,128)(2,1)S(1)}, u32[]{:S(2)}, u32[]{:S(2)}) collective-permute-start(bf16[128,1024]{1,0:T(8,128)(2,1)S(1)} %get-tuple-element.38), channel_id=1, source_target_pairs={{0,2},{1,3},{2,0},{3,1},{4,6},{5,7},{6,4},{7,5},{8,10},{9,11},{10,... | collective-permute-start | bytes 786440 | tf_op jit(solution)/shard_map/ppermute | solution.py:228
  24.1 0.5 %collective-permute-start.5 = (bf16[128,1024]{1,0:T(8,128)(2,1)S(1)}, bf16[128,1024]{1,0:T(8,128)(2,1)S(1)}, u32[]{:S(2)}, u32[]{:S(2)}) collective-permute-start(bf16[128,1024]{1,0:T(8,128)(2,1)S(1)} %get-tuple-element.43), channel_id=1, source_target_pairs={{0,6},{1,7},{2,4},{3,5},{4,2},{5,3},{6,0},{7,1},{8,14},{9,15},{10,... | collective-permute-start | bytes 786440 | tf_op jit(solution)/shard_map/ppermute | solution.py:228
  24.6 1.5 %collective-permute-start.6 = (bf16[128,1024]{1,0:T(8,128)(2,1)S(1)}, bf16[128,1024]{1,0:T(8,128)(2,1)S(1)}, u32[]{:S(2)}, u32[]{:S(2)}) collective-permute-start(bf16[128,1024]{1,0:T(8,128)(2,1)S(1)} %get-tuple-element.46), channel_id=1, source_target_pairs={{8,0},{16,8},{24,16},{9,1},{17,9},{25,17},{10,2},{18,10},{26,18},{... | collective-permute-start | bytes 786440 | tf_op jit(solution)/shard_map/ppermute | solution.py:223
  26.1 1.7 %filter_grad.1.refs_0_ = f32[64,128]{1,0:T(8,128)S(1)} custom-call(s32[1,128]{1,0:T(1,128)S(1)} %bitcast.2, bf16[128,1024]{1,0:T(8,128)(2,1)S(1)} %get-tuple-element.45.grad_ref, bf16[128,1024]{1,0:T(8,128)(2,1)S(1)} %multiply_convert_fusion.mixed_ref, bf16[128,1024]{1,0:T(8,128)(2,1)S(1)} %collective-permute-done.before_ref), custom_call_target="tpu_custom_call" | custom-call | flops 1870000000 | bytes 6120000 | tf_op jit(solution)/shard_map/filter_grad/pallas_call | solution.py:29
  27.8 4.7 %collective-permute-start.9 = (f32[64,128]{1,0:T(8,128)S(1)}, f32[64,128]{1,0:T(8,128)S(1)}, u32[]{:S(2)}, u32[]{:S(2)}) collective-permute-start(f32[64,128]{1,0:T(8,128)S(1)} %filter_grad.1.refs_0_), channel_id=1, source_target_pairs={{0,24},{8,0},{16,8},{24,16},{1,25},{9,1},{17,9},{25,17},{2,26},{10... | collective-permute-start | bytes 98312 | tf_op jit(solution)/shard_map/ppermute | solution.py:236
  32.5 1.0 %collective-permute-start.7 = (f32[64,128]{1,0:T(8,128)S(1)}, f32[64,128]{1,0:T(8,128)S(1)}, u32[]{:S(2)}, u32[]{:S(2)}) collective-permute-start(f32[64,128]{1,0:T(8,128)S(1)} %filter_grad.1.refs_0_), channel_id=1, source_target_pairs={{0,8},{8,16},{16,24},{24,0},{1,9},{9,17},{17,25},{25,1},{2,10},{10... | collective-permute-start | bytes 98312 | tf_op jit(solution)/shard_map/ppermute | solution.py:236
  33.5 3.0 %collective-permute-done.5 = bf16[128,1024]{1,0:T(8,128)(2,1)S(1)} collective-permute-done((bf16[128,1024]{1,0:T(8,128)(2,1)S(1)}, bf16[128,1024]{1,0:T(8,128)(2,1)S(1)}, u32[]{:S(2)}, u32[]{:S(2)}) %collective-permute-start.5) | collective-permute-done | bytes 262176 | tf_op jit(solution)/shard_map/ppermute | solution.py:228
  36.5 0.9 %add_convert_fusion = bf16[128,1024]{1,0:T(8,128)(2,1)} fusion(bf16[128,1024]{1,0:T(8,128)(2,1)S(1)} %collective-permute-done.5, bf16[128,1024]{1,0:T(8,128)(2,1)S(1)} %collective-permute-done.4, bf16[128,1024]{1,0:T(8,128)(2,1)S(1)} %collective-permute-done.3, bf16[128,1024]{1,0:T(8,128)(2,1)S(1)} %get-tuple-element.37), kind=kLoop, calls=%fused_computation | loop fusion | flops 1048576 | bytes 1310720 | tf_op jit(solution)/shard_map/convert_element_type | solution.py:289
  37.4 1.0 %collective-permute-done.7.refs_1_ = f32[64,128]{1,0:T(8,128)S(1)} collective-permute-done((f32[64,128]{1,0:T(8,128)S(1)}, f32[64,128]{1,0:T(8,128)S(1)}, u32[]{:S(2)}, u32[]{:S(2)}) %collective-permute-start.7) | collective-permute-done | bytes 32800 | tf_op jit(solution)/shard_map/ppermute | solution.py:236
  38.4 2.2 %input_grads.1 = (bf16[128,1024]{1,0:T(8,128)(2,1)}, bf16[128,1024]{1,0:T(8,128)(2,1)}, bf16[128,1024]{1,0:T(8,128)(2,1)}, f32[64,128]{1,0:T(8,128)}) custom-call(bf16[8192,256]{1,0:T(8,128)(2,1)S(1)} %get-tuple-element.44.band_ref, bf16[128,1024]{1,0:T(8,128)(2,1)S(1)} %get-tuple-element.45.grad_ref, ...), custom_call_target="tpu_custom_call" | custom-call | flops 2200000000 | bytes 7200000 | tf_op jit(solution)/shard_map/input_grads/pallas_call | solution.py:29
  (13 shorter events, 0.0 us)
Async XLA Ops:
  0.6 14.9 %copy-start = (bf16[128,1024]{1,0:T(8,128)(2,1)S(1)}, bf16[128,1024]{1,0:T(8,128)(2,1)}, u32[]{:S(2)}) copy-start(bf16[128,1024]{1,0:T(8,128)(2,1)} %queries_ref.1) | copy-start | bytes 786436
  1.8 13.7 %collective-permute-start = (bf16[128,1024]{1,0:T(8,128)(2,1)S(1)}, bf16[128,1024]{1,0:T(8,128)(2,1)S(1)}, u32[]{:S(2)}, u32[]{:S(2)}) collective-permute-start(bf16[128,1024]{1,0:T(8,128)(2,1)S(1)} %multiply_convert_fusion.mixed_ref), channel_id=1, source_target_pairs={{0,8},{8,16},{16,24},{1,9},{9,17},{17,25},{2,10},{10,18},{18,26},{... | collective-permute-start | bytes 786440 | tf_op jit(solution)/shard_map/ppermute | solution.py:223
  17.4 2.0 %collective-permute-start.1 = (bf16[256,1024]{1,0:T(8,128)(2,1)S(1)}, bf16[256,1024]{1,0:T(8,128)(2,1)S(1)}, u32[]{:S(2)}, u32[]{:S(2)}) collective-permute-start(bf16[256,1024]{1,0:T(8,128)(2,1)S(1)} %get-tuple-element.34), channel_id=1, source_target_pairs={{0,1},{1,0},{2,3},{3,2},{4,5},{5,4},{6,7},{7,6},{8,9},{9,8},{10,11... | collective-permute-start | bytes 1572872 | tf_op jit(solution)/shard_map/ppermute | solution.py:228
  18.2 2.1 %collective-permute-start.2 = (bf16[256,1024]{1,0:T(8,128)(2,1)S(1)}, bf16[256,1024]{1,0:T(8,128)(2,1)S(1)}, u32[]{:S(2)}, u32[]{:S(2)}) collective-permute-start(bf16[256,1024]{1,0:T(8,128)(2,1)S(1)} %get-tuple-element.36), channel_id=1, source_target_pairs={{0,1},{1,0},{2,3},{3,2},{4,5},{5,4},{6,7},{7,6},{8,9},{9,8},{10,11... | collective-permute-start | bytes 1572872 | tf_op jit(solution)/shard_map/ppermute | solution.py:228
  19.4 6.7 %copy-start.3 = (s32[128]{0:T(128)S(1)}, s32[128]{0:T(128)}, u32[]{:S(2)}) copy-start(s32[128]{0:T(128)} %param.10) | copy-start | bytes 1540
  20.1 18.2 %copy-start.1 = (bf16[128,1024]{1,0:T(8,128)(2,1)S(1)}, bf16[128,1024]{1,0:T(8,128)(2,1)}, u32[]{:S(2)}) copy-start(bf16[128,1024]{1,0:T(8,128)(2,1)} %values_ref.1) | copy-start | bytes 786436
  20.1 18.2 %copy-start.2 = (bf16[128,1024]{1,0:T(8,128)(2,1)S(1)}, bf16[128,1024]{1,0:T(8,128)(2,1)}, u32[]{:S(2)}) copy-start(bf16[128,1024]{1,0:T(8,128)(2,1)} %keys_ref.1) | copy-start | bytes 786436
  21.0 11.4 %collective-permute-start.4 = (bf16[128,1024]{1,0:T(8,128)(2,1)S(1)}, bf16[128,1024]{1,0:T(8,128)(2,1)S(1)}, u32[]{:S(2)}, u32[]{:S(2)}) collective-permute-start(bf16[128,1024]{1,0:T(8,128)(2,1)S(1)} %get-tuple-element.42), channel_id=1, source_target_pairs={{0,4},{1,5},{2,6},{3,7},{4,0},{5,1},{6,2},{7,3},{8,12},{9,13},{10,... | collective-permute-start | bytes 786440 | tf_op jit(solution)/shard_map/ppermute | solution.py:228
  22.7 9.8 %collective-permute-start.3 = (bf16[128,1024]{1,0:T(8,128)(2,1)S(1)}, bf16[128,1024]{1,0:T(8,128)(2,1)S(1)}, u32[]{:S(2)}, u32[]{:S(2)}) collective-permute-start(bf16[128,1024]{1,0:T(8,128)(2,1)S(1)} %get-tuple-element.38), channel_id=1, source_target_pairs={{0,2},{1,3},{2,0},{3,1},{4,6},{5,7},{6,4},{7,5},{8,10},{9,11},{10,... | collective-permute-start | bytes 786440 | tf_op jit(solution)/shard_map/ppermute | solution.py:228
  24.1 12.4 %collective-permute-start.5 = (bf16[128,1024]{1,0:T(8,128)(2,1)S(1)}, bf16[128,1024]{1,0:T(8,128)(2,1)S(1)}, u32[]{:S(2)}, u32[]{:S(2)}) collective-permute-start(bf16[128,1024]{1,0:T(8,128)(2,1)S(1)} %get-tuple-element.43), channel_id=1, source_target_pairs={{0,6},{1,7},{2,4},{3,5},{4,2},{5,3},{6,0},{7,1},{8,14},{9,15},{10,... | collective-permute-start | bytes 786440 | tf_op jit(solution)/shard_map/ppermute | solution.py:228
  24.6 13.7 %collective-permute-start.6 = (bf16[128,1024]{1,0:T(8,128)(2,1)S(1)}, bf16[128,1024]{1,0:T(8,128)(2,1)S(1)}, u32[]{:S(2)}, u32[]{:S(2)}) collective-permute-start(bf16[128,1024]{1,0:T(8,128)(2,1)S(1)} %get-tuple-element.46), channel_id=1, source_target_pairs={{8,0},{16,8},{24,16},{9,1},{17,9},{25,17},{10,2},{18,10},{26,18},{... | collective-permute-start | bytes 786440 | tf_op jit(solution)/shard_map/ppermute | solution.py:223
  27.8 9.6 %collective-permute-start.9 = (f32[64,128]{1,0:T(8,128)S(1)}, f32[64,128]{1,0:T(8,128)S(1)}, u32[]{:S(2)}, u32[]{:S(2)}) collective-permute-start(f32[64,128]{1,0:T(8,128)S(1)} %filter_grad.1.refs_0_), channel_id=1, source_target_pairs={{0,24},{8,0},{16,8},{24,16},{1,25},{9,1},{17,9},{25,17},{2,26},{10... | collective-permute-start | bytes 98312 | tf_op jit(solution)/shard_map/ppermute | solution.py:236
  32.5 4.9 %collective-permute-start.8 = (f32[64,128]{1,0:T(8,128)S(1)}, f32[64,128]{1,0:T(8,128)S(1)}, u32[]{:S(2)}, u32[]{:S(2)}) collective-permute-start(f32[64,128]{1,0:T(8,128)S(1)} %filter_grad.1.refs_0_), channel_id=1, source_target_pairs={{0,16},{8,24},{16,0},{24,8},{1,17},{9,25},{17,1},{25,9},{2,18},{10... | collective-permute-start | bytes 98312 | tf_op jit(solution)/shard_map/ppermute | solution.py:236
  32.5 5.9 %collective-permute-start.7 = (f32[64,128]{1,0:T(8,128)S(1)}, f32[64,128]{1,0:T(8,128)S(1)}, u32[]{:S(2)}, u32[]{:S(2)}) collective-permute-start(f32[64,128]{1,0:T(8,128)S(1)} %filter_grad.1.refs_0_), channel_id=1, source_target_pairs={{0,8},{8,16},{16,24},{24,0},{1,9},{9,17},{17,25},{25,1},{2,10},{10... | collective-permute-start | bytes 98312 | tf_op jit(solution)/shard_map/ppermute | solution.py:236

commit v3 on v2

--- a/solution.py
+++ b/solution.py
@@ -19,17 +19,19 @@
     return pl.CostEstimate(flops=int(us * 1.1e9), bytes_accessed=int(us * 3.6e6), transcendentals=0)
 
 
-def call(body, operands, outs, name, us, scratch=(), held=None):
+def call(body, operands, outs, name, us, scratch=(), held=None, hbm=0):
     shapes = [jax.ShapeDtypeStruct(*s) for s in outs]
-    aliases = {}
+    operands, aliases = list(operands), {}
+    for k in range(hbm):
+        operands[k] = pltpu.with_memory_space_constraint(operands[k], pltpu.HBM)
     if held is not None:
-        operands = [held_in_vmem(v) if k == held else v for k, v in enumerate(operands)]
+        operands[held] = held_in_vmem(operands[held])
         shapes = [pltpu.VMEM(operands[held].shape, operands[held].dtype)] + shapes
         aliases = {held: 0}
     return pl.pallas_call(
         body,
         out_shape=shapes,
-        in_specs=[VMEM] * len(operands),
+        in_specs=[pl.BlockSpec(memory_space=pltpu.HBM)] * hbm + [VMEM] * (len(operands) - hbm),
         out_specs=[VMEM] * len(shapes),
         input_output_aliases=aliases,
         scratch_shapes=list(scratch),
@@ -43,6 +45,10 @@
     return pltpu.with_memory_space_constraint(value, pltpu.VMEM)
 
 
+def apart(body):
+    pl.when(lax.axis_index("dp") >= 0)(body)
+
+
 def mirror(taps):
     i = lax.broadcasted_iota(jnp.int32, (taps, taps), 0)
     j = lax.broadcasted_iota(jnp.int32, (taps, taps), 1)
@@ -74,29 +80,27 @@
     return (s <= t) & (s >= doc), (s > t) & (s >= doc[:, taps - 1 :])
 
 
-def front_body(ahead, doc_hbm, filt_hbm, grad_hbm, weight_hbm, queries_hbm, fwd_ref, bwd_ref, gated_ref, conv_ref,
-               lead_ref, weight_ref, doc_ref, filt_ref, turned, grad_ref, grad_t, queries_ref, arrived, came):
+def front_body(blocks, late, ahead, doc_hbm, filt_hbm, grad_hbm, weight_hbm, fwd_ref, bwd_ref, total_ref, late_ref,
+               weight_ref, doc_ref, filt_ref, turned, grad_ref, came, arrived, landed):
     groups, taps = filt_ref.shape
-    chan = weight_ref.shape[0]
-    step = min(2 * LANES, chan)
-    count = chan // step
+    blocks, late = blocks(), late()
+    count = len(blocks)
     share = -(-groups // count)
     small = [
         pltpu.make_async_copy(src, dst, came.at[k])
-        for k, (src, dst) in enumerate(
-            ((doc_hbm, doc_ref), (filt_hbm, filt_ref), (grad_hbm, grad_ref), (queries_hbm, queries_ref))
-        )
+        for k, (src, dst) in enumerate(((doc_hbm, doc_ref), (filt_hbm, filt_ref)))
     ]
-    large = [
-        pltpu.make_async_copy(weight_hbm.at[pl.ds(k * step, step)], weight_ref.at[pl.ds(k * step, step)], arrived.at[k])
-        for k in range(count)
+    grads = [
+        pltpu.make_async_copy(grad_hbm.at[:, b], grad_ref.at[:, b], arrived.at[k]) for k, b in enumerate(blocks + late)
     ]
-    for copy in small + large[:ahead]:
+    weights = [
+        pltpu.make_async_copy(weight_hbm.at[:, b], weight_ref.at[:, b], landed.at[k]) for k, b in enumerate(blocks)
+    ]
+    for copy in small + grads[:1] + weights[:1] + grads[1:] + weights[1:ahead]:
         copy.start()
     small[0].wait()
     here, before = [m.astype(BF16) for m in row_masks(doc_ref, taps)]
     here_t, after = [m.astype(BF16) for m in column_masks(doc_ref, taps)]
-    _, doc = doc_offsets(doc_ref, taps)
     small[1].wait()
     turned[...] = jnp.dot(filt_ref[...].astype(BF16), mirror(taps).astype(BF16), preferred_element_type=F32)
 
@@ -104,8 +108,8 @@
         line = jnp.broadcast_to(ref[pl.ds(g, 1), :], (taps, taps))
         return pltpu.roll(line, 0, 1, stride=1, stride_axis=0).astype(BF16)
 
-    for k in range(count):
-        for g in range(k * share, min(groups, (k + 1) * share)):
+    def bands(start, stop):
+        for g in range(start, min(groups, stop)):
             rows = pl.ds(g * taps, taps)
             fwd = circulant(turned, g)
             fwd_ref[rows, :taps] = fwd * here
@@ -113,20 +117,38 @@
             bwd = circulant(filt_ref, g)
             bwd_ref[rows, :taps] = bwd * here_t
             bwd_ref[rows, taps:] = bwd * after
-        if k == 0:
-            small[2].wait()
-            for c in range(0, grad_ref.shape[1], LANES):
-                grad_t[pl.ds(c, LANES), :] = grad_ref[:, pl.ds(c, LANES)].T
-            small[3].wait()
-        large[k].wait()
+
+    for k, columns in enumerate(blocks):
+        grads[k].wait()
+        weights[k].wait()
         if k + ahead < count:
-            large[k + ahead].start()
-        columns = pl.ds(k * step, step)
-        total = jnp.dot(weight_ref[columns, :], grad_t[...], preferred_element_type=F32).T
-        gated_ref[:, columns] = total
-        conv_grad = (total * queries_ref[:, columns].astype(F32)).astype(BF16)
-        conv_ref[:, columns] = conv_grad
-        lead_ref[:, columns] = jnp.where(doc[:, :1] < 0, conv_grad, jnp.zeros_like(conv_grad))
+            weights[k + ahead].start()
+
+        @apart
+        def _():
+            part = jnp.dot(weight_ref[:, columns], grad_ref[:, columns].T, preferred_element_type=F32)
+            total_ref[...] = part if k == 0 else total_ref[...] + part
+            bands(k * share, (k + 1) * share)
+
+    for k, columns in enumerate(late):
+        grads[count + k].wait()
+        width = columns.size
+        late_ref[pl.ds(k * width, width), :] = grad_ref[:, columns].T
+
+
+def gated_grad_body(late, doc_ref, weight_ref, total_ref, late_ref, queries_ref, held_ref, gated_ref, conv_ref, lead_ref):
+    del held_ref
+    taps = doc_ref.shape[1]
+    total = total_ref[...]
+    for k, columns in enumerate(late()):
+        width = columns.size
+        total = total + jnp.dot(weight_ref[:, columns], late_ref[pl.ds(k * width, width), :], preferred_element_type=F32)
+    total = total.T
+    gated_ref[...] = total
+    conv_grad = (total * queries_ref[...].astype(F32)).astype(BF16)
+    conv_ref[...] = conv_grad
+    _, doc = doc_offsets(doc_ref, taps)
+    lead_ref[...] = jnp.where(doc[:, :1] < 0, conv_grad, jnp.zeros_like(conv_grad))
 
 
 def filtered(band_ref, near_ref, far_ref, columns, member):
@@ -149,16 +171,23 @@
     return pl.ds(pl.multiple_of(owner * width, width), width)
 
 
-def conv_body(member, offsets, band_ref, mixed_ref, before_ref, queries_ref, weight_ref, held_ref, conv_ref, gated_ref, *part_refs):
-    chan = mixed_ref.shape[1]
-
-    for tile in range(chan // LANES):
-        columns = pl.ds(tile * LANES, LANES)
-        conv = filtered(band_ref, mixed_ref, before_ref, columns, member)
-        conv_ref[:, columns] = conv
-        gated_ref[:, columns] = (queries_ref[:, columns].astype(F32) * conv).astype(BF16)
-
-    part_body(offsets, True, weight_ref, gated_ref, held_ref, *part_refs)
+def conv_body(member, offsets, late, weight_hbm, band_ref, mixed_ref, before_ref, queries_ref, weight_ref, held_ref, conv_ref, gated_ref, *refs):
+    *part_refs, landed = refs
+    copies = [pltpu.make_async_copy(weight_hbm.at[:, b], held_ref.at[:, b], landed.at[k]) for k, b in enumerate(late())]
+    for copy in copies:
+        copy.start()
+
+    @apart
+    def _():
+        for tile in range(mixed_ref.shape[1] // LANES):
+            columns = pl.ds(tile * LANES, LANES)
+            conv = filtered(band_ref, mixed_ref, before_ref, columns, member)
+            conv_ref[:, columns] = conv
+            gated_ref[:, columns] = (queries_ref[:, columns].astype(F32) * conv).astype(BF16)
+        part_body(offsets, True, held_ref, gated_ref, *part_refs)
+
+    for copy in copies:
+        copy.wait()
 
 
 def part_body(offsets, sibling, weight_ref, gated_ref, *refs):
@@ -205,11 +234,7 @@
 
 def input_grads_body(member, band_ref, grad_ref, after_ref, keys_ref, values_ref, gated_ref, conv_ref, *refs):
     chan = grad_ref.shape[1]
-    *term_refs, q_ref, k_ref, v_ref, filter_ref = refs
-    total = term_refs[0][...]
-    for ref in term_refs[1:]:
-        total = total + ref[...]
-    filter_ref[...] = total
+    q_ref, k_ref, v_ref = refs
     for tile in range(chan // LANES):
         columns = pl.ds(tile * LANES, LANES)
         mixed_grad = filtered(band_ref, grad_ref, after_ref, columns, member)
@@ -218,6 +243,12 @@
         q_ref[:, columns] = (gated_ref[:, columns] * conv_ref[:, columns]).astype(BF16)
 
 
+def finish_body(count, *refs):
+    *parts, out_ref, filter_ref = refs
+    out_ref[...] = sum(ref[...].astype(F32) for ref in parts[count:]).astype(BF16)
+    filter_ref[...] = sum(ref[...] for ref in parts[:count])
+
+
 def shift(value, axis, by):
     devices = lax.axis_size(axis)
     return lax.ppermute(value, axis, [(i, i + by) for i in range(devices) if 0 <= i + by < devices])
@@ -228,13 +259,9 @@
     return lax.ppermute(value, "tensor", [(i, i ^ mask) for i in range(devices)])
 
 
-def over_dp(terms):
+def turn(value, by):
     devices = lax.axis_size("dp")
-    if devices > 4:
-        return [lax.psum(terms, "dp")]
-    return [terms] + [
-        lax.ppermute(terms, "dp", [(i, (i + by) % devices) for i in range(devices)]) for by in range(1, devices)
-    ]
+    return lax.ppermute(value, "dp", [(i, (i + by) % devices) for i in range(devices)])
 
 
 def on_device(queries, keys, values, doc_start, filters, out_weight, out_grad):
@@ -250,33 +277,49 @@
 
     mixed = (keys.astype(F32) * values.astype(F32)).astype(BF16)
     before = shift(mixed, "dp", 1)
-    hbm = pl.BlockSpec(memory_space=pltpu.HBM)
-    fwd, bwd, gated_grad, conv_grad, leading, weight = pl.pallas_call(
-        functools.partial(front_body, 2),
-        out_shape=[bands, bands] + [jax.ShapeDtypeStruct(*s) for s in (tile32, tile, tile)] + [pltpu.VMEM(out_weight.shape, BF16)],
-        in_specs=[hbm] * 5,
-        out_specs=[VMEM] * 6,
+    staged = n == 8 and lax.axis_size("dp") == 4
+    some, rest = (3, 1), (2, 0)
+    if staged:
+        at = lambda pairs: [block_columns(offset, sibling, width) for sibling, offsets in pairs for offset in offsets]
+        blocks = functools.partial(at, ((True, some), (True, rest), (False, some)))
+        late = functools.partial(at, ((False, rest),))
+        early_count, late_count = 6, 2
+    else:
+        early_count, late_count = 8, 0
+        step = out_weight.shape[1] // early_count
+        blocks, late = lambda: [pl.ds(k * step, step) for k in range(early_count)], lambda: []
+    late_rows = max(late_count * width, LANES)
+    fwd, bwd, total, late_grad, weight = pl.pallas_call(
+        functools.partial(front_body, blocks, late, 6),
+        out_shape=[bands, bands] + [jax.ShapeDtypeStruct(*s) for s in (((chan, rows), F32), ((late_rows, rows), BF16))]
+        + [pltpu.VMEM(out_weight.shape, BF16)],
+        in_specs=[pl.BlockSpec(memory_space=pltpu.HBM)] * 4,
+        out_specs=[VMEM] * 5,
         scratch_shapes=[
             pltpu.VMEM(doc.shape, jnp.int32), pltpu.VMEM((groups, taps), F32), pltpu.VMEM((groups, taps), F32),
-            pltpu.VMEM(out_grad.shape, BF16), pltpu.VMEM(out_grad.shape[::-1], BF16), pltpu.VMEM(queries.shape, BF16),
-            pltpu.SemaphoreType.DMA((max(1, chan // (2 * LANES)),)), pltpu.SemaphoreType.DMA((4,)),
+            pltpu.VMEM(out_grad.shape, BF16), pltpu.SemaphoreType.DMA((2,)),
+            pltpu.SemaphoreType.DMA((early_count + late_count,)), pltpu.SemaphoreType.DMA((early_count,)),
         ],
         compiler_params=pltpu.CompilerParams(vmem_limit_bytes=16 * MIB),
-        cost_estimate=cost(6.5),
+        cost_estimate=cost(6.0),
         name="front",
-    )(*(pltpu.with_memory_space_constraint(v, pltpu.HBM) for v in (doc, filters, out_grad, out_weight, queries)))
+    )(*(pltpu.with_memory_space_constraint(v, pltpu.HBM) for v in (doc, filters, out_grad, out_weight)))
     fwd, bwd = held_in_vmem(fwd), held_in_vmem(bwd)
 
-    if n == 8:
-        some, rest = (3, 1), (2, 0)
+    landed = [pltpu.SemaphoreType.DMA((max(1, late_count),))]
+    finish_gated = functools.partial(gated_grad_body, late)
+    if staged:
         pair = ((2 * rows, width), BF16)
         weight, conv, gated, first = call(
-            functools.partial(conv_body, member, some), (fwd, mixed, before, queries, weight),
-            [tile32, tile, pair], "conv", 1.9, held=4,
+            functools.partial(conv_body, member, some, late), (out_weight, fwd, mixed, before, queries, weight),
+            [tile32, tile, pair], "conv", 1.9, held=5, hbm=1, scratch=landed,
         )
         first = swap(first, 1)
         weight, second = call(functools.partial(part_body, rest, True), (weight, gated), [pair], "part_rest", 0.8, held=0)
         second = swap(second, 1)
+        weight, gated_grad, conv_grad, leading = call(
+            finish_gated, (doc, weight, total, late_grad, queries), [tile32, tile, tile], "gated_grad", 1.5, held=1
+        )
         weight, far, near_x = call(
             functools.partial(part_body, some, False), (weight, gated, first), [block, block], "sum_some", 0.8, held=0
         )
@@ -284,12 +327,14 @@
         weight, near_y, own = call(
             functools.partial(part_body, rest, False), (weight, gated, second), [block, block], "sum_rest", 0.8, held=0
         )
-        near_y, leading, conv_grad = lax.optimization_barrier((near_y, leading, conv_grad))
         near_y = swap(near_y, 4)
-        output = sum(v.astype(F32) for v in (own, near_x, near_y, far)).astype(BF16)
     else:
         weight, conv, gated = call(
-            functools.partial(conv_body, member, ()), (fwd, mixed, before, queries, weight), [tile32, tile], "conv", 1.2, held=4
+            functools.partial(conv_body, member, (), late), (out_weight, fwd, mixed, before, queries, weight),
+            [tile32, tile], "conv", 1.2, held=5, hbm=1, scratch=landed,
+        )
+        weight, gated_grad, conv_grad, leading = call(
+            finish_gated, (doc, weight, total, late_grad, queries), [tile32, tile, tile], "gated_grad", 1.5, held=1
         )
         partial_out = jnp.dot(gated, out_weight, preferred_element_type=F32).astype(BF16)
         output = lax.psum_scatter(partial_out, "tensor", scatter_dimension=1, tiled=True)
@@ -299,11 +344,22 @@
         functools.partial(filter_grad_body, member, scale), (doc, conv_grad, mixed, before),
         [((groups, taps), F32)], "filter_grad", 1.7, scratch=[pltpu.VMEM((groups, SUBLANES, taps), F32)],
     )
-    terms = over_dp(terms)
-    q_grad, k_grad, v_grad, filter_grad = call(
-        functools.partial(input_grads_body, member), (bwd, conv_grad, after, keys, values, gated_grad, conv, *terms),
-        [tile, tile, tile, ((groups, taps), F32)], "input_grads", 2.0,
-    )
+    if staged:
+        terms = terms + lax.ppermute(terms, "dp", [(i, i ^ 1) for i in range(4)])
+        terms = (terms, turn(terms, 2))
+    else:
+        terms = (lax.psum(terms, "dp"),)
+    q_grad, k_grad, v_grad = call(
+        functools.partial(input_grads_body, member), (bwd, conv_grad, after, keys, values, gated_grad, conv),
+        [tile, tile, tile], "input_grads", 2.0,
+    )
+    if staged:
+        output, filter_grad = call(
+            functools.partial(finish_body, len(terms)), (*terms, own, near_x, near_y, far),
+            [block, ((groups, taps), F32)], "finish", 0.9,
+        )
+    else:
+        filter_grad = sum(terms)
     return (output, q_grad, k_grad, v_grad, filter_grad)
 
 

time: 40.8 us -> 37.8 us (0.926)
  waiting for transfers between devices: 4.75 us -> 1.96 us
  other arithmetic: 2.01 us -> 1.14 us
  Pallas kernels: 16.7 us -> 17.4 us
    ppermute x5, waiting for transfers between devices: 3.77 us -> 0.06 us  [swap(): lax.ppermute(value, 'tensor', [(i, i ^ mask) for i in range(devices)])]
    ppermute x3 -> x2, waiting for transfers between devices: 0.97 us -> 1.9 us  [the longest x1 1.89 us: on_device(): terms = terms + lax.ppermute(terms, 'dp', [(i, i ^ 1) for i in range(4)])]
    convert_element_type x1 -> x0, other arithmetic: 0.87 us -> none  [on_device(): sum((v.astype(F32) for v in (own, near_x, near_y, far))).astype(BF16)]
    pallas_call x7 -> x9, Pallas kernels: 16.7 us -> 17.4 us  [the longest x8 10.6 us: call(): pl.pallas_call(body, out_shape=shapes, in_specs=[pl.BlockSpec(memory_spac...]
    ppermute x3 -> x2, starting transfers between devices: 5.7 us -> 5.71 us  [the longest x1 3.02 us: turn(): lax.ppermute(value, 'dp', [(i, (i + by) % devices) for i in range(devices)])]
  transfers between devices with their start and end apart: 10 -> 9, of which waited for: 4 -> 1; matrix products, arithmetic and copies ran while one was open for 2% -> 0% of each run, Pallas kernels for 29% -> 38%
where the time goes in v3:
time: 37.8 us; the launch traced here: 37.6 us
  Pallas kernels  17.4 us (46%)
  starting transfers between devices  16.3 us (43%)
  waiting for transfers between devices  1.96 us (5%)
  other arithmetic  1.14 us (3%)
  between operations  0.78 us (2%)
    pallas_call x8, Pallas kernels, call(): pl.pallas_call(body, out_shape=shapes, in_specs=[pl.BlockSpec(memory_spac...  10.6 us
    pallas_call x1, Pallas kernels, on_device(): pl.pallas_call(functools.partial(front_body, blocks, late, 6), out_shape=...  6.85 us
    ppermute x2, starting transfers between devices, shift(): lax.ppermute(value, axis, [(i, i + by) for i in range(devices) if 0 <= i...  6.41 us
    ppermute x5, starting transfers between devices, swap(): lax.ppermute(value, 'tensor', [(i, i ^ mask) for i in range(devices)])  4.17 us
    ppermute x1, starting transfers between devices, turn(): lax.ppermute(value, 'dp', [(i, (i + by) % devices) for i in range(devices)])  3.02 us
    ppermute x1, starting transfers between devices, on_device(): terms = terms + lax.ppermute(terms, 'dp', [(i, i ^ 1) for i in range(4)])  2.7 us
    ppermute x1, waiting for transfers between devices, on_device(): terms = terms + lax.ppermute(terms, 'dp', [(i, i ^ 1) for i in range(4)])  1.89 us
    convert_element_type x1, other arithmetic, on_device(): mixed = (keys.astype(F32) * values.astype(F32)).astype(BF16)  1.14 us
  transfers between devices with their start and end apart: 9, of which 1 were waited for; matrix products, arithmetic and copies ran while one was open for 0% of the time, Pallas kernels for 38%

profile of v3, /device:TPU:0, one launch (start us, length us, event | category | flops | bytes accessed | tf_op | source)
XLA Modules:
  0.0 37.6 jit_solution(1357474468516088402)
XLA Ops:
  0.6 1.1 %multiply_convert_fusion.mixed_ref = bf16[128,1024]{1,0:T(8,128)(2,1)S(1)} fusion(bf16[128,1024]{1,0:T(8,128)(2,1)} %values_ref.1, bf16[128,1024]{1,0:T(8,128)(2,1)} %keys_ref.1), kind=kLoop, calls=%fused_computation | loop fusion | flops 524288 | bytes 786432 | tf_op jit(solution)/shard_map/convert_element_type | solution.py:278
  1.8 4.9 %collective-permute-start = (bf16[128,1024]{1,0:T(8,128)(2,1)S(1)}, bf16[128,1024]{1,0:T(8,128)(2,1)S(1)}, u32[]{:S(2)}, u32[]{:S(2)}) collective-permute-start(bf16[128,1024]{1,0:T(8,128)(2,1)S(1)} %multiply_convert_fusion.mixed_ref), channel_id=1, source_target_pairs={{0,8},{8,16},{16,24},{1,9},{9,17},{17,25},{2,10},{10,18},{18,26},{... | collective-permute-start | bytes 786440 | tf_op jit(solution)/shard_map/ppermute | solution.py:254
  6.7 6.8 %front.1 = (bf16[8192,256]{1,0:T(8,128)(2,1)S(1)}, bf16[8192,256]{1,0:T(8,128)(2,1)S(1)}, f32[1024,128]{1,0:T(8,128)S(1)}, bf16[2048,128]{1,0:T(8,128)(2,1)S(1)}, bf16[1024,8192]{1,0:T(8,128)(2,1)S(1)}) custom-call(s32[1,128]{1,0:T(1,128)} %bitcast.1, f32[64,128]{1,0:T(8,128)} %filt_hbm.1, bf16[128,8192]{1,0:T(8,128)(2,1)} %grad_hbm.1, ...), custom_call_target="tpu_custom_call" | custom-call | flops 6600000000 | bytes 21600000 | tf_op jit(solution)/shard_map/front/pallas_call | solution.py:292
  13.6 2.3 %conv.1 = (bf16[1024,8192]{1,0:T(8,128)(2,1)S(1)}, f32[128,1024]{1,0:T(8,128)S(1)}, bf16[128,1024]{1,0:T(8,128)(2,1)S(1)}, bf16[256,1024]{1,0:T(8,128)(2,1)S(1)}) custom-call(bf16[1024,8192]{1,0:T(8,128)(2,1)} %weight_hbm.3, bf16[8192,256]{1,0:T(8,128)(2,1)S(1)} %get-tuple-element.30.band_ref, ...), custom_call_target="tpu_custom_call", output_to_operand_aliasing={{0}: (5, {})} | custom-call | flops 2090000000 | bytes 6840000 | tf_op jit(solution)/shard_map/conv/pallas_call | solution.py:31
  15.9 0.0 copy-start.3
  15.9 0.1 collective-permute-start.3
  16.0 0.7 %part_rest.1 = (bf16[1024,8192]{1,0:T(8,128)(2,1)S(1)}, bf16[256,1024]{1,0:T(8,128)(2,1)S(1)}) custom-call(bf16[1024,8192]{1,0:T(8,128)(2,1)S(1)} %get-tuple-element.32.weight_ref, bf16[128,1024]{1,0:T(8,128)(2,1)S(1)} %get-tuple-element.33.gated_ref), custom_call_target="tpu_custom_call", output_to_operand_aliasing={{0}: (0, {})} | custom-call | flops 880000000 | bytes 2880000 | tf_op jit(solution)/shard_map/part_rest/pallas_call | solution.py:31
  16.7 0.6 %collective-permute-start.4 = (bf16[256,1024]{1,0:T(8,128)(2,1)S(1)}, bf16[256,1024]{1,0:T(8,128)(2,1)S(1)}, u32[]{:S(2)}, u32[]{:S(2)}) collective-permute-start(bf16[256,1024]{1,0:T(8,128)(2,1)S(1)} %get-tuple-element.41), channel_id=1, source_target_pairs={{0,1},{1,0},{2,3},{3,2},{4,5},{5,4},{6,7},{7,6},{8,9},{9,8},{10,11... | collective-permute-start | bytes 1572872 | tf_op jit(solution)/shard_map/ppermute | solution.py:259
  17.3 1.3 %gated_grad.1 = (bf16[1024,8192]{1,0:T(8,128)(2,1)S(1)}, f32[128,1024]{1,0:T(8,128)S(1)}, bf16[128,1024]{1,0:T(8,128)(2,1)S(1)}, bf16[128,1024]{1,0:T(8,128)(2,1)S(1)}) custom-call(s32[1,128]{1,0:T(1,128)S(1)} %bitcast.2, bf16[1024,8192]{1,0:T(8,128)(2,1)S(1)} %get-tuple-element.34.weight_ref, ...), custom_call_target="tpu_custom_call", output_to_operand_aliasing={{0}: (1, {})} | custom-call | flops 1650000000 | bytes 5400000 | tf_op jit(solution)/shard_map/gated_grad/pallas_call | solution.py:31
  18.6 1.5 %collective-permute-start.8 = (bf16[128,1024]{1,0:T(8,128)(2,1)S(1)}, bf16[128,1024]{1,0:T(8,128)(2,1)S(1)}, u32[]{:S(2)}, u32[]{:S(2)}) collective-permute-start(bf16[128,1024]{1,0:T(8,128)(2,1)S(1)} %get-tuple-element.48), channel_id=1, source_target_pairs={{8,0},{16,8},{24,16},{9,1},{17,9},{25,17},{10,2},{18,10},{26,18},{... | collective-permute-start | bytes 786440 | tf_op jit(solution)/shard_map/ppermute | solution.py:254
  20.1 0.0 copy-start.1
  20.1 0.0 copy-start.2
  20.1 0.8 %sum_some.1 = (bf16[1024,8192]{1,0:T(8,128)(2,1)S(1)}, bf16[128,1024]{1,0:T(8,128)(2,1)S(1)}, bf16[128,1024]{1,0:T(8,128)(2,1)S(1)}) custom-call(bf16[1024,8192]{1,0:T(8,128)(2,1)S(1)} %get-tuple-element.38.weight_ref, bf16[128,1024]{1,0:T(8,128)(2,1)S(1)} %get-tuple-element.33.gated_ref, ...), custom_call_target="tpu_custom_call", output_to_operand_aliasing={{0}: (0, {})} | custom-call | flops 880000000 | bytes 2880000 | tf_op jit(solution)/shard_map/sum_some/pallas_call | solution.py:31
  20.9 0.8 %sum_rest.1 = (bf16[1024,8192]{1,0:T(8,128)(2,1)S(1)}, bf16[128,1024]{1,0:T(8,128)(2,1)S(1)}, bf16[128,1024]{1,0:T(8,128)(2,1)S(1)}) custom-call(bf16[1024,8192]{1,0:T(8,128)(2,1)S(1)} %get-tuple-element.40.weight_ref, bf16[128,1024]{1,0:T(8,128)(2,1)S(1)} %get-tuple-element.33.gated_ref, ...), custom_call_target="tpu_custom_call", output_to_operand_aliasing={{0}: (0, {})} | custom-call | flops 880000000 | bytes 2880000 | tf_op jit(solution)/shard_map/sum_rest/pallas_call | solution.py:31
  21.7 1.6 %collective-permute-start.6 = (bf16[128,1024]{1,0:T(8,128)(2,1)S(1)}, bf16[128,1024]{1,0:T(8,128)(2,1)S(1)}, u32[]{:S(2)}, u32[]{:S(2)}) collective-permute-start(bf16[128,1024]{1,0:T(8,128)(2,1)S(1)} %get-tuple-element.44), channel_id=1, source_target_pairs={{0,4},{1,5},{2,6},{3,7},{4,0},{5,1},{6,2},{7,3},{8,12},{9,13},{10,... | collective-permute-start | bytes 786440 | tf_op jit(solution)/shard_map/ppermute | solution.py:259
  23.3 1.5 %collective-permute-start.5 = (bf16[128,1024]{1,0:T(8,128)(2,1)S(1)}, bf16[128,1024]{1,0:T(8,128)(2,1)S(1)}, u32[]{:S(2)}, u32[]{:S(2)}) collective-permute-start(bf16[128,1024]{1,0:T(8,128)(2,1)S(1)} %get-tuple-element.43), channel_id=1, source_target_pairs={{0,2},{1,3},{2,0},{3,1},{4,6},{5,7},{6,4},{7,5},{8,10},{9,11},{10,... | collective-permute-start | bytes 786440 | tf_op jit(solution)/shard_map/ppermute | solution.py:259
  24.8 0.5 %collective-permute-start.7 = (bf16[128,1024]{1,0:T(8,128)(2,1)S(1)}, bf16[128,1024]{1,0:T(8,128)(2,1)S(1)}, u32[]{:S(2)}, u32[]{:S(2)}) collective-permute-start(bf16[128,1024]{1,0:T(8,128)(2,1)S(1)} %get-tuple-element.45), channel_id=1, source_target_pairs={{0,6},{1,7},{2,4},{3,5},{4,2},{5,3},{6,0},{7,1},{8,14},{9,15},{10,... | collective-permute-start | bytes 786440 | tf_op jit(solution)/shard_map/ppermute | solution.py:259
  25.2 1.6 %filter_grad.1 = f32[64,128]{1,0:T(8,128)S(1)} custom-call(s32[1,128]{1,0:T(1,128)S(1)} %bitcast.3, bf16[128,1024]{1,0:T(8,128)(2,1)S(1)} %get-tuple-element.37.grad_ref, bf16[128,1024]{1,0:T(8,128)(2,1)S(1)} %multiply_convert_fusion.mixed_ref, bf16[128,1024]{1,0:T(8,128)(2,1)S(1)} %collective-permute-done.before_ref), custom_call_target="tpu_custom_call" | custom-call | flops 1870000000 | bytes 6120000 | tf_op jit(solution)/shard_map/filter_grad/pallas_call | solution.py:31
  26.9 2.7 %collective-permute-start.1 = (f32[64,128]{1,0:T(8,128)S(1)}, f32[64,128]{1,0:T(8,128)S(1)}, u32[]{:S(2)}, u32[]{:S(2)}) collective-permute-start(f32[64,128]{1,0:T(8,128)S(1)} %filter_grad.1), channel_id=1, source_target_pairs={{0,8},{8,0},{16,24},{24,16},{1,9},{9,1},{17,25},{25,17},{2,10},{10... | collective-permute-start | bytes 98312 | tf_op jit(solution)/shard_map/ppermute | solution.py:348
  29.6 1.9 %collective-permute-done.1 = f32[64,128]{1,0:T(8,128)S(1)} collective-permute-done((f32[64,128]{1,0:T(8,128)S(1)}, f32[64,128]{1,0:T(8,128)S(1)}, u32[]{:S(2)}, u32[]{:S(2)}) %collective-permute-start.1) | collective-permute-done | bytes 32800 | tf_op jit(solution)/shard_map/ppermute | solution.py:348
  31.5 3.0 %collective-permute-start.2 = (f32[64,128]{1,0:T(8,128)S(1)}, f32[64,128]{1,0:T(8,128)S(1)}, u32[]{:S(2)}, u32[]{:S(2)}) collective-permute-start(f32[64,128]{1,0:T(8,128)S(1)} %add.3.refs_0_), channel_id=1, source_target_pairs={{0,16},{8,24},{16,0},{24,8},{1,17},{9,25},{17,1},{25,9},{2,18},{10... | collective-permute-start | bytes 98312 | tf_op jit(solution)/shard_map/ppermute | solution.py:264
  34.5 2.2 %input_grads.1 = (bf16[128,1024]{1,0:T(8,128)(2,1)}, bf16[128,1024]{1,0:T(8,128)(2,1)}, bf16[128,1024]{1,0:T(8,128)(2,1)}) custom-call(bf16[8192,256]{1,0:T(8,128)(2,1)S(1)} %get-tuple-element.47.band_ref, bf16[128,1024]{1,0:T(8,128)(2,1)S(1)} %get-tuple-element.37.grad_ref, bf16[128,1024]{1,0:T(8,128)(2,1)S(1)} %collective-permute-done.8.after_ref, ...), custom_call_target="tpu_custom_call" | custom-call | flops 2200000000 | bytes 7200000 | tf_op jit(solution)/shard_map/input_grads/pallas_call | solution.py:31
  36.7 0.0 collective-permute-done.7.refs_5_
  36.8 0.9 %finish.1 = (bf16[128,1024]{1,0:T(8,128)(2,1)}, f32[64,128]{1,0:T(8,128)}) custom-call(f32[64,128]{1,0:T(8,128)S(1)} %add.3.refs_0_, f32[64,128]{1,0:T(8,128)S(1)} %collective-permute-done.2.refs_1_, bf16[128,1024]{1,0:T(8,128)(2,1)S(1)} %get-tuple-element.42.refs_2_, bf16[128,1024]{1,0:T(8,128)(2,1)S(1)} %collective-permute-done.5.refs_3_, ...), custom_call_target="tpu_custom_call" | custom-call | flops 990000000 | bytes 3240000 | tf_op jit(solution)/shard_map/finish/pallas_call | solution.py:31
  (13 shorter events, 0.0 us)
Async XLA Ops:
  0.6 13.0 %copy-start = (bf16[128,1024]{1,0:T(8,128)(2,1)S(1)}, bf16[128,1024]{1,0:T(8,128)(2,1)}, u32[]{:S(2)}) copy-start(bf16[128,1024]{1,0:T(8,128)(2,1)} %queries_ref.3) | copy-start | bytes 786436
  1.8 11.8 %collective-permute-start = (bf16[128,1024]{1,0:T(8,128)(2,1)S(1)}, bf16[128,1024]{1,0:T(8,128)(2,1)S(1)}, u32[]{:S(2)}, u32[]{:S(2)}) collective-permute-start(bf16[128,1024]{1,0:T(8,128)(2,1)S(1)} %multiply_convert_fusion.mixed_ref), channel_id=1, source_target_pairs={{0,8},{8,16},{16,24},{1,9},{9,17},{17,25},{2,10},{10,18},{18,26},{... | collective-permute-start | bytes 786440 | tf_op jit(solution)/shard_map/ppermute | solution.py:254
  15.9 1.4 %copy-start.3 = (s32[128]{0:T(128)S(1)}, s32[128]{0:T(128)}, u32[]{:S(2)}) copy-start(s32[128]{0:T(128)} %param.10) | copy-start | bytes 1540
  15.9 4.2 %collective-permute-start.3 = (bf16[256,1024]{1,0:T(8,128)(2,1)S(1)}, bf16[256,1024]{1,0:T(8,128)(2,1)S(1)}, u32[]{:S(2)}, u32[]{:S(2)}) collective-permute-start(bf16[256,1024]{1,0:T(8,128)(2,1)S(1)} %get-tuple-element.39), channel_id=1, source_target_pairs={{0,1},{1,0},{2,3},{3,2},{4,5},{5,4},{6,7},{7,6},{8,9},{9,8},{10,11... | collective-permute-start | bytes 1572872 | tf_op jit(solution)/shard_map/ppermute | solution.py:259
  16.7 4.2 %collective-permute-start.4 = (bf16[256,1024]{1,0:T(8,128)(2,1)S(1)}, bf16[256,1024]{1,0:T(8,128)(2,1)S(1)}, u32[]{:S(2)}, u32[]{:S(2)}) collective-permute-start(bf16[256,1024]{1,0:T(8,128)(2,1)S(1)} %get-tuple-element.41), channel_id=1, source_target_pairs={{0,1},{1,0},{2,3},{3,2},{4,5},{5,4},{6,7},{7,6},{8,9},{9,8},{10,11... | collective-permute-start | bytes 1572872 | tf_op jit(solution)/shard_map/ppermute | solution.py:259
  18.6 15.9 %collective-permute-start.8 = (bf16[128,1024]{1,0:T(8,128)(2,1)S(1)}, bf16[128,1024]{1,0:T(8,128)(2,1)S(1)}, u32[]{:S(2)}, u32[]{:S(2)}) collective-permute-start(bf16[128,1024]{1,0:T(8,128)(2,1)S(1)} %get-tuple-element.48), channel_id=1, source_target_pairs={{8,0},{16,8},{24,16},{9,1},{17,9},{25,17},{10,2},{18,10},{26,18},{... | collective-permute-start | bytes 786440 | tf_op jit(solution)/shard_map/ppermute | solution.py:254
  20.1 14.4 %copy-start.1 = (bf16[128,1024]{1,0:T(8,128)(2,1)S(1)}, bf16[128,1024]{1,0:T(8,128)(2,1)}, u32[]{:S(2)}) copy-start(bf16[128,1024]{1,0:T(8,128)(2,1)} %values_ref.1) | copy-start | bytes 786436
  20.1 14.4 %copy-start.2 = (bf16[128,1024]{1,0:T(8,128)(2,1)S(1)}, bf16[128,1024]{1,0:T(8,128)(2,1)}, u32[]{:S(2)}) copy-start(bf16[128,1024]{1,0:T(8,128)(2,1)} %keys_ref.1) | copy-start | bytes 786436
  21.7 15.0 %collective-permute-start.6 = (bf16[128,1024]{1,0:T(8,128)(2,1)S(1)}, bf16[128,1024]{1,0:T(8,128)(2,1)S(1)}, u32[]{:S(2)}, u32[]{:S(2)}) collective-permute-start(bf16[128,1024]{1,0:T(8,128)(2,1)S(1)} %get-tuple-element.44), channel_id=1, source_target_pairs={{0,4},{1,5},{2,6},{3,7},{4,0},{5,1},{6,2},{7,3},{8,12},{9,13},{10,... | collective-permute-start | bytes 786440 | tf_op jit(solution)/shard_map/ppermute | solution.py:259
  23.3 13.5 %collective-permute-start.5 = (bf16[128,1024]{1,0:T(8,128)(2,1)S(1)}, bf16[128,1024]{1,0:T(8,128)(2,1)S(1)}, u32[]{:S(2)}, u32[]{:S(2)}) collective-permute-start(bf16[128,1024]{1,0:T(8,128)(2,1)S(1)} %get-tuple-element.43), channel_id=1, source_target_pairs={{0,2},{1,3},{2,0},{3,1},{4,6},{5,7},{6,4},{7,5},{8,10},{9,11},{10,... | collective-permute-start | bytes 786440 | tf_op jit(solution)/shard_map/ppermute | solution.py:259
  24.8 12.0 %collective-permute-start.7 = (bf16[128,1024]{1,0:T(8,128)(2,1)S(1)}, bf16[128,1024]{1,0:T(8,128)(2,1)S(1)}, u32[]{:S(2)}, u32[]{:S(2)}) collective-permute-start(bf16[128,1024]{1,0:T(8,128)(2,1)S(1)} %get-tuple-element.45), channel_id=1, source_target_pairs={{0,6},{1,7},{2,4},{3,5},{4,2},{5,3},{6,0},{7,1},{8,14},{9,15},{10,... | collective-permute-start | bytes 786440 | tf_op jit(solution)/shard_map/ppermute | solution.py:259
  26.9 4.6 %collective-permute-start.1 = (f32[64,128]{1,0:T(8,128)S(1)}, f32[64,128]{1,0:T(8,128)S(1)}, u32[]{:S(2)}, u32[]{:S(2)}) collective-permute-start(f32[64,128]{1,0:T(8,128)S(1)} %filter_grad.1), channel_id=1, source_target_pairs={{0,8},{8,0},{16,24},{24,16},{1,9},{9,1},{17,25},{25,17},{2,10},{10... | collective-permute-start | bytes 98312 | tf_op jit(solution)/shard_map/ppermute | solution.py:348
  31.5 5.2 %collective-permute-start.2 = (f32[64,128]{1,0:T(8,128)S(1)}, f32[64,128]{1,0:T(8,128)S(1)}, u32[]{:S(2)}, u32[]{:S(2)}) collective-permute-start(f32[64,128]{1,0:T(8,128)S(1)} %add.3.refs_0_), channel_id=1, source_target_pairs={{0,16},{8,24},{16,0},{24,8},{1,17},{9,25},{17,1},{25,9},{2,18},{10... | collective-permute-start | bytes 98312 | tf_op jit(solution)/shard_map/ppermute | solution.py:264

commit v4 on v3

--- a/solution.py
+++ b/solution.py
@@ -85,7 +85,7 @@
     groups, taps = filt_ref.shape
     blocks, late = blocks(), late()
     count = len(blocks)
-    share = -(-groups // count)
+    share = -(-groups // max(1, count - 1))
     small = [
         pltpu.make_async_copy(src, dst, came.at[k])
         for k, (src, dst) in enumerate(((doc_hbm, doc_ref), (filt_hbm, filt_ref)))
@@ -281,16 +281,16 @@
     some, rest = (3, 1), (2, 0)
     if staged:
         at = lambda pairs: [block_columns(offset, sibling, width) for sibling, offsets in pairs for offset in offsets]
-        blocks = functools.partial(at, ((True, some), (True, rest), (False, some)))
-        late = functools.partial(at, ((False, rest),))
-        early_count, late_count = 6, 2
+        blocks = functools.partial(at, ((True, some), (True, rest), (False, (3, 1, 2))))
+        late = functools.partial(at, ((False, (0,)),))
+        early_count, late_count = 7, 1
     else:
         early_count, late_count = 8, 0
         step = out_weight.shape[1] // early_count
         blocks, late = lambda: [pl.ds(k * step, step) for k in range(early_count)], lambda: []
     late_rows = max(late_count * width, LANES)
     fwd, bwd, total, late_grad, weight = pl.pallas_call(
-        functools.partial(front_body, blocks, late, 6),
+        functools.partial(front_body, blocks, late, 7),
         out_shape=[bands, bands] + [jax.ShapeDtypeStruct(*s) for s in (((chan, rows), F32), ((late_rows, rows), BF16))]
         + [pltpu.VMEM(out_weight.shape, BF16)],
         in_specs=[pl.BlockSpec(memory_space=pltpu.HBM)] * 4,
@@ -309,25 +309,19 @@
     landed = [pltpu.SemaphoreType.DMA((max(1, late_count),))]
     finish_gated = functools.partial(gated_grad_body, late)
     if staged:
-        pair = ((2 * rows, width), BF16)
-        weight, conv, gated, first = call(
-            functools.partial(conv_body, member, some, late), (out_weight, fwd, mixed, before, queries, weight),
-            [tile32, tile, pair], "conv", 1.9, held=5, hbm=1, scratch=landed,
-        )
-        first = swap(first, 1)
-        weight, second = call(functools.partial(part_body, rest, True), (weight, gated), [pair], "part_rest", 0.8, held=0)
-        second = swap(second, 1)
+        stack = ((len(some + rest) * rows, width), BF16)
+        weight, conv, gated, came = call(
+            functools.partial(conv_body, member, some + rest, late), (out_weight, fwd, mixed, before, queries, weight),
+            [tile32, tile, stack], "conv", 2.6, held=5, hbm=1, scratch=landed,
+        )
+        came = swap(came, 1)
         weight, gated_grad, conv_grad, leading = call(
             finish_gated, (doc, weight, total, late_grad, queries), [tile32, tile, tile], "gated_grad", 1.5, held=1
         )
-        weight, far, near_x = call(
-            functools.partial(part_body, some, False), (weight, gated, first), [block, block], "sum_some", 0.8, held=0
-        )
-        far, near_x = swap(far, 6), swap(near_x, 2)
-        weight, near_y, own = call(
-            functools.partial(part_body, rest, False), (weight, gated, second), [block, block], "sum_rest", 0.8, held=0
-        )
-        near_y = swap(near_y, 4)
+        weight, far, near_x, near_y, own = call(
+            functools.partial(part_body, some + rest, False), (weight, gated, came), [block] * 4, "sums", 1.4, held=0
+        )
+        far, near_x, near_y = swap(far, 6), swap(near_x, 2), swap(near_y, 4)
     else:
         weight, conv, gated = call(
             functools.partial(conv_body, member, (), late), (out_weight, fwd, mixed, before, queries, weight),

time: 37.8 us -> 37.1 us (0.981)
  Pallas kernels: 17.4 us -> 16.6 us
  waiting for transfers between devices: 1.96 us -> 2.67 us
  starting transfers between devices: 16.3 us -> 15.7 us
    pallas_call x8 -> x6, Pallas kernels: 10.6 us -> 9.25 us  [call(): pl.pallas_call(body, out_shape=shapes, in_specs=[pl.BlockSpec(memory_spac...]
    ppermute x5 -> x4, waiting for transfers between devices: 0.06 us -> 0.77 us  [swap(): lax.ppermute(value, 'tensor', [(i, i ^ mask) for i in range(devices)])]
    ppermute x5 -> x4, starting transfers between devices: 4.17 us -> 3.62 us  [swap(): lax.ppermute(value, 'tensor', [(i, i ^ mask) for i in range(devices)])]
    pallas_call x1, Pallas kernels: 6.85 us -> 7.36 us  [on_device(): pl.pallas_call(functools.partial(front_body, blocks, late, 7), out_shape=...]
  transfers between devices with their start and end apart: 9 -> 8, of which waited for: 1 -> 3; matrix products, arithmetic and copies ran while one was open for 0% -> 0% of each run, Pallas kernels for 38% -> 36%
where the time goes in v4:
time: 37.1 us; the launch traced here: 36.9 us
  Pallas kernels  16.6 us (45%)
  starting transfers between devices  15.7 us (42%)
  waiting for transfers between devices  2.67 us (7%)
  other arithmetic  1.14 us (3%)
  between operations  0.75 us (2%)
    pallas_call x6, Pallas kernels, call(): pl.pallas_call(body, out_shape=shapes, in_specs=[pl.BlockSpec(memory_spac...  9.25 us
    pallas_call x1, Pallas kernels, on_device(): pl.pallas_call(functools.partial(front_body, blocks, late, 7), out_shape=...  7.36 us
    ppermute x2, starting transfers between devices, shift(): lax.ppermute(value, axis, [(i, i + by) for i in range(devices) if 0 <= i...  6.55 us
    ppermute x4, starting transfers between devices, swap(): lax.ppermute(value, 'tensor', [(i, i ^ mask) for i in range(devices)])  3.62 us
    ppermute x1, starting transfers between devices, turn(): lax.ppermute(value, 'dp', [(i, (i + by) % devices) for i in range(devices)])  3.03 us
    ppermute x1, starting transfers between devices, on_device(): terms = terms + lax.ppermute(terms, 'dp', [(i, i ^ 1) for i in range(4)])  2.5 us
    ppermute x1, waiting for transfers between devices, on_device(): terms = terms + lax.ppermute(terms, 'dp', [(i, i ^ 1) for i in range(4)])  1.89 us
    convert_element_type x1, other arithmetic, on_device(): mixed = (keys.astype(F32) * values.astype(F32)).astype(BF16)  1.14 us
  transfers between devices with their start and end apart: 8, of which 3 were waited for; matrix products, arithmetic and copies ran while one was open for 0% of the time, Pallas kernels for 36%

profile of v4, /device:TPU:0, one launch (start us, length us, event | category | flops | bytes accessed | tf_op | source)
XLA Modules:
  0.0 36.9 jit_solution(15263232981038392846)
XLA Ops:
  0.6 1.1 %multiply_convert_fusion.mixed_ref = bf16[128,1024]{1,0:T(8,128)(2,1)S(1)} fusion(bf16[128,1024]{1,0:T(8,128)(2,1)} %values_ref.1, bf16[128,1024]{1,0:T(8,128)(2,1)} %keys_ref.1), kind=kLoop, calls=%fused_computation | loop fusion | flops 524288 | bytes 786432 | tf_op jit(solution)/shard_map/convert_element_type | solution.py:278
  1.8 4.9 %collective-permute-start = (bf16[128,1024]{1,0:T(8,128)(2,1)S(1)}, bf16[128,1024]{1,0:T(8,128)(2,1)S(1)}, u32[]{:S(2)}, u32[]{:S(2)}) collective-permute-start(bf16[128,1024]{1,0:T(8,128)(2,1)S(1)} %multiply_convert_fusion.mixed_ref), channel_id=1, source_target_pairs={{0,8},{8,16},{16,24},{1,9},{9,17},{17,25},{2,10},{10,18},{18,26},{... | collective-permute-start | bytes 786440 | tf_op jit(solution)/shard_map/ppermute | solution.py:254
  6.7 7.4 %front.1 = (bf16[8192,256]{1,0:T(8,128)(2,1)S(1)}, bf16[8192,256]{1,0:T(8,128)(2,1)S(1)}, f32[1024,128]{1,0:T(8,128)S(1)}, bf16[1024,128]{1,0:T(8,128)(2,1)S(1)}, bf16[1024,8192]{1,0:T(8,128)(2,1)S(1)}) custom-call(s32[1,128]{1,0:T(1,128)} %bitcast.1, f32[64,128]{1,0:T(8,128)} %filt_hbm.1, bf16[128,8192]{1,0:T(8,128)(2,1)} %grad_hbm.1, ...), custom_call_target="tpu_custom_call" | custom-call | flops 6600000000 | bytes 21600000 | tf_op jit(solution)/shard_map/front/pallas_call | solution.py:292
  14.1 0.0 collective-permute-done.before_ref
  14.1 0.0 copy-start.3
  14.1 2.4 %conv.1 = (bf16[1024,8192]{1,0:T(8,128)(2,1)S(1)}, f32[128,1024]{1,0:T(8,128)S(1)}, bf16[128,1024]{1,0:T(8,128)(2,1)S(1)}, bf16[512,1024]{1,0:T(8,128)(2,1)S(1)}) custom-call(bf16[1024,8192]{1,0:T(8,128)(2,1)} %weight_hbm.3, bf16[8192,256]{1,0:T(8,128)(2,1)S(1)} %get-tuple-element.27.band_ref, ...), custom_call_target="tpu_custom_call", output_to_operand_aliasing={{0}: (5, {})} | custom-call | flops 2860000000 | bytes 9360000 | tf_op jit(solution)/shard_map/conv/pallas_call | solution.py:31
  16.5 0.1 collective-permute-start.3
  16.6 0.8 %gated_grad.1 = (bf16[1024,8192]{1,0:T(8,128)(2,1)S(1)}, f32[128,1024]{1,0:T(8,128)S(1)}, bf16[128,1024]{1,0:T(8,128)(2,1)S(1)}, bf16[128,1024]{1,0:T(8,128)(2,1)S(1)}) custom-call(s32[1,128]{1,0:T(1,128)S(1)} %bitcast.2, bf16[1024,8192]{1,0:T(8,128)(2,1)S(1)} %get-tuple-element.29.weight_ref, ...), custom_call_target="tpu_custom_call", output_to_operand_aliasing={{0}: (1, {})} | custom-call | flops 1650000000 | bytes 5400000 | tf_op jit(solution)/shard_map/gated_grad/pallas_call | solution.py:31
  17.4 0.0 copy-start.2
  17.4 1.6 %collective-permute-start.7 = (bf16[128,1024]{1,0:T(8,128)(2,1)S(1)}, bf16[128,1024]{1,0:T(8,128)(2,1)S(1)}, u32[]{:S(2)}, u32[]{:S(2)}) collective-permute-start(bf16[128,1024]{1,0:T(8,128)(2,1)S(1)} %get-tuple-element.42), channel_id=1, source_target_pairs={{8,0},{16,8},{24,16},{9,1},{17,9},{25,17},{10,2},{18,10},{26,18},{... | collective-permute-start | bytes 786440 | tf_op jit(solution)/shard_map/ppermute | solution.py:254
  19.1 0.2 collective-permute-done.3.refs_0_
  19.3 1.3 %sums.1 = (bf16[1024,8192]{1,0:T(8,128)(2,1)S(1)}, bf16[128,1024]{1,0:T(8,128)(2,1)S(1)}, bf16[128,1024]{1,0:T(8,128)(2,1)S(1)}, bf16[128,1024]{1,0:T(8,128)(2,1)S(1)}, bf16[128,1024]{1,0:T(8,128)(2,1)S(1)}) custom-call(bf16[1024,8192]{1,0:T(8,128)(2,1)S(1)} %get-tuple-element.33.weight_ref, ...), custom_call_target="tpu_custom_call", output_to_operand_aliasing={{0}: (0, {})} | custom-call | flops 1540000000 | bytes 5040000 | tf_op jit(solution)/shard_map/sums/pallas_call | solution.py:31
  20.6 1.6 %collective-permute-start.4 = (bf16[128,1024]{1,0:T(8,128)(2,1)S(1)}, bf16[128,1024]{1,0:T(8,128)(2,1)S(1)}, u32[]{:S(2)}, u32[]{:S(2)}) collective-permute-start(bf16[128,1024]{1,0:T(8,128)(2,1)S(1)} %get-tuple-element.37), channel_id=1, source_target_pairs={{0,2},{1,3},{2,0},{3,1},{4,6},{5,7},{6,4},{7,5},{8,10},{9,11},{10,... | collective-permute-start | bytes 786440 | tf_op jit(solution)/shard_map/ppermute | solution.py:259
  22.2 1.5 %collective-permute-start.5 = (bf16[128,1024]{1,0:T(8,128)(2,1)S(1)}, bf16[128,1024]{1,0:T(8,128)(2,1)S(1)}, u32[]{:S(2)}, u32[]{:S(2)}) collective-permute-start(bf16[128,1024]{1,0:T(8,128)(2,1)S(1)} %get-tuple-element.38), channel_id=1, source_target_pairs={{0,4},{1,5},{2,6},{3,7},{4,0},{5,1},{6,2},{7,3},{8,12},{9,13},{10,... | collective-permute-start | bytes 786440 | tf_op jit(solution)/shard_map/ppermute | solution.py:259
  23.7 0.5 %collective-permute-start.6 = (bf16[128,1024]{1,0:T(8,128)(2,1)S(1)}, bf16[128,1024]{1,0:T(8,128)(2,1)S(1)}, u32[]{:S(2)}, u32[]{:S(2)}) collective-permute-start(bf16[128,1024]{1,0:T(8,128)(2,1)S(1)} %get-tuple-element.39), channel_id=1, source_target_pairs={{0,6},{1,7},{2,4},{3,5},{4,2},{5,3},{6,0},{7,1},{8,14},{9,15},{10,... | collective-permute-start | bytes 786440 | tf_op jit(solution)/shard_map/ppermute | solution.py:259
  24.2 1.6 %filter_grad.1 = f32[64,128]{1,0:T(8,128)S(1)} custom-call(s32[1,128]{1,0:T(1,128)S(1)} %bitcast.3, bf16[128,1024]{1,0:T(8,128)(2,1)S(1)} %get-tuple-element.32.grad_ref, bf16[128,1024]{1,0:T(8,128)(2,1)S(1)} %multiply_convert_fusion.mixed_ref, bf16[128,1024]{1,0:T(8,128)(2,1)S(1)} %collective-permute-done.before_ref), custom_call_target="tpu_custom_call" | custom-call | flops 1870000000 | bytes 6120000 | tf_op jit(solution)/shard_map/filter_grad/pallas_call | solution.py:31
  25.8 2.5 %collective-permute-start.1 = (f32[64,128]{1,0:T(8,128)S(1)}, f32[64,128]{1,0:T(8,128)S(1)}, u32[]{:S(2)}, u32[]{:S(2)}) collective-permute-start(f32[64,128]{1,0:T(8,128)S(1)} %filter_grad.1), channel_id=1, source_target_pairs={{0,8},{8,0},{16,24},{24,16},{1,9},{9,1},{17,25},{25,17},{2,10},{10... | collective-permute-start | bytes 98312 | tf_op jit(solution)/shard_map/ppermute | solution.py:342
  28.3 1.9 %collective-permute-done.1 = f32[64,128]{1,0:T(8,128)S(1)} collective-permute-done((f32[64,128]{1,0:T(8,128)S(1)}, f32[64,128]{1,0:T(8,128)S(1)}, u32[]{:S(2)}, u32[]{:S(2)}) %collective-permute-start.1) | collective-permute-done | bytes 32800 | tf_op jit(solution)/shard_map/ppermute | solution.py:342
  30.2 3.0 %collective-permute-start.2 = (f32[64,128]{1,0:T(8,128)S(1)}, f32[64,128]{1,0:T(8,128)S(1)}, u32[]{:S(2)}, u32[]{:S(2)}) collective-permute-start(f32[64,128]{1,0:T(8,128)S(1)} %add.3.refs_0_), channel_id=1, source_target_pairs={{0,16},{8,24},{16,0},{24,8},{1,17},{9,25},{17,1},{25,9},{2,18},{10... | collective-permute-start | bytes 98312 | tf_op jit(solution)/shard_map/ppermute | solution.py:264
  33.3 0.0 collective-permute-done.7.after_ref
  33.3 2.2 %input_grads.1 = (bf16[128,1024]{1,0:T(8,128)(2,1)}, bf16[128,1024]{1,0:T(8,128)(2,1)}, bf16[128,1024]{1,0:T(8,128)(2,1)}) custom-call(bf16[8192,256]{1,0:T(8,128)(2,1)S(1)} %get-tuple-element.41.band_ref, bf16[128,1024]{1,0:T(8,128)(2,1)S(1)} %get-tuple-element.32.grad_ref, bf16[128,1024]{1,0:T(8,128)(2,1)S(1)} %collective-permute-done.7.after_ref, ...), custom_call_target="tpu_custom_call" | custom-call | flops 2200000000 | bytes 7200000 | tf_op jit(solution)/shard_map/input_grads/pallas_call | solution.py:31
  35.5 0.6 %collective-permute-done.5.refs_4_ = bf16[128,1024]{1,0:T(8,128)(2,1)S(1)} collective-permute-done((bf16[128,1024]{1,0:T(8,128)(2,1)S(1)}, bf16[128,1024]{1,0:T(8,128)(2,1)S(1)}, u32[]{:S(2)}, u32[]{:S(2)}) %collective-permute-start.5) | collective-permute-done | bytes 262176 | tf_op jit(solution)/shard_map/ppermute | solution.py:259
  36.0 0.0 collective-permute-done.6.refs_5_
  36.0 0.9 %finish.1 = (bf16[128,1024]{1,0:T(8,128)(2,1)}, f32[64,128]{1,0:T(8,128)}) custom-call(f32[64,128]{1,0:T(8,128)S(1)} %add.3.refs_0_, f32[64,128]{1,0:T(8,128)S(1)} %collective-permute-done.2.refs_1_, bf16[128,1024]{1,0:T(8,128)(2,1)S(1)} %get-tuple-element.36.refs_2_, bf16[128,1024]{1,0:T(8,128)(2,1)S(1)} %collective-permute-done.4.refs_3_, ...), custom_call_target="tpu_custom_call" | custom-call | flops 990000000 | bytes 3240000 | tf_op jit(solution)/shard_map/finish/pallas_call | solution.py:31
  (9 shorter events, 0.0 us)
Async XLA Ops:
  0.6 13.5 %copy-start = (bf16[128,1024]{1,0:T(8,128)(2,1)S(1)}, bf16[128,1024]{1,0:T(8,128)(2,1)}, u32[]{:S(2)}) copy-start(bf16[128,1024]{1,0:T(8,128)(2,1)} %queries_ref.3) | copy-start | bytes 786436
  1.8 12.3 %collective-permute-start = (bf16[128,1024]{1,0:T(8,128)(2,1)S(1)}, bf16[128,1024]{1,0:T(8,128)(2,1)S(1)}, u32[]{:S(2)}, u32[]{:S(2)}) collective-permute-start(bf16[128,1024]{1,0:T(8,128)(2,1)S(1)} %multiply_convert_fusion.mixed_ref), channel_id=1, source_target_pairs={{0,8},{8,16},{16,24},{1,9},{9,17},{17,25},{2,10},{10,18},{18,26},{... | collective-permute-start | bytes 786440 | tf_op jit(solution)/shard_map/ppermute | solution.py:254
  14.1 2.5 %copy-start.3 = (s32[128]{0:T(128)S(1)}, s32[128]{0:T(128)}, u32[]{:S(2)}) copy-start(s32[128]{0:T(128)} %param.10) | copy-start | bytes 1540
  16.5 2.7 %collective-permute-start.3 = (bf16[512,1024]{1,0:T(8,128)(2,1)S(1)}, bf16[512,1024]{1,0:T(8,128)(2,1)S(1)}, u32[]{:S(2)}, u32[]{:S(2)}) collective-permute-start(bf16[512,1024]{1,0:T(8,128)(2,1)S(1)} %get-tuple-element.35), channel_id=1, source_target_pairs={{0,1},{1,0},{2,3},{3,2},{4,5},{5,4},{6,7},{7,6},{8,9},{9,8},{10,11... | collective-permute-start | bytes 3145736 | tf_op jit(solution)/shard_map/ppermute | solution.py:259
  17.4 15.8 %copy-start.1 = (bf16[128,1024]{1,0:T(8,128)(2,1)S(1)}, bf16[128,1024]{1,0:T(8,128)(2,1)}, u32[]{:S(2)}) copy-start(bf16[128,1024]{1,0:T(8,128)(2,1)} %values_ref.1) | copy-start | bytes 786436
  17.4 15.8 %copy-start.2 = (bf16[128,1024]{1,0:T(8,128)(2,1)S(1)}, bf16[128,1024]{1,0:T(8,128)(2,1)}, u32[]{:S(2)}) copy-start(bf16[128,1024]{1,0:T(8,128)(2,1)} %keys_ref.1) | copy-start | bytes 786436
  17.4 15.8 %collective-permute-start.7 = (bf16[128,1024]{1,0:T(8,128)(2,1)S(1)}, bf16[128,1024]{1,0:T(8,128)(2,1)S(1)}, u32[]{:S(2)}, u32[]{:S(2)}) collective-permute-start(bf16[128,1024]{1,0:T(8,128)(2,1)S(1)} %get-tuple-element.42), channel_id=1, source_target_pairs={{8,0},{16,8},{24,16},{9,1},{17,9},{25,17},{10,2},{18,10},{26,18},{... | collective-permute-start | bytes 786440 | tf_op jit(solution)/shard_map/ppermute | solution.py:254
  20.6 14.9 %collective-permute-start.4 = (bf16[128,1024]{1,0:T(8,128)(2,1)S(1)}, bf16[128,1024]{1,0:T(8,128)(2,1)S(1)}, u32[]{:S(2)}, u32[]{:S(2)}) collective-permute-start(bf16[128,1024]{1,0:T(8,128)(2,1)S(1)} %get-tuple-element.37), channel_id=1, source_target_pairs={{0,2},{1,3},{2,0},{3,1},{4,6},{5,7},{6,4},{7,5},{8,10},{9,11},{10,... | collective-permute-start | bytes 786440 | tf_op jit(solution)/shard_map/ppermute | solution.py:259
  22.2 13.9 %collective-permute-start.5 = (bf16[128,1024]{1,0:T(8,128)(2,1)S(1)}, bf16[128,1024]{1,0:T(8,128)(2,1)S(1)}, u32[]{:S(2)}, u32[]{:S(2)}) collective-permute-start(bf16[128,1024]{1,0:T(8,128)(2,1)S(1)} %get-tuple-element.38), channel_id=1, source_target_pairs={{0,4},{1,5},{2,6},{3,7},{4,0},{5,1},{6,2},{7,3},{8,12},{9,13},{10,... | collective-permute-start | bytes 786440 | tf_op jit(solution)/shard_map/ppermute | solution.py:259
  23.7 12.3 %collective-permute-start.6 = (bf16[128,1024]{1,0:T(8,128)(2,1)S(1)}, bf16[128,1024]{1,0:T(8,128)(2,1)S(1)}, u32[]{:S(2)}, u32[]{:S(2)}) collective-permute-start(bf16[128,1024]{1,0:T(8,128)(2,1)S(1)} %get-tuple-element.39), channel_id=1, source_target_pairs={{0,6},{1,7},{2,4},{3,5},{4,2},{5,3},{6,0},{7,1},{8,14},{9,15},{10,... | collective-permute-start | bytes 786440 | tf_op jit(solution)/shard_map/ppermute | solution.py:259
  25.8 4.4 %collective-permute-start.1 = (f32[64,128]{1,0:T(8,128)S(1)}, f32[64,128]{1,0:T(8,128)S(1)}, u32[]{:S(2)}, u32[]{:S(2)}) collective-permute-start(f32[64,128]{1,0:T(8,128)S(1)} %filter_grad.1), channel_id=1, source_target_pairs={{0,8},{8,0},{16,24},{24,16},{1,9},{9,1},{17,25},{25,17},{2,10},{10... | collective-permute-start | bytes 98312 | tf_op jit(solution)/shard_map/ppermute | solution.py:342
  30.2 5.2 %collective-permute-start.2 = (f32[64,128]{1,0:T(8,128)S(1)}, f32[64,128]{1,0:T(8,128)S(1)}, u32[]{:S(2)}, u32[]{:S(2)}) collective-permute-start(f32[64,128]{1,0:T(8,128)S(1)} %add.3.refs_0_), channel_id=1, source_target_pairs={{0,16},{8,24},{16,0},{24,8},{1,17},{9,25},{17,1},{25,9},{2,18},{10... | collective-permute-start | bytes 98312 | tf_op jit(solution)/shard_map/ppermute | solution.py:264

commit v5 on v4

--- a/solution.py
+++ b/solution.py
@@ -232,6 +232,14 @@
     )
 
 
+def own_and_filter_grad_body(body, offsets, weight_ref, gated_ref, came_ref, *refs):
+    *operand_refs, held_ref, own_ref, terms_ref, sums = refs
+    rows = own_ref.shape[0]
+    last = came_ref.at[pl.ds(came_ref.shape[0] - rows, rows)]
+    part_body(offsets, False, weight_ref, gated_ref, last, held_ref, own_ref)
+    body(*operand_refs, terms_ref, sums)
+
+
 def input_grads_body(member, band_ref, grad_ref, after_ref, keys_ref, values_ref, gated_ref, conv_ref, *refs):
     chan = grad_ref.shape[1]
     q_ref, k_ref, v_ref = refs
@@ -318,8 +326,8 @@
         weight, gated_grad, conv_grad, leading = call(
             finish_gated, (doc, weight, total, late_grad, queries), [tile32, tile, tile], "gated_grad", 1.5, held=1
         )
-        weight, far, near_x, near_y, own = call(
-            functools.partial(part_body, some + rest, False), (weight, gated, came), [block] * 4, "sums", 1.4, held=0
+        weight, far, near_x, near_y = call(
+            functools.partial(part_body, (some + rest)[:3], False), (weight, gated, came), [block] * 3, "sums", 1.1, held=0
         )
         far, near_x, near_y = swap(far, 6), swap(near_x, 2), swap(near_y, 4)
     else:
@@ -334,10 +342,15 @@
         output = lax.psum_scatter(partial_out, "tensor", scatter_dimension=1, tiled=True)
     after = shift(leading, "dp", -1)
     scale = (rows * lax.axis_size("dp") * member) ** (-0.5)
-    (terms,) = call(
-        functools.partial(filter_grad_body, member, scale), (doc, conv_grad, mixed, before),
-        [((groups, taps), F32)], "filter_grad", 1.7, scratch=[pltpu.VMEM((groups, SUBLANES, taps), F32)],
-    )
+    body, operands = functools.partial(filter_grad_body, member, scale), (doc, conv_grad, mixed, before)
+    scratch = [pltpu.VMEM((groups, SUBLANES, taps), F32)]
+    if staged:
+        weight, own, terms = call(
+            functools.partial(own_and_filter_grad_body, body, rest[1:]), (weight, gated, came, *operands),
+            [block, ((groups, taps), F32)], "filter_grad", 2.0, scratch=scratch, held=0,
+        )
+    else:
+        (terms,) = call(body, operands, [((groups, taps), F32)], "filter_grad", 1.7, scratch=scratch)
     if staged:
         terms = terms + lax.ppermute(terms, "dp", [(i, i ^ 1) for i in range(4)])
         terms = (terms, turn(terms, 2))

time: 37.1 us -> 36.7 us (0.989)
  transfers between devices with their start and end apart: 8 -> 8, of which waited for: 3 -> 3; matrix products, arithmetic and copies ran while one was open for 0% -> 0% of each run, Pallas kernels for 36% -> 37%
where the time goes in v5:
time: 36.7 us; the launch traced here: 36.5 us
  Pallas kernels  16.7 us (46%)
  starting transfers between devices  15.4 us (42%)
  waiting for transfers between devices  2.48 us (7%)
  other arithmetic  1.14 us (3%)
  between operations  0.74 us (2%)
    pallas_call x6, Pallas kernels, call(): pl.pallas_call(body, out_shape=shapes, in_specs=[pl.BlockSpec(memory_spac...  9.29 us
    pallas_call x1, Pallas kernels, on_device(): pl.pallas_call(functools.partial(front_body, blocks, late, 7), out_shape=...  7.37 us
    ppermute x2, starting transfers between devices, shift(): lax.ppermute(value, axis, [(i, i + by) for i in range(devices) if 0 <= i...  6.41 us
    ppermute x4, starting transfers between devices, swap(): lax.ppermute(value, 'tensor', [(i, i ^ mask) for i in range(devices)])  3.62 us
    ppermute x1, starting transfers between devices, turn(): lax.ppermute(value, 'dp', [(i, (i + by) % devices) for i in range(devices)])  3.03 us
    ppermute x1, starting transfers between devices, on_device(): terms = terms + lax.ppermute(terms, 'dp', [(i, i ^ 1) for i in range(4)])  2.38 us
    ppermute x1, waiting for transfers between devices, on_device(): terms = terms + lax.ppermute(terms, 'dp', [(i, i ^ 1) for i in range(4)])  1.89 us
    convert_element_type x1, other arithmetic, on_device(): mixed = (keys.astype(F32) * values.astype(F32)).astype(BF16)  1.14 us
  transfers between devices with their start and end apart: 8, of which 3 were waited for; matrix products, arithmetic and copies ran while one was open for 0% of the time, Pallas kernels for 37%

profile of v5, /device:TPU:0, one launch (start us, length us, event | category | flops | bytes accessed | tf_op | source)
XLA Modules:
  0.0 36.5 jit_solution(16027682150955106427)
XLA Ops:
  0.6 1.1 %multiply_convert_fusion.mixed_ref.refs_2_ = bf16[128,1024]{1,0:T(8,128)(2,1)S(1)} fusion(bf16[128,1024]{1,0:T(8,128)(2,1)} %values_ref.1, bf16[128,1024]{1,0:T(8,128)(2,1)} %keys_ref.1), kind=kLoop, calls=%fused_computation | loop fusion | flops 524288 | bytes 786432 | tf_op jit(solution)/shard_map/convert_element_type | solution.py:286
  1.8 4.9 %collective-permute-start = (bf16[128,1024]{1,0:T(8,128)(2,1)S(1)}, bf16[128,1024]{1,0:T(8,128)(2,1)S(1)}, u32[]{:S(2)}, u32[]{:S(2)}) collective-permute-start(bf16[128,1024]{1,0:T(8,128)(2,1)S(1)} %multiply_convert_fusion.mixed_ref.refs_2_), channel_id=1, source_target_pairs={{0,8},{8,16},{16,24},{1,9},{9,17},{17,25},{2,10},{10,18},{18,26},{... | collective-permute-start | bytes 786440 | tf_op jit(solution)/shard_map/ppermute | solution.py:262
  6.7 7.4 %front.1 = (bf16[8192,256]{1,0:T(8,128)(2,1)S(1)}, bf16[8192,256]{1,0:T(8,128)(2,1)S(1)}, f32[1024,128]{1,0:T(8,128)S(1)}, bf16[1024,128]{1,0:T(8,128)(2,1)S(1)}, bf16[1024,8192]{1,0:T(8,128)(2,1)S(1)}) custom-call(s32[1,128]{1,0:T(1,128)} %bitcast.1, f32[64,128]{1,0:T(8,128)} %filt_hbm.1, bf16[128,8192]{1,0:T(8,128)(2,1)} %grad_hbm.1, ...), custom_call_target="tpu_custom_call" | custom-call | flops 6600000000 | bytes 21600000 | tf_op jit(solution)/shard_map/front/pallas_call | solution.py:300
  14.1 0.0 collective-permute-done.before_ref.refs_3_
  14.1 0.0 copy-start.3
  14.1 2.4 %conv.1 = (bf16[1024,8192]{1,0:T(8,128)(2,1)S(1)}, f32[128,1024]{1,0:T(8,128)S(1)}, bf16[128,1024]{1,0:T(8,128)(2,1)S(1)}, bf16[512,1024]{1,0:T(8,128)(2,1)S(1)}) custom-call(bf16[1024,8192]{1,0:T(8,128)(2,1)} %weight_hbm.3, bf16[8192,256]{1,0:T(8,128)(2,1)S(1)} %get-tuple-element.29.band_ref, ...), custom_call_target="tpu_custom_call", output_to_operand_aliasing={{0}: (5, {})} | custom-call | flops 2860000000 | bytes 9360000 | tf_op jit(solution)/shard_map/conv/pallas_call | solution.py:31
  16.5 0.1 collective-permute-start.1
  16.6 0.8 %gated_grad.1 = (bf16[1024,8192]{1,0:T(8,128)(2,1)S(1)}, f32[128,1024]{1,0:T(8,128)S(1)}, bf16[128,1024]{1,0:T(8,128)(2,1)S(1)}, bf16[128,1024]{1,0:T(8,128)(2,1)S(1)}) custom-call(s32[1,128]{1,0:T(1,128)S(1)} %bitcast.2, bf16[1024,8192]{1,0:T(8,128)(2,1)S(1)} %get-tuple-element.31.weight_ref, ...), custom_call_target="tpu_custom_call", output_to_operand_aliasing={{0}: (1, {})} | custom-call | flops 1650000000 | bytes 5400000 | tf_op jit(solution)/shard_map/gated_grad/pallas_call | solution.py:31
  17.4 1.5 %collective-permute-start.7 = (bf16[128,1024]{1,0:T(8,128)(2,1)S(1)}, bf16[128,1024]{1,0:T(8,128)(2,1)S(1)}, u32[]{:S(2)}, u32[]{:S(2)}) collective-permute-start(bf16[128,1024]{1,0:T(8,128)(2,1)S(1)} %get-tuple-element.46), channel_id=1, source_target_pairs={{8,0},{16,8},{24,16},{9,1},{17,9},{25,17},{10,2},{18,10},{26,18},{... | collective-permute-start | bytes 786440 | tf_op jit(solution)/shard_map/ppermute | solution.py:262
  18.9 0.4 collective-permute-done.1.refs_0_.came_ref
  19.3 1.1 %sums.1 = (bf16[1024,8192]{1,0:T(8,128)(2,1)S(1)}, bf16[128,1024]{1,0:T(8,128)(2,1)S(1)}, bf16[128,1024]{1,0:T(8,128)(2,1)S(1)}, bf16[128,1024]{1,0:T(8,128)(2,1)S(1)}) custom-call(bf16[1024,8192]{1,0:T(8,128)(2,1)S(1)} %get-tuple-element.34.weight_ref, bf16[128,1024]{1,0:T(8,128)(2,1)S(1)} %get-tuple-element.35.gated_ref, ...), custom_call_target="tpu_custom_call", output_to_operand_aliasing={{0}: (0, {})} | custom-call | flops 1210000000 | bytes 3960000 | tf_op jit(solution)/shard_map/sums/pallas_call | solution.py:31
  20.4 1.6 %collective-permute-start.4 = (bf16[128,1024]{1,0:T(8,128)(2,1)S(1)}, bf16[128,1024]{1,0:T(8,128)(2,1)S(1)}, u32[]{:S(2)}, u32[]{:S(2)}) collective-permute-start(bf16[128,1024]{1,0:T(8,128)(2,1)S(1)} %get-tuple-element.41), channel_id=1, source_target_pairs={{0,2},{1,3},{2,0},{3,1},{4,6},{5,7},{6,4},{7,5},{8,10},{9,11},{10,... | collective-permute-start | bytes 786440 | tf_op jit(solution)/shard_map/ppermute | solution.py:267
  21.9 1.5 %collective-permute-start.5 = (bf16[128,1024]{1,0:T(8,128)(2,1)S(1)}, bf16[128,1024]{1,0:T(8,128)(2,1)S(1)}, u32[]{:S(2)}, u32[]{:S(2)}) collective-permute-start(bf16[128,1024]{1,0:T(8,128)(2,1)S(1)} %get-tuple-element.42), channel_id=1, source_target_pairs={{0,4},{1,5},{2,6},{3,7},{4,0},{5,1},{6,2},{7,3},{8,12},{9,13},{10,... | collective-permute-start | bytes 786440 | tf_op jit(solution)/shard_map/ppermute | solution.py:267
  23.4 0.5 %collective-permute-start.6 = (bf16[128,1024]{1,0:T(8,128)(2,1)S(1)}, bf16[128,1024]{1,0:T(8,128)(2,1)S(1)}, u32[]{:S(2)}, u32[]{:S(2)}) collective-permute-start(bf16[128,1024]{1,0:T(8,128)(2,1)S(1)} %get-tuple-element.43), channel_id=1, source_target_pairs={{0,6},{1,7},{2,4},{3,5},{4,2},{5,3},{6,0},{7,1},{8,14},{9,15},{10,... | collective-permute-start | bytes 786440 | tf_op jit(solution)/shard_map/ppermute | solution.py:267
  23.9 2.0 %filter_grad.1 = (bf16[1024,8192]{1,0:T(8,128)(2,1)S(1)}, bf16[128,1024]{1,0:T(8,128)(2,1)S(1)}, f32[64,128]{1,0:T(8,128)S(1)}) custom-call(bf16[1024,8192]{1,0:T(8,128)(2,1)S(1)} %get-tuple-element.37.weight_ref, bf16[128,1024]{1,0:T(8,128)(2,1)S(1)} %get-tuple-element.35.gated_ref, ...), custom_call_target="tpu_custom_call", output_to_operand_aliasing={{0}: (0, {})} | custom-call | flops 2200000000 | bytes 7200000 | tf_op jit(solution)/shard_map/filter_grad/pallas_call | solution.py:31
  25.9 2.4 %collective-permute-start.2 = (f32[64,128]{1,0:T(8,128)S(1)}, f32[64,128]{1,0:T(8,128)S(1)}, u32[]{:S(2)}, u32[]{:S(2)}) collective-permute-start(f32[64,128]{1,0:T(8,128)S(1)} %get-tuple-element.39), channel_id=1, source_target_pairs={{0,8},{8,0},{16,24},{24,16},{1,9},{9,1},{17,25},{25,17},{2,10},{10... | collective-permute-start | bytes 98312 | tf_op jit(solution)/shard_map/ppermute | solution.py:355
  28.3 1.9 %collective-permute-done.2 = f32[64,128]{1,0:T(8,128)S(1)} collective-permute-done((f32[64,128]{1,0:T(8,128)S(1)}, f32[64,128]{1,0:T(8,128)S(1)}, u32[]{:S(2)}, u32[]{:S(2)}) %collective-permute-start.2) | collective-permute-done | bytes 32800 | tf_op jit(solution)/shard_map/ppermute | solution.py:355
  30.2 3.0 %collective-permute-start.3 = (f32[64,128]{1,0:T(8,128)S(1)}, f32[64,128]{1,0:T(8,128)S(1)}, u32[]{:S(2)}, u32[]{:S(2)}) collective-permute-start(f32[64,128]{1,0:T(8,128)S(1)} %add.3.refs_0_), channel_id=1, source_target_pairs={{0,16},{8,24},{16,0},{24,8},{1,17},{9,25},{17,1},{25,9},{2,18},{10... | collective-permute-start | bytes 98312 | tf_op jit(solution)/shard_map/ppermute | solution.py:272
  33.2 0.0 collective-permute-done.7.after_ref
  33.2 2.2 %input_grads.1 = (bf16[128,1024]{1,0:T(8,128)(2,1)}, bf16[128,1024]{1,0:T(8,128)(2,1)}, bf16[128,1024]{1,0:T(8,128)(2,1)}) custom-call(bf16[8192,256]{1,0:T(8,128)(2,1)S(1)} %get-tuple-element.45.band_ref, bf16[128,1024]{1,0:T(8,128)(2,1)S(1)} %get-tuple-element.38.refs_1_.grad_ref, bf16[128,1024]{1,0:T(8,128)(2,1)S(1)} %collective-permute-done.7.after_ref, ...), custom_call_target="tpu_custom_call" | custom-call | flops 2200000000 | bytes 7200000 | tf_op jit(solution)/shard_map/input_grads/pallas_call | solution.py:31
  35.4 0.0 collective-permute-done.3.refs_1_
  35.4 0.0 collective-permute-done.4.refs_3_
  35.4 0.2 collective-permute-done.5.refs_4_
  35.6 0.8 %finish.1 = (bf16[128,1024]{1,0:T(8,128)(2,1)}, f32[64,128]{1,0:T(8,128)}) custom-call(f32[64,128]{1,0:T(8,128)S(1)} %add.3.refs_0_, f32[64,128]{1,0:T(8,128)S(1)} %collective-permute-done.3.refs_1_, bf16[128,1024]{1,0:T(8,128)(2,1)S(1)} %get-tuple-element.40.refs_2_, bf16[128,1024]{1,0:T(8,128)(2,1)S(1)} %collective-permute-done.4.refs_3_, ...), custom_call_target="tpu_custom_call" | custom-call | flops 990000000 | bytes 3240000 | tf_op jit(solution)/shard_map/finish/pallas_call | solution.py:31
  (9 shorter events, 0.0 us)
Async XLA Ops:
  0.6 13.5 %copy-start = (bf16[128,1024]{1,0:T(8,128)(2,1)S(1)}, bf16[128,1024]{1,0:T(8,128)(2,1)}, u32[]{:S(2)}) copy-start(bf16[128,1024]{1,0:T(8,128)(2,1)} %queries_ref.3) | copy-start | bytes 786436
  1.8 12.3 %collective-permute-start = (bf16[128,1024]{1,0:T(8,128)(2,1)S(1)}, bf16[128,1024]{1,0:T(8,128)(2,1)S(1)}, u32[]{:S(2)}, u32[]{:S(2)}) collective-permute-start(bf16[128,1024]{1,0:T(8,128)(2,1)S(1)} %multiply_convert_fusion.mixed_ref.refs_2_), channel_id=1, source_target_pairs={{0,8},{8,16},{16,24},{1,9},{9,17},{17,25},{2,10},{10,18},{18,26},{... | collective-permute-start | bytes 786440 | tf_op jit(solution)/shard_map/ppermute | solution.py:262
  14.1 2.5 %copy-start.3 = (s32[128]{0:T(128)S(1)}, s32[128]{0:T(128)}, u32[]{:S(2)}) copy-start(s32[128]{0:T(128)} %param.10) | copy-start | bytes 1540
  16.5 2.7 %collective-permute-start.1 = (bf16[512,1024]{1,0:T(8,128)(2,1)S(1)}, bf16[512,1024]{1,0:T(8,128)(2,1)S(1)}, u32[]{:S(2)}, u32[]{:S(2)}) collective-permute-start(bf16[512,1024]{1,0:T(8,128)(2,1)S(1)} %get-tuple-element.36), channel_id=1, source_target_pairs={{0,1},{1,0},{2,3},{3,2},{4,5},{5,4},{6,7},{7,6},{8,9},{9,8},{10,11... | collective-permute-start | bytes 3145736 | tf_op jit(solution)/shard_map/ppermute | solution.py:267
  17.4 15.7 %collective-permute-start.7 = (bf16[128,1024]{1,0:T(8,128)(2,1)S(1)}, bf16[128,1024]{1,0:T(8,128)(2,1)S(1)}, u32[]{:S(2)}, u32[]{:S(2)}) collective-permute-start(bf16[128,1024]{1,0:T(8,128)(2,1)S(1)} %get-tuple-element.46), channel_id=1, source_target_pairs={{8,0},{16,8},{24,16},{9,1},{17,9},{25,17},{10,2},{18,10},{26,18},{... | collective-permute-start | bytes 786440 | tf_op jit(solution)/shard_map/ppermute | solution.py:262
  19.3 13.9 %copy-start.1 = (bf16[128,1024]{1,0:T(8,128)(2,1)S(1)}, bf16[128,1024]{1,0:T(8,128)(2,1)}, u32[]{:S(2)}) copy-start(bf16[128,1024]{1,0:T(8,128)(2,1)} %values_ref.1) | copy-start | bytes 786436
  19.3 13.9 %copy-start.2 = (bf16[128,1024]{1,0:T(8,128)(2,1)S(1)}, bf16[128,1024]{1,0:T(8,128)(2,1)}, u32[]{:S(2)}) copy-start(bf16[128,1024]{1,0:T(8,128)(2,1)} %keys_ref.1) | copy-start | bytes 786436
  20.4 15.1 %collective-permute-start.4 = (bf16[128,1024]{1,0:T(8,128)(2,1)S(1)}, bf16[128,1024]{1,0:T(8,128)(2,1)S(1)}, u32[]{:S(2)}, u32[]{:S(2)}) collective-permute-start(bf16[128,1024]{1,0:T(8,128)(2,1)S(1)} %get-tuple-element.41), channel_id=1, source_target_pairs={{0,2},{1,3},{2,0},{3,1},{4,6},{5,7},{6,4},{7,5},{8,10},{9,11},{10,... | collective-permute-start | bytes 786440 | tf_op jit(solution)/shard_map/ppermute | solution.py:267
  21.9 13.7 %collective-permute-start.5 = (bf16[128,1024]{1,0:T(8,128)(2,1)S(1)}, bf16[128,1024]{1,0:T(8,128)(2,1)S(1)}, u32[]{:S(2)}, u32[]{:S(2)}) collective-permute-start(bf16[128,1024]{1,0:T(8,128)(2,1)S(1)} %get-tuple-element.42), channel_id=1, source_target_pairs={{0,4},{1,5},{2,6},{3,7},{4,0},{5,1},{6,2},{7,3},{8,12},{9,13},{10,... | collective-permute-start | bytes 786440 | tf_op jit(solution)/shard_map/ppermute | solution.py:267
  23.4 12.2 %collective-permute-start.6 = (bf16[128,1024]{1,0:T(8,128)(2,1)S(1)}, bf16[128,1024]{1,0:T(8,128)(2,1)S(1)}, u32[]{:S(2)}, u32[]{:S(2)}) collective-permute-start(bf16[128,1024]{1,0:T(8,128)(2,1)S(1)} %get-tuple-element.43), channel_id=1, source_target_pairs={{0,6},{1,7},{2,4},{3,5},{4,2},{5,3},{6,0},{7,1},{8,14},{9,15},{10,... | collective-permute-start | bytes 786440 | tf_op jit(solution)/shard_map/ppermute | solution.py:267
  25.9 4.3 %collective-permute-start.2 = (f32[64,128]{1,0:T(8,128)S(1)}, f32[64,128]{1,0:T(8,128)S(1)}, u32[]{:S(2)}, u32[]{:S(2)}) collective-permute-start(f32[64,128]{1,0:T(8,128)S(1)} %get-tuple-element.39), channel_id=1, source_target_pairs={{0,8},{8,0},{16,24},{24,16},{1,9},{9,1},{17,25},{25,17},{2,10},{10... | collective-permute-start | bytes 98312 | tf_op jit(solution)/shard_map/ppermute | solution.py:355
  30.2 5.2 %collective-permute-start.3 = (f32[64,128]{1,0:T(8,128)S(1)}, f32[64,128]{1,0:T(8,128)S(1)}, u32[]{:S(2)}, u32[]{:S(2)}) collective-permute-start(f32[64,128]{1,0:T(8,128)S(1)} %add.3.refs_0_), channel_id=1, source_target_pairs={{0,16},{8,24},{16,0},{24,8},{1,17},{9,25},{17,1},{25,9},{2,18},{10... | collective-permute-start | bytes 98312 | tf_op jit(solution)/shard_map/ppermute | solution.py:272

commit v6 on v5

--- a/solution.py
+++ b/solution.py
@@ -200,7 +200,7 @@
         if sibling:
             refs[-1][stacked, :] = part.astype(BF16)
         else:
-            summed = part.astype(BF16).astype(F32) + refs[0][stacked, :].astype(F32)
+            summed = part + refs[0][stacked, :].astype(F32)
             refs[k - len(offsets)][...] = summed.astype(BF16)
 
 

time: 36.7 us -> 36.6 us (level)
  no operation moved by 1% of the time
where the time goes in v6:
time: 36.6 us; the launch traced here: 36.4 us
  Pallas kernels  16.6 us (45%)
  starting transfers between devices  15.4 us (42%)
  waiting for transfers between devices  2.49 us (7%)
  other arithmetic  1.14 us (3%)
  between operations  0.74 us (2%)
    pallas_call x6, Pallas kernels, call(): pl.pallas_call(body, out_shape=shapes, in_specs=[pl.BlockSpec(memory_spac...  9.23 us
    pallas_call x1, Pallas kernels, on_device(): pl.pallas_call(functools.partial(front_body, blocks, late, 7), out_shape=...  7.37 us
    ppermute x2, starting transfers between devices, shift(): lax.ppermute(value, axis, [(i, i + by) for i in range(devices) if 0 <= i...  6.41 us
    ppermute x4, starting transfers between devices, swap(): lax.ppermute(value, 'tensor', [(i, i ^ mask) for i in range(devices)])  3.62 us
    ppermute x1, starting transfers between devices, turn(): lax.ppermute(value, 'dp', [(i, (i + by) % devices) for i in range(devices)])  3.02 us
    ppermute x1, starting transfers between devices, on_device(): terms = terms + lax.ppermute(terms, 'dp', [(i, i ^ 1) for i in range(4)])  2.37 us
    ppermute x1, waiting for transfers between devices, on_device(): terms = terms + lax.ppermute(terms, 'dp', [(i, i ^ 1) for i in range(4)])  1.89 us
    convert_element_type x1, other arithmetic, on_device(): mixed = (keys.astype(F32) * values.astype(F32)).astype(BF16)  1.14 us
  transfers between devices with their start and end apart: 8, of which 3 were waited for; matrix products, arithmetic and copies ran while one was open for 0% of the time, Pallas kernels for 37%

profile of v6, /device:TPU:0, one launch (start us, length us, event | category | flops | bytes accessed | tf_op | source)
XLA Modules:
  0.0 36.4 jit_solution(17483927730746600192)
XLA Ops:
  0.6 1.1 %multiply_convert_fusion.mixed_ref.refs_2_ = bf16[128,1024]{1,0:T(8,128)(2,1)S(1)} fusion(bf16[128,1024]{1,0:T(8,128)(2,1)} %values_ref.1, bf16[128,1024]{1,0:T(8,128)(2,1)} %keys_ref.1), kind=kLoop, calls=%fused_computation | loop fusion | flops 524288 | bytes 786432 | tf_op jit(solution)/shard_map/convert_element_type | solution.py:286
  1.8 4.9 %collective-permute-start = (bf16[128,1024]{1,0:T(8,128)(2,1)S(1)}, bf16[128,1024]{1,0:T(8,128)(2,1)S(1)}, u32[]{:S(2)}, u32[]{:S(2)}) collective-permute-start(bf16[128,1024]{1,0:T(8,128)(2,1)S(1)} %multiply_convert_fusion.mixed_ref.refs_2_), channel_id=1, source_target_pairs={{0,8},{8,16},{16,24},{1,9},{9,17},{17,25},{2,10},{10,18},{18,26},{... | collective-permute-start | bytes 786440 | tf_op jit(solution)/shard_map/ppermute | solution.py:262
  6.7 7.4 %front.1 = (bf16[8192,256]{1,0:T(8,128)(2,1)S(1)}, bf16[8192,256]{1,0:T(8,128)(2,1)S(1)}, f32[1024,128]{1,0:T(8,128)S(1)}, bf16[1024,128]{1,0:T(8,128)(2,1)S(1)}, bf16[1024,8192]{1,0:T(8,128)(2,1)S(1)}) custom-call(s32[1,128]{1,0:T(1,128)} %bitcast.1, f32[64,128]{1,0:T(8,128)} %filt_hbm.1, bf16[128,8192]{1,0:T(8,128)(2,1)} %grad_hbm.1, ...), custom_call_target="tpu_custom_call" | custom-call | flops 6600000000 | bytes 21600000 | tf_op jit(solution)/shard_map/front/pallas_call | solution.py:300
  14.1 0.0 collective-permute-done.before_ref.refs_3_
  14.1 0.0 copy-start.3
  14.1 2.4 %conv.1 = (bf16[1024,8192]{1,0:T(8,128)(2,1)S(1)}, f32[128,1024]{1,0:T(8,128)S(1)}, bf16[128,1024]{1,0:T(8,128)(2,1)S(1)}, bf16[512,1024]{1,0:T(8,128)(2,1)S(1)}) custom-call(bf16[1024,8192]{1,0:T(8,128)(2,1)} %weight_hbm.3, bf16[8192,256]{1,0:T(8,128)(2,1)S(1)} %get-tuple-element.29.band_ref, ...), custom_call_target="tpu_custom_call", output_to_operand_aliasing={{0}: (5, {})} | custom-call | flops 2860000000 | bytes 9360000 | tf_op jit(solution)/shard_map/conv/pallas_call | solution.py:31
  16.5 0.1 collective-permute-start.1
  16.6 0.8 %gated_grad.1 = (bf16[1024,8192]{1,0:T(8,128)(2,1)S(1)}, f32[128,1024]{1,0:T(8,128)S(1)}, bf16[128,1024]{1,0:T(8,128)(2,1)S(1)}, bf16[128,1024]{1,0:T(8,128)(2,1)S(1)}) custom-call(s32[1,128]{1,0:T(1,128)S(1)} %bitcast.2, bf16[1024,8192]{1,0:T(8,128)(2,1)S(1)} %get-tuple-element.31.weight_ref, ...), custom_call_target="tpu_custom_call", output_to_operand_aliasing={{0}: (1, {})} | custom-call | flops 1650000000 | bytes 5400000 | tf_op jit(solution)/shard_map/gated_grad/pallas_call | solution.py:31
  17.4 1.5 %collective-permute-start.7 = (bf16[128,1024]{1,0:T(8,128)(2,1)S(1)}, bf16[128,1024]{1,0:T(8,128)(2,1)S(1)}, u32[]{:S(2)}, u32[]{:S(2)}) collective-permute-start(bf16[128,1024]{1,0:T(8,128)(2,1)S(1)} %get-tuple-element.46), channel_id=1, source_target_pairs={{8,0},{16,8},{24,16},{9,1},{17,9},{25,17},{10,2},{18,10},{26,18},{... | collective-permute-start | bytes 786440 | tf_op jit(solution)/shard_map/ppermute | solution.py:262
  18.9 0.4 collective-permute-done.1.refs_0_.came_ref
  19.3 1.0 %sums.1 = (bf16[1024,8192]{1,0:T(8,128)(2,1)S(1)}, bf16[128,1024]{1,0:T(8,128)(2,1)S(1)}, bf16[128,1024]{1,0:T(8,128)(2,1)S(1)}, bf16[128,1024]{1,0:T(8,128)(2,1)S(1)}) custom-call(bf16[1024,8192]{1,0:T(8,128)(2,1)S(1)} %get-tuple-element.34.weight_ref, bf16[128,1024]{1,0:T(8,128)(2,1)S(1)} %get-tuple-element.35.gated_ref, ...), custom_call_target="tpu_custom_call", output_to_operand_aliasing={{0}: (0, {})} | custom-call | flops 1210000000 | bytes 3960000 | tf_op jit(solution)/shard_map/sums/pallas_call | solution.py:31
  20.3 1.5 %collective-permute-start.4 = (bf16[128,1024]{1,0:T(8,128)(2,1)S(1)}, bf16[128,1024]{1,0:T(8,128)(2,1)S(1)}, u32[]{:S(2)}, u32[]{:S(2)}) collective-permute-start(bf16[128,1024]{1,0:T(8,128)(2,1)S(1)} %get-tuple-element.41), channel_id=1, source_target_pairs={{0,2},{1,3},{2,0},{3,1},{4,6},{5,7},{6,4},{7,5},{8,10},{9,11},{10,... | collective-permute-start | bytes 786440 | tf_op jit(solution)/shard_map/ppermute | solution.py:267
  21.9 1.5 %collective-permute-start.5 = (bf16[128,1024]{1,0:T(8,128)(2,1)S(1)}, bf16[128,1024]{1,0:T(8,128)(2,1)S(1)}, u32[]{:S(2)}, u32[]{:S(2)}) collective-permute-start(bf16[128,1024]{1,0:T(8,128)(2,1)S(1)} %get-tuple-element.42), channel_id=1, source_target_pairs={{0,4},{1,5},{2,6},{3,7},{4,0},{5,1},{6,2},{7,3},{8,12},{9,13},{10,... | collective-permute-start | bytes 786440 | tf_op jit(solution)/shard_map/ppermute | solution.py:267
  23.4 0.5 %collective-permute-start.6 = (bf16[128,1024]{1,0:T(8,128)(2,1)S(1)}, bf16[128,1024]{1,0:T(8,128)(2,1)S(1)}, u32[]{:S(2)}, u32[]{:S(2)}) collective-permute-start(bf16[128,1024]{1,0:T(8,128)(2,1)S(1)} %get-tuple-element.43), channel_id=1, source_target_pairs={{0,6},{1,7},{2,4},{3,5},{4,2},{5,3},{6,0},{7,1},{8,14},{9,15},{10,... | collective-permute-start | bytes 786440 | tf_op jit(solution)/shard_map/ppermute | solution.py:267
  23.9 2.0 %filter_grad.1 = (bf16[1024,8192]{1,0:T(8,128)(2,1)S(1)}, bf16[128,1024]{1,0:T(8,128)(2,1)S(1)}, f32[64,128]{1,0:T(8,128)S(1)}) custom-call(bf16[1024,8192]{1,0:T(8,128)(2,1)S(1)} %get-tuple-element.37.weight_ref, bf16[128,1024]{1,0:T(8,128)(2,1)S(1)} %get-tuple-element.35.gated_ref, ...), custom_call_target="tpu_custom_call", output_to_operand_aliasing={{0}: (0, {})} | custom-call | flops 2200000000 | bytes 7200000 | tf_op jit(solution)/shard_map/filter_grad/pallas_call | solution.py:31
  25.8 2.4 %collective-permute-start.2 = (f32[64,128]{1,0:T(8,128)S(1)}, f32[64,128]{1,0:T(8,128)S(1)}, u32[]{:S(2)}, u32[]{:S(2)}) collective-permute-start(f32[64,128]{1,0:T(8,128)S(1)} %get-tuple-element.39), channel_id=1, source_target_pairs={{0,8},{8,0},{16,24},{24,16},{1,9},{9,1},{17,25},{25,17},{2,10},{10... | collective-permute-start | bytes 98312 | tf_op jit(solution)/shard_map/ppermute | solution.py:355
  28.2 1.9 %collective-permute-done.2 = f32[64,128]{1,0:T(8,128)S(1)} collective-permute-done((f32[64,128]{1,0:T(8,128)S(1)}, f32[64,128]{1,0:T(8,128)S(1)}, u32[]{:S(2)}, u32[]{:S(2)}) %collective-permute-start.2) | collective-permute-done | bytes 32800 | tf_op jit(solution)/shard_map/ppermute | solution.py:355
  30.1 3.0 %collective-permute-start.3 = (f32[64,128]{1,0:T(8,128)S(1)}, f32[64,128]{1,0:T(8,128)S(1)}, u32[]{:S(2)}, u32[]{:S(2)}) collective-permute-start(f32[64,128]{1,0:T(8,128)S(1)} %add.3.refs_0_), channel_id=1, source_target_pairs={{0,16},{8,24},{16,0},{24,8},{1,17},{9,25},{17,1},{25,9},{2,18},{10... | collective-permute-start | bytes 98312 | tf_op jit(solution)/shard_map/ppermute | solution.py:272
  33.1 0.0 collective-permute-done.7.after_ref
  33.1 2.2 %input_grads.1 = (bf16[128,1024]{1,0:T(8,128)(2,1)}, bf16[128,1024]{1,0:T(8,128)(2,1)}, bf16[128,1024]{1,0:T(8,128)(2,1)}) custom-call(bf16[8192,256]{1,0:T(8,128)(2,1)S(1)} %get-tuple-element.45.band_ref, bf16[128,1024]{1,0:T(8,128)(2,1)S(1)} %get-tuple-element.38.refs_1_.grad_ref, bf16[128,1024]{1,0:T(8,128)(2,1)S(1)} %collective-permute-done.7.after_ref, ...), custom_call_target="tpu_custom_call" | custom-call | flops 2200000000 | bytes 7200000 | tf_op jit(solution)/shard_map/input_grads/pallas_call | solution.py:31
  35.3 0.0 collective-permute-done.3.refs_1_
  35.3 0.0 collective-permute-done.4.refs_3_
  35.3 0.2 collective-permute-done.5.refs_4_
  35.6 0.8 %finish.1 = (bf16[128,1024]{1,0:T(8,128)(2,1)}, f32[64,128]{1,0:T(8,128)}) custom-call(f32[64,128]{1,0:T(8,128)S(1)} %add.3.refs_0_, f32[64,128]{1,0:T(8,128)S(1)} %collective-permute-done.3.refs_1_, bf16[128,1024]{1,0:T(8,128)(2,1)S(1)} %get-tuple-element.40.refs_2_, bf16[128,1024]{1,0:T(8,128)(2,1)S(1)} %collective-permute-done.4.refs_3_, ...), custom_call_target="tpu_custom_call" | custom-call | flops 990000000 | bytes 3240000 | tf_op jit(solution)/shard_map/finish/pallas_call | solution.py:31
  (9 shorter events, 0.0 us)
Async XLA Ops:
  0.6 13.5 %copy-start = (bf16[128,1024]{1,0:T(8,128)(2,1)S(1)}, bf16[128,1024]{1,0:T(8,128)(2,1)}, u32[]{:S(2)}) copy-start(bf16[128,1024]{1,0:T(8,128)(2,1)} %queries_ref.3) | copy-start | bytes 786436
  1.8 12.3 %collective-permute-start = (bf16[128,1024]{1,0:T(8,128)(2,1)S(1)}, bf16[128,1024]{1,0:T(8,128)(2,1)S(1)}, u32[]{:S(2)}, u32[]{:S(2)}) collective-permute-start(bf16[128,1024]{1,0:T(8,128)(2,1)S(1)} %multiply_convert_fusion.mixed_ref.refs_2_), channel_id=1, source_target_pairs={{0,8},{8,16},{16,24},{1,9},{9,17},{17,25},{2,10},{10,18},{18,26},{... | collective-permute-start | bytes 786440 | tf_op jit(solution)/shard_map/ppermute | solution.py:262
  14.1 2.5 %copy-start.3 = (s32[128]{0:T(128)S(1)}, s32[128]{0:T(128)}, u32[]{:S(2)}) copy-start(s32[128]{0:T(128)} %param.10) | copy-start | bytes 1540
  16.5 2.7 %collective-permute-start.1 = (bf16[512,1024]{1,0:T(8,128)(2,1)S(1)}, bf16[512,1024]{1,0:T(8,128)(2,1)S(1)}, u32[]{:S(2)}, u32[]{:S(2)}) collective-permute-start(bf16[512,1024]{1,0:T(8,128)(2,1)S(1)} %get-tuple-element.36), channel_id=1, source_target_pairs={{0,1},{1,0},{2,3},{3,2},{4,5},{5,4},{6,7},{7,6},{8,9},{9,8},{10,11... | collective-permute-start | bytes 3145736 | tf_op jit(solution)/shard_map/ppermute | solution.py:267
  17.4 15.7 %collective-permute-start.7 = (bf16[128,1024]{1,0:T(8,128)(2,1)S(1)}, bf16[128,1024]{1,0:T(8,128)(2,1)S(1)}, u32[]{:S(2)}, u32[]{:S(2)}) collective-permute-start(bf16[128,1024]{1,0:T(8,128)(2,1)S(1)} %get-tuple-element.46), channel_id=1, source_target_pairs={{8,0},{16,8},{24,16},{9,1},{17,9},{25,17},{10,2},{18,10},{26,18},{... | collective-permute-start | bytes 786440 | tf_op jit(solution)/shard_map/ppermute | solution.py:262
  19.3 13.8 %copy-start.1 = (bf16[128,1024]{1,0:T(8,128)(2,1)S(1)}, bf16[128,1024]{1,0:T(8,128)(2,1)}, u32[]{:S(2)}) copy-start(bf16[128,1024]{1,0:T(8,128)(2,1)} %values_ref.1) | copy-start | bytes 786436
  19.3 13.8 %copy-start.2 = (bf16[128,1024]{1,0:T(8,128)(2,1)S(1)}, bf16[128,1024]{1,0:T(8,128)(2,1)}, u32[]{:S(2)}) copy-start(bf16[128,1024]{1,0:T(8,128)(2,1)} %keys_ref.1) | copy-start | bytes 786436
  20.3 15.0 %collective-permute-start.4 = (bf16[128,1024]{1,0:T(8,128)(2,1)S(1)}, bf16[128,1024]{1,0:T(8,128)(2,1)S(1)}, u32[]{:S(2)}, u32[]{:S(2)}) collective-permute-start(bf16[128,1024]{1,0:T(8,128)(2,1)S(1)} %get-tuple-element.41), channel_id=1, source_target_pairs={{0,2},{1,3},{2,0},{3,1},{4,6},{5,7},{6,4},{7,5},{8,10},{9,11},{10,... | collective-permute-start | bytes 786440 | tf_op jit(solution)/shard_map/ppermute | solution.py:267
  21.9 13.7 %collective-permute-start.5 = (bf16[128,1024]{1,0:T(8,128)(2,1)S(1)}, bf16[128,1024]{1,0:T(8,128)(2,1)S(1)}, u32[]{:S(2)}, u32[]{:S(2)}) collective-permute-start(bf16[128,1024]{1,0:T(8,128)(2,1)S(1)} %get-tuple-element.42), channel_id=1, source_target_pairs={{0,4},{1,5},{2,6},{3,7},{4,0},{5,1},{6,2},{7,3},{8,12},{9,13},{10,... | collective-permute-start | bytes 786440 | tf_op jit(solution)/shard_map/ppermute | solution.py:267
  23.4 12.2 %collective-permute-start.6 = (bf16[128,1024]{1,0:T(8,128)(2,1)S(1)}, bf16[128,1024]{1,0:T(8,128)(2,1)S(1)}, u32[]{:S(2)}, u32[]{:S(2)}) collective-permute-start(bf16[128,1024]{1,0:T(8,128)(2,1)S(1)} %get-tuple-element.43), channel_id=1, source_target_pairs={{0,6},{1,7},{2,4},{3,5},{4,2},{5,3},{6,0},{7,1},{8,14},{9,15},{10,... | collective-permute-start | bytes 786440 | tf_op jit(solution)/shard_map/ppermute | solution.py:267
  25.8 4.3 %collective-permute-start.2 = (f32[64,128]{1,0:T(8,128)S(1)}, f32[64,128]{1,0:T(8,128)S(1)}, u32[]{:S(2)}, u32[]{:S(2)}) collective-permute-start(f32[64,128]{1,0:T(8,128)S(1)} %get-tuple-element.39), channel_id=1, source_target_pairs={{0,8},{8,0},{16,24},{24,16},{1,9},{9,1},{17,25},{25,17},{2,10},{10... | collective-permute-start | bytes 98312 | tf_op jit(solution)/shard_map/ppermute | solution.py:355
  30.1 5.2 %collective-permute-start.3 = (f32[64,128]{1,0:T(8,128)S(1)}, f32[64,128]{1,0:T(8,128)S(1)}, u32[]{:S(2)}, u32[]{:S(2)}) collective-permute-start(f32[64,128]{1,0:T(8,128)S(1)} %add.3.refs_0_), channel_id=1, source_target_pairs={{0,16},{8,24},{16,0},{24,8},{1,17},{9,25},{17,1},{25,9},{2,18},{10... | collective-permute-start | bytes 98312 | tf_op jit(solution)/shard_map/ppermute | solution.py:272
